TPU v7x, 512 devices: a whole 4x4x16 slice. The times are simulated.
512 devices in a mesh: slab: 32 (over z, x_hi), coil: 16 (over y, x_lo, core).
Axes of the slice: x: 4 (x_hi: 2, x_lo: 2; x = x_hi * 2 + x_lo), y: 4, z: 16, core: 2. Of those that a mesh axis runs over, the one named last changes fastest.
Arguments:
- image_estimate: bfloat16 [2, 2, 8, 512, 512], P(None, None, None, 'slab'), may hold values from -6 to 6
- coil_maps: bfloat16 [2, 32, 8, 512, 512], P(None, 'coil', None, 'slab'), may hold values from -1.5 to 1.5
- measured: bfloat16 [2, 2, 8, 32, 512, 512], P(None, None, None, 'coil', 'slab'), may hold values from -2 to 2
- sampled_blocks: int32 [2, 512, 4], P(None, 'slab'), may hold values 0 or 1
Outputs:
- gradient: float32 [2, 2, 8, 512, 512], P(None, None, None, 'slab')
All inputs are finite; a program needn't handle non-finite values. No bound on the sum of `sampled_blocks` on one device may be relied on, other than what follows from the above.
Results may differ from a plain program's by a relative error of at most 0.0034.
Values may be sent and summed in bfloat16 or wider, within the bound.
No kernel may reach another device: no remote copies, remote signals or barrier semaphores. Data moves between devices by JAX's collectives and lax.ppermute only.
A program may use at most 64 MiB of HBM per device.

v0:
```python
import math

import jax
import jax.numpy as jnp
from jax import lax
from jax.sharding import PartitionSpec as P


def dft_table(length, sign):
    indices = jnp.arange(length, dtype=jnp.int32)
    angles = (indices[:, None] * indices[None, :] % length).astype(jnp.float32) * (
        2.0 * math.pi / length
    )
    cosine = jnp.cos(angles) / math.sqrt(length)
    sinusoid = jnp.sin(angles) * (sign / math.sqrt(length))
    upper_rows = jnp.stack([cosine, -sinusoid], axis=1)
    lower_rows = jnp.stack([sinusoid, cosine], axis=1)
    return jnp.stack([upper_rows, lower_rows], axis=0).astype(jnp.bfloat16)


def z_work(arrived, measured_block, weight, table_z, table_zi):
    frame_count, readout, coil_count, _, slab_count, merged = arrived.shape
    ky_lo = measured_block.shape[4]
    len_z = measured_block.shape[5]
    z_lo = merged // ky_lo
    arrived = arrived.reshape(frame_count, readout, coil_count, 2, slab_count, ky_lo, z_lo)
    spectrum = jnp.einsum(
        "fxcphlz,phzqk->qfxclk",
        arrived,
        table_z.reshape(2, slab_count, z_lo, 2, len_z),
        preferred_element_type=jnp.float32,
    )
    residual = (
        weight[None, :, None, None] * (spectrum - measured_block.astype(jnp.float32))
    ).astype(jnp.bfloat16)
    back_z = jnp.einsum(
        "qfxclk,qkphz->fxcphlz",
        residual,
        table_zi.reshape(2, len_z, 2, slab_count, z_lo),
        preferred_element_type=jnp.float32,
    )
    return back_z.astype(jnp.bfloat16).reshape(
        frame_count, readout, coil_count, 2, slab_count, ky_lo * z_lo
    )


def shards(image_estimate, coil_maps, measured, sampled_blocks):
    slab_count = lax.axis_size("slab")
    frame_count = image_estimate.shape[1]
    readout = image_estimate.shape[2]
    z_lo = image_estimate.shape[3]
    len_y = image_estimate.shape[4]
    coil_count = coil_maps.shape[1]
    len_z = z_lo * slab_count
    ky_lo = len_y // slab_count
    block_count = sampled_blocks.shape[2]
    table_y = dft_table(len_y, 1.0)
    table_yi = dft_table(len_y, -1.0)
    table_z = dft_table(len_z, 1.0)
    table_zi = dft_table(len_z, -1.0)
    image_re = image_estimate[0].astype(jnp.float32)[:, :, None]
    image_im = image_estimate[1].astype(jnp.float32)[:, :, None]
    maps_turned = jnp.swapaxes(coil_maps, 1, 2)
    map_re = maps_turned[0].astype(jnp.float32)
    map_im = maps_turned[1].astype(jnp.float32)
    coil_images = jnp.stack(
        [map_re * image_re - map_im * image_im, map_re * image_im + map_im * image_re]
    ).astype(jnp.bfloat16)
    along_y = jnp.einsum(
        "pfxczy,pyqhl->fxcqhlz",
        coil_images,
        table_y.reshape(2, len_y, 2, slab_count, ky_lo),
        preferred_element_type=jnp.float32,
    )
    outgoing = along_y.astype(jnp.bfloat16).reshape(
        frame_count, readout, coil_count, 2, slab_count, ky_lo * z_lo
    )
    weight = jnp.repeat(sampled_blocks.astype(jnp.float32), len_z // block_count, axis=2)
    arrived = lax.all_to_all(outgoing, "slab", split_axis=4, concat_axis=4, tiled=True)
    back_z = z_work(arrived, measured, weight, table_z, table_zi)
    returned = lax.all_to_all(back_z, "slab", split_axis=4, concat_axis=4, tiled=True)
    returned = returned.reshape(frame_count, readout, coil_count, 2, slab_count, ky_lo, z_lo)
    back_image = jnp.einsum(
        "fxcphlz,phlqy->qfxczy",
        returned,
        table_yi.reshape(2, slab_count, ky_lo, 2, len_y),
        preferred_element_type=jnp.float32,
    )
    grad_re = jnp.sum(map_re * back_image[0] + map_im * back_image[1], axis=2)
    grad_im = jnp.sum(map_re * back_image[1] - map_im * back_image[0], axis=2)
    partial_sum = jnp.stack([grad_re, grad_im])
    return lax.psum(partial_sum, "coil")


def solution(mesh):
    return jax.shard_map(
        shards,
        mesh=mesh,
        in_specs=(
            P(None, None, None, "slab", None),
            P(None, "coil", None, "slab", None),
            P(None, None, None, "coil", "slab", None),
            P(None, "slab", None),
        ),
        out_specs=P(None, None, None, "slab", None),
        check_vma=False,
    )
```

profile of v0, /device:TPU:1, one launch (start us, length us, event | category | flops | bytes accessed | tf_op | source)
XLA Modules:
  0.0 356.2 jit_solution(15652553332352650602)
XLA Ops:
  6.5 1.1 fusion.59
  7.7 1.1 bitcast_convert_fusion.3
  8.9 5.0 %negate_convert_fusion.2 = (bf16[1,512,1,32,16]{1,4,0,3,2:T(8,128)(2,1)S(1)}, bf16[1,512,1,32,16]{1,4,0,3,2:T(8,128)(2,1)S(1)}, bf16[1,512,1,32,16]{1,4,0,3,2:T(...) fusion(s32[32,16]{1,0:T(8,128)S(1)} %multiply_add_fusion), kind=kLoop, calls=%fused_computation.62 | loop fusion | flops 6291456 | bytes 2623488 | tf_op jit(solution)/shard_map/convert.23
  13.9 0.0 copy-start
  13.9 0.4 subtract_convert_fusion
  14.2 10.8 %fusion = bf16[2,8,2,2,32,16,16]{6,5,2,1,0,4,3:T(8,128)(2,1)} fusion(bf16[1,512,1,32,16]{1,4,0,3,2:T(8,128)(2,1)S(1)} %get-tuple-element.17, bf16[1,512,1,32,16]{1,4,0,3,2:T(8,128)(2,1)S(1)} %get-tuple-element.15, bf16[1,512,1,32,16]{1,4,0,3,2:T(8,128)(2,1)S(1)} %get-tuple-element.14, bf16[1,2,8,2,16,512]{5,4,0,3,2,1:T(8,128)(2,1)S(1)} %get-tuple-element.8, ...), kind=kOutput, calls=%fused_computation.2 | convolution fusion | flops 1084751872 | bytes 3670016 | tf_op jit(solution)/shard_map/pfxczy,pyqhl->fxcqhlz/dot_general | solution.py:69
  25.1 0.0 copy-done
  25.1 11.3 %copy.27 = bf16[2,8,2,2,32,16,16]{4,6,5,3,2,1,0:T(8,128)(2,1)} copy(bf16[2,8,2,2,32,16,16]{6,5,2,1,0,4,3:T(8,128)(2,1)} %fusion) | data formatting | bytes 2097152 | tf_op jit(solution)/shard_map/convert_element_type | solution.py:75
  36.4 0.0 copy-start.4
  36.4 4.8 %copy.28 = bf16[2,8,2,2,32,256]{5,1,3,2,0,4:T(8,128)(2,1)} copy(bf16[2,8,2,2,32,256]{4,5,3,2,1,0:T(8,128)(2,1)} %bitcast.114) | data formatting | bytes 2097152 | tf_op jit(solution)/shard_map/reshape | solution.py:75
  41.3 18.5 %all-to-all-start = ((bf16[2,8,2,2,32,256]{5,1,3,2,0,4:T(8,128)(2,1)}), bf16[2,8,2,2,32,256]{5,1,3,2,0,4:T(8,128)(2,1)S(1)}, u32[]{:S(2)}, u32[]{:S(2)}) async-start(bf16[2,8,2,2,32,256]{5,1,3,2,0,4:T(8,128)(2,1)} %copy.28), calls=%async_computation | async-start | bytes 2097152 | tf_op jit(solution)/shard_map/all_to_all | solution.py:79
  59.8 0.0 all-reduce.2.cloned.1.call-start
  59.8 0.1 copy.23
  59.9 0.0 copy-done.4
  59.9 0.1 copy.24
  60.0 0.1 broadcast_in_dim.2
  60.1 6.2 %negate_convert_fusion.3 = (bf16[1,32,16,1,512]{4,1,2,0,3:T(8,128)(2,1)}, bf16[1,32,16,1,512]{4,1,2,0,3:T(8,128)(2,1)}, bf16[1,32,16,1,512]{4,1,2,0,3:T(8,128)(2...) fusion(s32[32,16]{0,1:T(8,128)S(1)} %copy.23), kind=kLoop, calls=%fused_computation.66 | loop fusion | flops 6291456 | bytes 2623488 | tf_op jit(solution)/shard_map/convert.29
  66.3 46.6 %all-to-all-done = bf16[2,8,2,2,32,256]{5,1,3,2,0,4:T(8,128)(2,1)S(1)} async-done(((bf16[2,8,2,2,32,256]{5,1,3,2,0,4:T(8,128)(2,1)}), bf16[2,8,2,2,32,256]{5,1,3,2,0,4:T(8,128)(2,1)S(1)}, u32[]{:S(2)}, u32[]{:S(2)}) %all-to-all-start) | async-done | bytes 1048608 | tf_op jit(solution)/shard_map/all_to_all | solution.py:79
  112.9 3.3 copy.29
  116.2 0.0 copy-start.1
  116.2 5.6 %fusion.37 = bf16[2,2,8,2,16,512,1,1]{5,4,3,2,1,0,7,6:T(8,128)(2,1)S(1)} fusion(bf16[2,2,8,2,16,512]{5,4,3,2,1,0:T(8,128)(2,1)} %param.6, bf16[2,8,2,2,32,16,16]{4,6,5,3,2,1,0:T(8,128)(2,1)} %bitcast.117, bf16[1,32,16,1,512]{4,1,2,0,3:T(8,128)(2,1)} %get-tuple-element.22, bf16[1,32,16,1,512]{4,1,2,0,3:T(8,128)(2,1)} %get-tuple-element.20, ...), kind=kOutput, calls=%fused_computation.43 | convolution fusion | flops 1084227584 | bytes 4784128 | tf_op jit(solution)/shard_map/fxcphlz,phzqk->qfxclk/dot_general | solution.py:27
  121.8 0.0 copy-done.1
  121.8 10.9 %fusion.1 = bf16[2,8,2,2,32,16,16]{5,6,2,1,0,4,3:T(8,128)(2,1)} fusion(bf16[2,2,8,2,16,512,1,1]{5,4,3,2,1,0,7,6:T(8,128)(2,1)S(1)} %fusion.37, bf16[1,512,1,32,16]{1,4,0,3,2:T(8,128)(2,1)S(1)} %copy-done.1, bf16[1,512,1,32,16]{1,4,0,3,2:T(8,128)(2,1)S(1)} %get-tuple-element.16, bf16[1,512,1,32,16]{1,4,0,3,2:T(8,128)(2,1)S(1)} %get-tuple-element.13), kind=kOutput, calls=%fused_computation.3 | convolution fusion | flops 1082654720 | bytes 3670016 | tf_op jit(solution)/shard_map/qfxclk,qkphz->fxcphlz/dot_general | solution.py:36
  132.7 12.9 %copy.32 = bf16[2,8,2,2,32,16,16]{4,6,5,3,2,1,0:T(8,128)(2,1)} copy(bf16[2,8,2,2,32,16,16]{5,6,2,1,0,4,3:T(8,128)(2,1)} %fusion.1) | data formatting | bytes 2097152 | tf_op jit(solution)/shard_map/convert_element_type | solution.py:42
  145.6 3.9 %copy.33 = bf16[2,8,2,2,32,256]{5,1,3,2,0,4:T(8,128)(2,1)S(1)} copy(bf16[2,8,2,2,32,256]{4,5,3,2,1,0:T(8,128)(2,1)} %bitcast.115) | data formatting | bytes 2097152 | tf_op jit(solution)/shard_map/reshape | solution.py:42
  149.5 59.9 %all_to_all.10 = bf16[2,8,2,2,32,256]{5,1,3,2,0,4:T(8,128)(2,1)S(1)} all-to-all(bf16[2,8,2,2,32,256]{5,1,3,2,0,4:T(8,128)(2,1)S(1)} %copy.33), channel_id=1, replica_groups=mesh['slab'=32,'coil'=16] {'slab'}, dimensions={4} | all-to-all | bytes 2097152 | tf_op jit(solution)/shard_map/all_to_all | solution.py:81
  209.4 0.0 copy-start.2
  209.4 0.0 copy-start.3
  209.5 3.3 copy.34
  212.7 0.0 copy-done.2
  212.7 0.0 copy-done.3
  212.7 4.0 %fusion.32 = f32[2,2,8,2,16,512]{5,4,3,2,1,0:T(8,128)S(1)} fusion(bf16[2,8,2,2,32,16,16]{4,6,5,3,2,1,0:T(8,128)(2,1)} %bitcast.116, bf16[1,32,16,1,512]{4,1,2,0,3:T(8,128)(2,1)} %get-tuple-element.22, bf16[1,32,16,1,512]{4,1,2,0,3:T(8,128)(2,1)S(1)} %copy-done.3, bf16[1,32,16,1,512]{4,1,2,0,3:T(8,128)(2,1)S(1)} %copy-done.2), kind=kOutput, calls=%fused_computation.36 | convolution fusion | flops 1076887552 | bytes 4718592 | tf_op jit(solution)/shard_map/fxcphlz,phlqy->qfxczy/dot_general | solution.py:83
  216.7 0.4 add_reduce_fusion
  217.1 1.0 pad_maximum_fusion.11
  218.2 0.0 all-reduce.2.cloned.1.call-update
  218.2 128.8 %all-reduce.2.cloned.1.call-done = f32[2,2,8,16,512]{4,3,2,1,0:T(8,128)} async-done(((f32[2,2,8,16,512]{4,3,2,1,0:T(8,128)}), f32[2,2,8,16,512]{4,3,2,1,0:T(8,128)}) %all-reduce.2.cloned.1.call-update) | async-done | bytes 1048592 | tf_op jit(solution)/shard_map/psum | solution.py:92
  347.0 2.3 copy.79
  (3 shorter events, 0.0 us)
Async XLA Ops:
  13.9 11.2 %copy-start = (bf16[1,512,1,32,16]{1,4,0,3,2:T(8,128)(2,1)}, bf16[1,512,1,32,16]{1,4,0,3,2:T(8,128)(2,1)S(1)}, u32[]{:S(2)}) copy-start(bf16[1,512,1,32,16]{1,4,0,3,2:T(8,128)(2,1)S(1)} %get-tuple-element.17) | copy-start | bytes 1572868
  36.4 23.5 %copy-start.4 = (s32[2,16,4]{1,2,0:T(4,128)S(1)}, s32[2,16,4]{1,2,0:T(4,128)}, u32[]{:S(2)}) copy-start(s32[2,16,4]{1,2,0:T(4,128)} %param.7) | copy-start | bytes 1540
  41.3 71.6 %all-to-all-start = ((bf16[2,8,2,2,32,256]{5,1,3,2,0,4:T(8,128)(2,1)}), bf16[2,8,2,2,32,256]{5,1,3,2,0,4:T(8,128)(2,1)S(1)}, u32[]{:S(2)}, u32[]{:S(2)}) async-start(bf16[2,8,2,2,32,256]{5,1,3,2,0,4:T(8,128)(2,1)} %copy.28), calls=%async_computation | async-start | bytes 2097152 | tf_op jit(solution)/shard_map/all_to_all | solution.py:79
  59.8 287.2 %all-reduce.2.cloned.1.call-start = ((), (), s32[]{:S(2)}) async-start(), calls=%async_computation.2 | async-start | bytes 2097152 | tf_op jit(solution)/shard_map/psum | solution.py:92
  116.2 5.6 %copy-start.1 = (bf16[1,512,1,32,16]{1,4,0,3,2:T(8,128)(2,1)S(1)}, bf16[1,512,1,32,16]{1,4,0,3,2:T(8,128)(2,1)}, u32[]{:S(2)}) copy-start(bf16[1,512,1,32,16]{1,4,0,3,2:T(8,128)(2,1)} %copy-done) | copy-start | bytes 1572868
  209.4 3.3 copy-start.2
  209.4 3.3 copy-start.3
Sparse Core Ops, SparseCore 0:
  218.3 128.6 all-reduce.1
where the time goes:
time: 357 us; the launch traced here: 356 us
  waiting for transfers between devices  175 us (49%)
  blocking collectives  59.9 us (17%)
  local copies, waits for them, and re-layouts  42.2 us (12%)
  matrix products  31.3 us (9%)
  starting transfers between devices  18.5 us (5%)
  other arithmetic  15.3 us (4%)
  between operations  13.5 us (4%)
    psum x1, waiting for transfers between devices, shards(): return lax.psum(partial_sum, 'coil')  129 us
    all_to_all x1, blocking collectives, shards(): lax.all_to_all(back_z, 'slab', split_axis=4, concat_axis=4, tiled=True)  59.9 us
    all_to_all x1, waiting for transfers between devices, shards(): lax.all_to_all(outgoing, 'slab', split_axis=4, concat_axis=4, tiled=True)  46.6 us
    all_to_all x1, starting transfers between devices, shards(): lax.all_to_all(outgoing, 'slab', split_axis=4, concat_axis=4, tiled=True)  18.5 us
    convert_element_type x1, local copies, waits for them, and re-layouts, z_work(): back_z.astype(jnp.bfloat16)  12.9 us
    another operation x3, other arithmetic  11.5 us
    convert_element_type x1, local copies, waits for them, and re-layouts, shards(): along_y.astype(jnp.bfloat16)  11.3 us
    dot_general x1, matrix products, z_work(): jnp.einsum('qfxclk,qkphz->fxcphlz', residual, table_zi.reshape(2, len_z,...  10.9 us
  transfers between devices with their start and end apart: 2, of which 2 were waited for; matrix products, arithmetic and copies ran while one was open for 2% of the time, Pallas kernels for 0%

commit v1 on v0

v1 whole, which is shorter than its diff:
```python
import math

import jax
import jax.numpy as jnp
import ml_dtypes
import numpy as np
from jax import lax
from jax.experimental import pallas as pl
from jax.experimental.pallas import tpu as pltpu
from jax.sharding import PartitionSpec as P

LANES = 128
VMEM_LIMIT = 48 * 1024 * 1024


def dft_tables(length):
    indices = np.arange(length)
    angles = (indices[:, None] * indices[None, :] % length) * (2.0 * math.pi / length)
    cosine = (np.cos(angles) / math.sqrt(length)).astype(ml_dtypes.bfloat16)
    sine = (np.sin(angles) / math.sqrt(length)).astype(ml_dtypes.bfloat16)
    return cosine, sine


def swap_runs(block, run):
    count, rows, lanes = block.shape
    position = lax.broadcasted_iota(jnp.int32, (1, 1, 1, rows, lanes), 4) // run
    step = 1
    while step < count:
        pairs = block.reshape(count // (2 * step), 2, step, rows, lanes)
        low, high = pairs[:, 0:1], pairs[:, 1:2]
        shape = low.shape
        flat = (-1, lanes)
        high_moved = pltpu.roll(high.reshape(flat), step * run, 1).reshape(shape)
        low_moved = pltpu.roll(low.reshape(flat), lanes - step * run, 1).reshape(shape)
        upper = (position & step) != 0
        new_low = jnp.where(upper, high_moved, low)
        new_high = jnp.where(upper, high, low_moved)
        block = jnp.concatenate([new_low, new_high], axis=1).reshape(count, rows, lanes)
        step *= 2
    return block


def forward_y(maps_ref, image_ref, cos_ref, sin_ref, out_ref, lhs):
    coils, readout, z_lo, _ = maps_ref.shape[1:]
    half = readout * coils * z_lo
    for x in range(readout):
        image_re = image_ref[0, 0, x].astype(jnp.float32)
        image_im = image_ref[1, 0, x].astype(jnp.float32)
        for c in range(coils):
            map_re = maps_ref[0, c, x].astype(jnp.float32)
            map_im = maps_ref[1, c, x].astype(jnp.float32)
            row = (x * coils + c) * z_lo
            lhs[row : row + z_lo] = (map_re * image_re - map_im * image_im).astype(jnp.bfloat16)
            row += half
            lhs[row : row + z_lo] = (map_re * image_im + map_im * image_re).astype(jnp.bfloat16)
    by_cos = jnp.dot(lhs[...], cos_ref[...], preferred_element_type=jnp.float32)
    by_sin = jnp.dot(lhs[...], sin_ref[...], preferred_element_type=jnp.float32)
    parts = (by_cos[:half] + by_sin[half:], by_cos[half:] - by_sin[:half])
    group = readout * coils
    run = LANES // group
    for p, part in enumerate(parts):
        for tb in range(part.shape[1] // LANES):
            block = part[:, tb * LANES : (tb + 1) * LANES].reshape(group, z_lo, LANES)
            out_ref[tb * group : (tb + 1) * group, :, p * LANES : (p + 1) * LANES] = swap_runs(
                block, run
            ).astype(jnp.bfloat16)


def z_work(arrived_ref, measured_ref, weight_ref, cos_ref, sin_ref, out_ref, residual):
    blocks = weight_ref.shape[1]
    width = arrived_ref.shape[1] // 2
    depth = arrived_ref.shape[0] // blocks
    by_cos = jnp.dot(cos_ref[...], arrived_ref[...], preferred_element_type=jnp.float32)
    by_sin = jnp.dot(sin_ref[...], arrived_ref[...], preferred_element_type=jnp.float32)
    target_re = measured_ref[0].astype(jnp.float32).T
    target_im = measured_ref[1].astype(jnp.float32).T
    spectrum_re = by_cos[:, :width] + by_sin[:, width:]
    spectrum_im = by_cos[:, width:] - by_sin[:, :width]
    for b in range(blocks):
        rows = slice(b * depth, (b + 1) * depth)
        weight = weight_ref[0, b : b + 1, :]
        residual[rows, :width] = (weight * (spectrum_re[rows] - target_re[rows])).astype(jnp.bfloat16)
        residual[rows, width:] = (weight * (spectrum_im[rows] - target_im[rows])).astype(jnp.bfloat16)
    by_cos = jnp.dot(cos_ref[...], residual[...], preferred_element_type=jnp.float32)
    by_sin = jnp.dot(sin_ref[...], residual[...], preferred_element_type=jnp.float32)
    out_ref[:, :width] = (by_cos[:, :width] - by_sin[:, width:]).astype(jnp.bfloat16)
    out_ref[:, width:] = (by_cos[:, width:] + by_sin[:, :width]).astype(jnp.bfloat16)


def backward_y(returned_ref, maps_ref, cos_ref, sin_ref, out_ref, lhs):
    coils, readout, z_lo, _ = maps_ref.shape[1:]
    half = readout * coils * z_lo
    group = readout * coils
    run = LANES // group
    for p in range(2):
        for tb in range(lhs.shape[1] // LANES):
            block = returned_ref[tb * group : (tb + 1) * group, :, p * LANES : (p + 1) * LANES]
            block = swap_runs(block.astype(jnp.float32), run)
            lhs[p * half : (p + 1) * half, tb * LANES : (tb + 1) * LANES] = block.reshape(
                half, LANES
            ).astype(jnp.bfloat16)
    by_cos = jnp.dot(lhs[...], cos_ref[...], preferred_element_type=jnp.float32)
    by_sin = jnp.dot(lhs[...], sin_ref[...], preferred_element_type=jnp.float32)
    back_re = by_cos[:half] - by_sin[half:]
    back_im = by_cos[half:] + by_sin[:half]
    for x in range(readout):
        sum_re = sum_im = None
        for c in range(coils):
            map_re = maps_ref[0, c, x].astype(jnp.float32)
            map_im = maps_ref[1, c, x].astype(jnp.float32)
            row = (x * coils + c) * z_lo
            re, im = back_re[row : row + z_lo], back_im[row : row + z_lo]
            grad_re = map_re * re + map_im * im
            grad_im = map_re * im - map_im * re
            sum_re = grad_re if sum_re is None else sum_re + grad_re
            sum_im = grad_im if sum_im is None else sum_im + grad_im
        out_ref[x, 0] = sum_re.astype(jnp.bfloat16)
        out_ref[x, 1] = sum_im.astype(jnp.bfloat16)


def coil_sum(terms_ref, out_ref):
    total = jnp.sum(terms_ref[...].astype(jnp.float32), axis=0).astype(jnp.bfloat16)
    out_ref[...] = jnp.broadcast_to(total[None], out_ref.shape)


def call(kernel, name, out_shape, grid, in_specs, out_specs, scratch, flops, bytes_accessed):
    return pl.pallas_call(
        kernel,
        name=name,
        out_shape=out_shape,
        grid=grid,
        in_specs=in_specs,
        out_specs=out_specs,
        scratch_shapes=scratch,
        compiler_params=pltpu.CompilerParams(
            dimension_semantics=("arbitrary",), vmem_limit_bytes=VMEM_LIMIT
        ),
        cost_estimate=pl.CostEstimate(
            flops=flops, bytes_accessed=bytes_accessed, transcendentals=0
        ),
    )


def shards(image_estimate, coil_maps, measured, sampled_blocks, cosine, sine):
    slabs = lax.axis_size("slab")
    groups = lax.axis_size("coil")
    _, frames, readout, z_lo, len_y = image_estimate.shape
    coils = coil_maps.shape[1]
    ky_lo, len_z = measured.shape[4:]
    block_count = sampled_blocks.shape[2]
    group = LANES // ky_lo
    part = group // coils
    parts = readout // part
    steps = frames * parts
    lanes = steps * 2 * LANES
    half = group * z_lo

    maps_spec = pl.BlockSpec((2, coils, part, z_lo, len_y), lambda i: (0, 0, i % parts, 0, 0))
    image_spec = pl.BlockSpec((2, 1, part, z_lo, len_y), lambda i: (0, i // parts, i % parts, 0, 0))
    table_spec = pl.BlockSpec((len_y, len_y), lambda i: (0, 0))
    turned_spec = pl.BlockSpec((slabs, z_lo, 2 * LANES), lambda i: (0, 0, i))
    columns_spec = pl.BlockSpec((len_z, 2 * LANES), lambda i: (0, i))
    table_bytes = 4 * len_y * len_y

    outgoing = call(
        forward_y,
        "forward_y",
        jax.ShapeDtypeStruct((slabs, z_lo, lanes), jnp.bfloat16),
        (steps,),
        [maps_spec, image_spec, table_spec, table_spec],
        turned_spec,
        [pltpu.VMEM((2 * half, len_y), jnp.bfloat16)],
        8 * steps * half * len_y * len_y,
        8 * steps * half * len_y + table_bytes,
    )(coil_maps, image_estimate, cosine, sine)
    arrived = lax.all_to_all(outgoing, "slab", split_axis=0, concat_axis=0, tiled=True)

    weight = jnp.swapaxes(sampled_blocks.astype(jnp.float32), 1, 2)
    weight = jnp.tile(weight, (1, 1, group))
    back_z = call(
        z_work,
        "z_work",
        jax.ShapeDtypeStruct((len_z, lanes), jnp.bfloat16),
        (steps,),
        [
            columns_spec,
            pl.BlockSpec((2, LANES, len_z), lambda i: (0, i, 0)),
            pl.BlockSpec((1, block_count, LANES), lambda i: (i // parts, 0, 0)),
            table_spec,
            table_spec,
        ],
        columns_spec,
        [pltpu.VMEM((len_z, 2 * LANES), jnp.bfloat16)],
        16 * steps * half * len_z * len_z,
        12 * steps * half * len_z + table_bytes,
    )(
        arrived.reshape(len_z, lanes),
        measured.reshape(2, steps * LANES, len_z),
        weight,
        cosine,
        sine,
    )
    returned = lax.all_to_all(
        back_z.reshape(slabs, z_lo, lanes), "slab", split_axis=0, concat_axis=0, tiled=True
    )

    partial_sum = call(
        backward_y,
        "backward_y",
        jax.ShapeDtypeStruct((frames * readout, 2, z_lo, len_y), jnp.bfloat16),
        (steps,),
        [turned_spec, maps_spec, table_spec, table_spec],
        pl.BlockSpec((part, 2, z_lo, len_y), lambda i: (i, 0, 0, 0)),
        [pltpu.VMEM((2 * half, len_y), jnp.bfloat16)],
        8 * steps * half * len_y * len_y,
        8 * steps * half * len_y + table_bytes,
    )(returned, coil_maps, cosine, sine)

    pieces = frames * readout // groups
    rows = pieces * 2 * z_lo
    terms = lax.all_to_all(partial_sum, "coil", split_axis=0, concat_axis=0, tiled=True)
    sum_spec = pl.BlockSpec((groups, rows, len_y), lambda i: (0, 0, 0))
    total = call(
        coil_sum,
        "coil_sum",
        jax.ShapeDtypeStruct((groups, rows, len_y), jnp.bfloat16),
        (1,),
        [sum_spec],
        sum_spec,
        [],
        groups * rows * len_y,
        4 * groups * rows * len_y,
    )(terms.reshape(groups, rows, len_y))
    whole = lax.all_to_all(total, "coil", split_axis=0, concat_axis=0, tiled=True)
    whole = whole.reshape(frames, readout, 2, z_lo, len_y)
    return jnp.moveaxis(whole, 2, 0).astype(jnp.float32)


def solution(mesh):
    body = jax.shard_map(
        shards,
        mesh=mesh,
        in_specs=(
            P(None, None, None, "slab", None),
            P(None, "coil", None, "slab", None),
            P(None, None, None, "coil", "slab", None),
            P(None, "slab", None),
            P(None, None),
            P(None, None),
        ),
        out_specs=P(None, None, None, "slab", None),
        check_vma=False,
    )

    def run(image_estimate, coil_maps, measured, sampled_blocks):
        cosine, sine = dft_tables(image_estimate.shape[4])
        return body(
            image_estimate, coil_maps, measured, sampled_blocks, jnp.asarray(cosine), jnp.asarray(sine)
        )

    return run
```

time: 357 us -> 179 us (0.50)
  waiting for transfers between devices: 175 us -> 53 us
  local copies, waits for them, and re-layouts: 42.2 us -> 4.27 us
  matrix products: 31.3 us -> 0 us
  blocking collectives: 59.9 us -> 89.5 us
  other arithmetic: 15.3 us -> 1.1 us
  between operations: 13.5 us -> 0.08 us
  Pallas kernels: 0 us -> 11 us
    psum x1 -> x0, waiting for transfers between devices: 129 us -> none  [shards(): return lax.psum(partial_sum, 'coil')]
    dot_general x4 -> x0, matrix products: 31.3 us -> none  [the longest x1 10.9 us: z_work(): jnp.einsum('qfxclk,qkphz->fxcphlz', residual, table_zi.reshape(2, len_z,...]
    all_to_all x1 -> x3, blocking collectives: 59.9 us -> 89.5 us  [the longest x1 60 us: shards(): lax.all_to_all(back_z.reshape(slabs, z_lo, lanes), 'slab', split_axis=0,...]
    convert_element_type x3 -> x0, local copies, waits for them, and re-layouts: 24.4 us -> none  [the longest x1 12.9 us: z_work(): back_z.astype(jnp.bfloat16)]
    another operation x4 -> x0, other arithmetic: 12.6 us -> none
    pallas_call x0 -> x4, Pallas kernels: none -> 11 us  [the longest x1 3.67 us: shards(): call(z_work, 'z_work', jax.ShapeDtypeStruct((len_z, lanes), jnp.bfloat16)...]
    reshape x2 -> x0, local copies, waits for them, and re-layouts: 8.76 us -> none  [the longest x1 4.84 us: shards(): along_y.astype(jnp.bfloat16)]
    all_to_all x2 -> x0, local copies, waits for them, and re-layouts: 6.57 us -> none  [the longest x1 3.28 us: shards(): lax.all_to_all(outgoing, 'slab', split_axis=4, concat_axis=4, tiled=True)]
  transfers between devices with their start and end apart: 2 -> 1, of which waited for: 2 -> 1; matrix products, arithmetic and copies ran while one was open for 2% -> 0% of each run, Pallas kernels for 0% -> 0%
where the time goes in v1:
time: 179 us; the launch traced here: 178 us
  blocking collectives  89.5 us (50%)
  waiting for transfers between devices  53 us (30%)
  starting transfers between devices  18.6 us (10%)
  Pallas kernels  11 us (6%)
  local copies, waits for them, and re-layouts  4.27 us (2%)
    all_to_all x1, blocking collectives, shards(): lax.all_to_all(back_z.reshape(slabs, z_lo, lanes), 'slab', split_axis=0,...  60 us
    all_to_all x1, waiting for transfers between devices, shards(): lax.all_to_all(outgoing, 'slab', split_axis=0, concat_axis=0, tiled=True)  53 us
    all_to_all x1, starting transfers between devices, shards(): lax.all_to_all(outgoing, 'slab', split_axis=0, concat_axis=0, tiled=True)  18.6 us
    all_to_all x1, blocking collectives, shards(): lax.all_to_all(partial_sum, 'coil', split_axis=0, concat_axis=0, tiled=True)  16 us
    all_to_all x1, blocking collectives, shards(): lax.all_to_all(total, 'coil', split_axis=0, concat_axis=0, tiled=True)  13.5 us
    unnamed x18, local copies, waits for them, and re-layouts  4.19 us
    pallas_call x1, Pallas kernels, shards(): call(z_work, 'z_work', jax.ShapeDtypeStruct((len_z, lanes), jnp.bfloat16)...  3.67 us
    pallas_call x1, Pallas kernels, shards(): call(forward_y, 'forward_y', jax.ShapeDtypeStruct((slabs, z_lo, lanes), j...  3.67 us
  transfers between devices with their start and end apart: 1, of which 1 were waited for; matrix products, arithmetic and copies ran while one was open for 0% of the time, Pallas kernels for 0%

profile of v1, /device:TPU:1, one launch (start us, length us, event | category | flops | bytes accessed | tf_op | source)
XLA Modules:
  0.0 177.6 jit_solution(6087518903202437414)
XLA Ops:
  0.0 0.0 copy-start.1
  0.0 1.0 copy-done.1
  1.0 0.0 copy-start.2
  1.0 1.0 copy-done.2
  2.1 0.0 copy-start.4
  2.1 1.0 copy-done.4
  3.1 0.0 copy-start.6
  3.1 1.0 copy-done.6
  4.2 0.0 copy-start.8
  4.2 3.7 %forward_y.1 = bf16[32,16,1024]{2,1,0:T(8,128)(2,1)} custom-call(bf16[2,2,8,16,512]{4,3,2,1,0:T(8,128)(2,1)S(1)} %copy-done.2, bf16[2,2,8,16,512]{4,3,2,1,0:T(8,128)(2,1)S(1)} %copy-done.1, bf16[512,512]{1,0:T(8,128)(2,1)S(1)} %copy-done.4, bf16[512,512]{1,0:T(8,128)(2,1)S(1)} %copy-done.6), custom_call_target="tpu_custom_call" | custom-call | flops 1073741824 | bytes 3145728 | tf_op jit(solution)/shard_map/forward_y/pallas_call | solution.py:165
  7.8 0.0 copy-start
  7.8 0.0 copy-start.5
  7.8 0.0 copy-start.7
  7.8 18.6 %all-to-all-start = ((bf16[32,16,1024]{2,1,0:T(8,128)(2,1)}), bf16[32,16,1024]{2,1,0:T(8,128)(2,1)S(1)}, u32[]{:S(2)}, u32[]{:S(2)}) async-start(bf16[32,16,1024]{2,1,0:T(8,128)(2,1)} %forward_y.1), calls=%async_computation | async-start | bytes 2097152 | tf_op jit(solution)/shard_map/all_to_all | solution.py:176
  26.5 0.0 copy-done.8
  26.5 0.1 tile.10.weight_ref
  26.6 53.0 %all-to-all-done = bf16[32,16,1024]{2,1,0:T(8,128)(2,1)S(1)} async-done(((bf16[32,16,1024]{2,1,0:T(8,128)(2,1)}), bf16[32,16,1024]{2,1,0:T(8,128)(2,1)S(1)}, u32[]{:S(2)}, u32[]{:S(2)}) %all-to-all-start) | async-done | bytes 1048608 | tf_op jit(solution)/shard_map/all_to_all | solution.py:176
  79.6 0.0 copy-done
  79.6 0.0 copy-done.5
  79.6 0.0 copy-done.7
  79.6 3.7 %z_work.1 = bf16[512,1024]{1,0:T(8,128)(2,1)S(1)} custom-call(bf16[512,1024]{1,0:T(8,128)(2,1)S(1)} %bitcast.13, bf16[2,512,512]{2,1,0:T(8,128)(2,1)S(1)} %bitcast.15, f32[2,4,128]{2,1,0:T(4,128)S(1)} %tile.10.weight_ref, bf16[512,512]{1,0:T(8,128)(2,1)S(1)} %copy-done.5, bf16[512,512]{1,0:T(8,128)(2,1)S(1)} %copy-done.7), custom_call_target="tpu_custom_call" | custom-call | flops 2147483648 | bytes 4194304 | tf_op jit(solution)/shard_map/z_work/pallas_call | solution.py:180
  83.3 0.0 copy-start.3
  83.3 60.0 %all_to_all.20.returned_ref = bf16[32,16,1024]{2,1,0:T(8,128)(2,1)S(1)} all-to-all(bf16[32,16,1024]{2,1,0:T(8,128)(2,1)S(1)} %bitcast.14), channel_id=1, replica_groups=mesh['slab'=32,'coil'=16] {'slab'}, dimensions={0} | all-to-all | bytes 2097152 | tf_op jit(solution)/shard_map/all_to_all | solution.py:203
  143.4 0.0 copy-done.3
  143.4 3.6 %backward_y.1 = bf16[16,2,16,512]{3,2,1,0:T(8,128)(2,1)S(1)} custom-call(bf16[32,16,1024]{2,1,0:T(8,128)(2,1)S(1)} %all_to_all.20.returned_ref, bf16[2,2,8,16,512]{4,3,2,1,0:T(8,128)(2,1)S(1)} %copy-done.3, bf16[512,512]{1,0:T(8,128)(2,1)S(1)} %copy-done.5, bf16[512,512]{1,0:T(8,128)(2,1)S(1)} %copy-done.7), custom_call_target="tpu_custom_call" | custom-call | flops 1073741824 | bytes 3145728 | tf_op jit(solution)/shard_map/backward_y/pallas_call | solution.py:207
  147.0 16.0 %all_to_all.21 = bf16[16,2,16,512]{3,2,1,0:T(8,128)(2,1)S(1)} all-to-all(bf16[16,2,16,512]{3,2,1,0:T(8,128)(2,1)S(1)} %backward_y.1), channel_id=1, replica_groups=mesh['slab'=32,'coil'=16] {'coil'}, dimensions={0} | all-to-all | bytes 1048576 | tf_op jit(solution)/shard_map/all_to_all | solution.py:221
  162.9 0.1 coil_sum.1
  163.0 13.5 %all_to_all.22 = bf16[16,32,512]{2,1,0:T(8,128)(2,1)S(1)} all-to-all(bf16[16,32,512]{2,1,0:T(8,128)(2,1)S(1)} %coil_sum.1), channel_id=1, replica_groups=mesh['slab'=32,'coil'=16] {'coil'}, dimensions={0} | all-to-all | bytes 1048576 | tf_op jit(solution)/shard_map/all_to_all | solution.py:234
  176.5 1.1 copy_bitcast_fusion
  (2 shorter events, 0.0 us)
Async XLA Ops:
  0.0 1.0 copy-start.1
  1.0 1.0 copy-start.2
  2.1 1.0 copy-start.4
  3.1 1.0 copy-start.6
  4.2 22.3 %copy-start.8 = (s32[2,16,4]{1,2,0:T(4,128)S(1)}, s32[2,16,4]{1,2,0:T(4,128)}, u32[]{:S(2)}) copy-start(s32[2,16,4]{1,2,0:T(4,128)} %param.9) | copy-start | bytes 1540
  7.8 71.8 %copy-start = (bf16[2,2,8,2,16,512]{5,4,3,2,1,0:T(8,128)(2,1)S(1)}, bf16[2,2,8,2,16,512]{5,4,3,2,1,0:T(8,128)(2,1)}, u32[]{:S(2)}) copy-start(bf16[2,2,8,2,16,512]{5,4,3,2,1,0:T(8,128)(2,1)} %param.8) | copy-start | bytes 3145732
  7.8 71.8 %copy-start.5 = (bf16[512,512]{1,0:T(8,128)(2,1)S(1)}, bf16[512,512]{1,0:T(8,128)(2,1)}, u32[]{:S(2)}) copy-start(bf16[512,512]{1,0:T(8,128)(2,1)} %constant.4.clone.cos_ref) | copy-start | bytes 1572868
  7.8 71.8 %copy-start.7 = (bf16[512,512]{1,0:T(8,128)(2,1)S(1)}, bf16[512,512]{1,0:T(8,128)(2,1)}, u32[]{:S(2)}) copy-start(bf16[512,512]{1,0:T(8,128)(2,1)} %constant.5.clone.sin_ref) | copy-start | bytes 1572868
  7.8 71.8 %all-to-all-start = ((bf16[32,16,1024]{2,1,0:T(8,128)(2,1)}), bf16[32,16,1024]{2,1,0:T(8,128)(2,1)S(1)}, u32[]{:S(2)}, u32[]{:S(2)}) async-start(bf16[32,16,1024]{2,1,0:T(8,128)(2,1)} %forward_y.1), calls=%async_computation | async-start | bytes 2097152 | tf_op jit(solution)/shard_map/all_to_all | solution.py:176
  83.3 60.1 %copy-start.3 = (bf16[2,2,8,16,512]{4,3,2,1,0:T(8,128)(2,1)S(1)}, bf16[2,2,8,16,512]{4,3,2,1,0:T(8,128)(2,1)}, u32[]{:S(2)}) copy-start(bf16[2,2,8,16,512]{4,3,2,1,0:T(8,128)(2,1)} %maps_ref.3) | copy-start | bytes 1572868

commit v2 on v1

v2 whole, which is shorter than its diff:
```python
import math

import jax
import jax.numpy as jnp
import ml_dtypes
import numpy as np
from jax import lax
from jax.experimental import pallas as pl
from jax.experimental.pallas import tpu as pltpu
from jax.sharding import PartitionSpec as P

LANES = 128
VMEM_LIMIT = 48 * 1024 * 1024


def dft_tables(length):
    indices = np.arange(length)
    angles = (indices[:, None] * indices[None, :] % length) * (2.0 * math.pi / length)
    cosine = (np.cos(angles) / math.sqrt(length)).astype(ml_dtypes.bfloat16)
    sine = (np.sin(angles) / math.sqrt(length)).astype(ml_dtypes.bfloat16)
    return cosine, sine


def swap_runs(block, run):
    count, rows, lanes = block.shape
    position = lax.broadcasted_iota(jnp.int32, (1, 1, 1, rows, lanes), 4) // run
    step = 1
    while step < count:
        pairs = block.reshape(count // (2 * step), 2, step, rows, lanes)
        low, high = pairs[:, 0:1], pairs[:, 1:2]
        shape = low.shape
        flat = (-1, lanes)
        high_moved = pltpu.roll(high.reshape(flat), step * run, 1).reshape(shape)
        low_moved = pltpu.roll(low.reshape(flat), lanes - step * run, 1).reshape(shape)
        upper = (position & step) != 0
        new_low = jnp.where(upper, high_moved, low)
        new_high = jnp.where(upper, high, low_moved)
        block = jnp.concatenate([new_low, new_high], axis=1).reshape(count, rows, lanes)
        step *= 2
    return block


def forward_y(maps_ref, image_ref, cos_ref, sin_ref, out_ref, lhs):
    coils, readout, z_lo, _ = maps_ref.shape[1:]
    frames = image_ref.shape[1]
    group = readout * frames * coils
    half = group * z_lo
    for x in range(readout):
        for f in range(frames):
            image_re = image_ref[0, f, x].astype(jnp.float32)
            image_im = image_ref[1, f, x].astype(jnp.float32)
            for c in range(coils):
                map_re = maps_ref[0, c, x].astype(jnp.float32)
                map_im = maps_ref[1, c, x].astype(jnp.float32)
                row = ((x * frames + f) * coils + c) * z_lo
                lhs[row : row + z_lo] = (map_re * image_re - map_im * image_im).astype(jnp.bfloat16)
                row += half
                lhs[row : row + z_lo] = (map_re * image_im + map_im * image_re).astype(jnp.bfloat16)
    by_cos = jnp.dot(lhs[...], cos_ref[...], preferred_element_type=jnp.float32)
    by_sin = jnp.dot(lhs[...], sin_ref[...], preferred_element_type=jnp.float32)
    parts = (by_cos[:half] + by_sin[half:], by_cos[half:] - by_sin[:half])
    run = LANES // group
    for p, part in enumerate(parts):
        for tb in range(part.shape[1] // LANES):
            block = part[:, tb * LANES : (tb + 1) * LANES].reshape(group, z_lo, LANES)
            out_ref[tb * group : (tb + 1) * group, :, p * LANES : (p + 1) * LANES] = swap_runs(
                block, run
            ).astype(jnp.bfloat16)


def z_work(arrived_ref, measured_ref, weight_ref, cos_ref, sin_ref, out_ref, residual):
    blocks = weight_ref.shape[0]
    width = arrived_ref.shape[1] // 2
    depth = arrived_ref.shape[0] // blocks
    _, frames, readout, coils, ky_lo, len_z = measured_ref.shape
    by_cos = jnp.dot(cos_ref[...], arrived_ref[...], preferred_element_type=jnp.float32)
    by_sin = jnp.dot(sin_ref[...], arrived_ref[...], preferred_element_type=jnp.float32)
    target = []
    for p in range(2):
        rows = [
            measured_ref[p, f, x].astype(jnp.float32).reshape(coils * ky_lo, len_z)
            for x in range(readout)
            for f in range(frames)
        ]
        target.append(jnp.concatenate(rows, axis=0).T)
    spectrum_re = by_cos[:, :width] + by_sin[:, width:]
    spectrum_im = by_cos[:, width:] - by_sin[:, :width]
    for b in range(blocks):
        rows = slice(b * depth, (b + 1) * depth)
        weight = weight_ref[b : b + 1, :]
        residual[rows, :width] = (weight * (spectrum_re[rows] - target[0][rows])).astype(jnp.bfloat16)
        residual[rows, width:] = (weight * (spectrum_im[rows] - target[1][rows])).astype(jnp.bfloat16)
    by_cos = jnp.dot(cos_ref[...], residual[...], preferred_element_type=jnp.float32)
    by_sin = jnp.dot(sin_ref[...], residual[...], preferred_element_type=jnp.float32)
    back_re = by_cos[:, :width] - by_sin[:, width:]
    back_im = by_cos[:, width:] + by_sin[:, :width]
    run = width // readout
    lower = lax.broadcasted_iota(jnp.int32, back_re.shape, 1) < run
    slabs, z_lo = out_ref.shape[0], out_ref.shape[2]
    for x, part in enumerate(
        (
            jnp.where(lower, back_re, pltpu.roll(back_im, run, 1)),
            jnp.where(lower, pltpu.roll(back_re, run, 1), back_im),
        )
    ):
        out_ref[:, x] = part.reshape(slabs, z_lo, width).astype(jnp.bfloat16)


def backward_y(place_ref, returned_ref, maps_ref, cos_ref, sin_ref, out_ref, lhs, total):
    step = pl.program_id(0)
    chip, core = place_ref[0], place_ref[1]
    chips, rows = returned_ref.shape[1:3]
    cores, _, coils, z_part, _ = maps_ref.shape[1:]
    frames = total.shape[1]
    group = 2 * frames * coils
    run = LANES // group
    half = lhs.shape[0] // 2

    @pl.when(step == 0)
    def _():
        total[...] = jnp.zeros_like(total)

    for q in range(chips):
        for tb in range(lhs.shape[1] // LANES):
            block = returned_ref[tb * group : (tb + 1) * group, q].astype(jnp.float32)
            block = swap_runs(block, run).astype(jnp.bfloat16)
            for p in range(2):
                for f in range(frames):
                    for c in range(coils):
                        row = p * half + ((f * chips + q) * coils + c) * rows
                        lhs[row : row + rows, tb * LANES : (tb + 1) * LANES] = block[
                            (p * frames + f) * coils + c
                        ]
    by_cos = jnp.dot(lhs[...], cos_ref[...], preferred_element_type=jnp.float32)
    by_sin = jnp.dot(lhs[...], sin_ref[...], preferred_element_type=jnp.float32)
    back_re = by_cos[:half] - by_sin[half:]
    back_im = by_cos[half:] + by_sin[:half]
    sums = [[total[0, f], total[1, f]] for f in range(frames)]
    for q in range(chips):
        source = (step * chips + q) ^ chip
        for k in range(cores):
            for c in range(coils):
                map_re = maps_ref[source, k ^ core, 0, c].astype(jnp.float32)
                map_im = maps_ref[source, k ^ core, 1, c].astype(jnp.float32)
                for f in range(frames):
                    row = ((f * chips + q) * coils + c) * rows + k * z_part
                    re, im = back_re[row : row + z_part], back_im[row : row + z_part]
                    sums[f][0] = sums[f][0] + (map_re * re + map_im * im)
                    sums[f][1] = sums[f][1] + (map_re * im - map_im * re)
    for f in range(frames):
        total[0, f] = sums[f][0]
        total[1, f] = sums[f][1]

    @pl.when(step == pl.num_programs(0) - 1)
    def _():
        whole = jnp.concatenate([total[p, f] for p in range(2) for f in range(frames)], axis=0)
        out_ref[...] = jnp.broadcast_to(whole.astype(jnp.bfloat16)[None], out_ref.shape)


def call(kernel, name, out_shape, grid_spec, flops, bytes_accessed):
    return pl.pallas_call(
        kernel,
        name=name,
        out_shape=out_shape,
        grid_spec=grid_spec,
        compiler_params=pltpu.CompilerParams(
            dimension_semantics=("arbitrary",), vmem_limit_bytes=VMEM_LIMIT
        ),
        cost_estimate=pl.CostEstimate(
            flops=flops, bytes_accessed=bytes_accessed, transcendentals=0
        ),
    )


def maps_by_readout(coil_maps, place):
    cores = 2
    chips = lax.axis_size("coil") // cores
    chip, core = place[0], place[1]
    _, coils, readout, z_lo, len_y = coil_maps.shape
    halves = coil_maps.reshape(2, coils, readout, cores, z_lo // cores, len_y)
    own = lax.dynamic_index_in_dim(halves, core, 3, keepdims=False)
    other = lax.dynamic_index_in_dim(halves, 1 - core, 3, keepdims=False)
    devices = range(chips * cores)
    got = lax.ppermute(other, "coil", [(i, i ^ 1) for i in devices])
    both = jnp.stack([own, got])
    pieces = []
    for k in range(chips):
        piece = lax.dynamic_index_in_dim(both, chip ^ k, 3, keepdims=False)
        if k:
            piece = lax.ppermute(piece, "coil", [(i, i ^ (cores * k)) for i in devices])
        pieces.append(piece)
    return jnp.stack(pieces)


def shards(image_estimate, coil_maps, measured, sampled_blocks, cosine, sine):
    slabs = lax.axis_size("slab")
    groups = lax.axis_size("coil")
    _, frames, readout, z_lo, len_y = image_estimate.shape
    coils = coil_maps.shape[1]
    ky_lo, len_z = measured.shape[4:]
    block_count = sampled_blocks.shape[2]
    group = LANES // ky_lo
    part = group // (coils * frames)
    steps = readout // part
    lanes = steps * 2 * LANES
    half = group * z_lo
    cores = 2
    chips = groups // cores
    z_part = z_lo // cores
    me = lax.axis_index("coil")
    place = jnp.stack([me // cores, me % cores]).astype(jnp.int32)

    maps_spec = pl.BlockSpec((2, coils, part, z_lo, len_y), lambda i: (0, 0, i, 0, 0))
    image_spec = pl.BlockSpec((2, frames, part, z_lo, len_y), lambda i: (0, 0, i, 0, 0))
    table_spec = pl.BlockSpec((len_y, len_y), lambda i: (0, 0))
    table_bytes = 4 * len_y * len_y

    outgoing = call(
        forward_y,
        "forward_y",
        jax.ShapeDtypeStruct((slabs, z_lo, lanes), jnp.bfloat16),
        pl.GridSpec(
            grid=(steps,),
            in_specs=[maps_spec, image_spec, table_spec, table_spec],
            out_specs=pl.BlockSpec((slabs, z_lo, 2 * LANES), lambda i: (0, 0, i)),
            scratch_shapes=[pltpu.VMEM((2 * half, len_y), jnp.bfloat16)],
        ),
        8 * steps * half * len_y * len_y,
        8 * steps * half * len_y + table_bytes,
    )(coil_maps, image_estimate, cosine, sine)
    outgoing, late_maps = lax.optimization_barrier((outgoing, coil_maps))
    arrived = lax.all_to_all(outgoing, "slab", split_axis=0, concat_axis=0, tiled=True)
    own_maps = maps_by_readout(late_maps, place)

    weight = jnp.transpose(sampled_blocks.astype(jnp.float32), (2, 0, 1))[:, None, :, None, :]
    weight = jnp.broadcast_to(weight, (block_count, part, frames, coils, ky_lo))
    back_z = call(
        z_work,
        "z_work",
        jax.ShapeDtypeStruct((slabs, readout, z_lo, LANES), jnp.bfloat16),
        pl.GridSpec(
            grid=(steps,),
            in_specs=[
                pl.BlockSpec((len_z, 2 * LANES), lambda i: (0, i)),
                pl.BlockSpec(
                    (2, frames, part, coils, ky_lo, len_z), lambda i: (0, 0, i, 0, 0, 0)
                ),
                pl.BlockSpec((block_count, LANES), lambda i: (0, 0)),
                table_spec,
                table_spec,
            ],
            out_specs=pl.BlockSpec((slabs, part, z_lo, LANES), lambda i: (0, i, 0, 0)),
            scratch_shapes=[pltpu.VMEM((len_z, 2 * LANES), jnp.bfloat16)],
        ),
        16 * steps * half * len_z * len_z,
        12 * steps * half * len_z + table_bytes,
    )(
        arrived.reshape(len_z, lanes),
        measured,
        weight.reshape(block_count, LANES),
        cosine,
        sine,
    )
    returned = lax.all_to_all(
        back_z.reshape(slabs * groups, z_part, LANES),
        ("slab", "coil"),
        split_axis=0,
        concat_axis=0,
        tiled=True,
    )

    pair = 2
    rows = 2 * frames * z_part
    total = call(
        backward_y,
        "backward_y",
        jax.ShapeDtypeStruct((groups, rows, len_y), jnp.bfloat16),
        pltpu.PrefetchScalarGridSpec(
            num_scalar_prefetch=1,
            grid=(chips // pair,),
            in_specs=[
                pl.BlockSpec((slabs, pair, z_lo, LANES), lambda i, s: (0, i, 0, 0)),
                pl.BlockSpec(
                    (chips, cores, 2, coils, z_part, len_y), lambda i, s: (0, 0, 0, 0, 0, 0)
                ),
                pl.BlockSpec((len_y, len_y), lambda i, s: (0, 0)),
                pl.BlockSpec((len_y, len_y), lambda i, s: (0, 0)),
            ],
            out_specs=pl.BlockSpec((groups, rows, len_y), lambda i, s: (0, 0, 0)),
            scratch_shapes=[
                pltpu.VMEM((2 * frames * pair * coils * z_lo, len_y), jnp.bfloat16),
                pltpu.VMEM((2, frames, z_part, len_y), jnp.float32),
            ],
        ),
        8 * steps * half * len_y * len_y,
        8 * steps * half * len_y + table_bytes,
    )(place, returned.reshape(slabs, chips, z_lo, LANES), own_maps, cosine, sine)

    whole = lax.all_to_all(total, "coil", split_axis=0, concat_axis=0, tiled=True)
    whole = whole.reshape(readout, cores, 2, frames, z_part, len_y)
    whole = jnp.transpose(whole, (2, 3, 0, 1, 4, 5)).astype(jnp.float32)
    return whole.reshape(2, frames, readout, z_lo, len_y)


def solution(mesh):
    body = jax.shard_map(
        shards,
        mesh=mesh,
        in_specs=(
            P(None, None, None, "slab", None),
            P(None, "coil", None, "slab", None),
            P(None, None, None, "coil", "slab", None),
            P(None, "slab", None),
            P(None, None),
            P(None, None),
        ),
        out_specs=P(None, None, None, "slab", None),
        check_vma=False,
    )

    def run(image_estimate, coil_maps, measured, sampled_blocks):
        cosine, sine = dft_tables(image_estimate.shape[4])
        return body(
            image_estimate, coil_maps, measured, sampled_blocks, jnp.asarray(cosine), jnp.asarray(sine)
        )

    return run
```

time: 179 us -> 174 us (0.972)
  blocking collectives: 89.5 us -> 14.2 us
  starting transfers between devices: 18.6 us -> 60.4 us
  waiting for transfers between devices: 53 us -> 80.3 us
    all_to_all x2 -> x0, blocking collectives: 76 us -> none  [the longest x1 60 us: shards(): lax.all_to_all(back_z.reshape(slabs, z_lo, lanes), 'slab', split_axis=0,...]
    ppermute x0 -> x8, starting transfers between devices: none -> 28.8 us  [the longest x7 22.5 us: maps_by_readout(): piece = lax.ppermute(piece, 'coil', [(i, i ^ cores * k) for i in devices])]
    all_to_all x0 -> x1, waiting for transfers between devices: none -> 24.2 us  [shards(): lax.all_to_all(back_z.reshape(slabs * groups, z_part, LANES), ('slab', 'c...]
    all_to_all x0 -> x1, starting transfers between devices: none -> 13 us  [shards(): lax.all_to_all(back_z.reshape(slabs * groups, z_part, LANES), ('slab', 'c...]
    ppermute x0 -> x8, waiting for transfers between devices: none -> 3.08 us  [the longest x7 2.14 us: maps_by_readout(): piece = lax.ppermute(piece, 'coil', [(i, i ^ cores * k) for i in devices])]
    pallas_call x3 -> x2, Pallas kernels: 7.37 us -> 8.58 us  [the longest x1 4.62 us: shards(): call(z_work, 'z_work', jax.ShapeDtypeStruct((slabs, readout, z_lo, LANES)...]
    unnamed x18 -> x24, local copies, waits for them, and re-layouts: 4.19 us -> 4.22 us
  transfers between devices with their start and end apart: 1 -> 10, of which waited for: 1 -> 4; matrix products, arithmetic and copies ran while one was open for 0% -> 0% of each run, Pallas kernels for 0% -> 0%
where the time goes in v2:
time: 174 us; the launch traced here: 173 us
  waiting for transfers between devices  80.3 us (46%)
  starting transfers between devices  60.4 us (35%)
  blocking collectives  14.2 us (8%)
  Pallas kernels  12.1 us (7%)
  local copies, waits for them, and re-layouts  4.41 us (3%)
    all_to_all x1, waiting for transfers between devices, shards(): lax.all_to_all(outgoing, 'slab', split_axis=0, concat_axis=0, tiled=True)  53 us
    all_to_all x1, waiting for transfers between devices, shards(): lax.all_to_all(back_z.reshape(slabs * groups, z_part, LANES), ('slab', 'c...  24.2 us
    ppermute x7, starting transfers between devices, maps_by_readout(): piece = lax.ppermute(piece, 'coil', [(i, i ^ cores * k) for i in devices])  22.5 us
    all_to_all x1, starting transfers between devices, shards(): lax.all_to_all(outgoing, 'slab', split_axis=0, concat_axis=0, tiled=True)  18.6 us
    all_to_all x1, blocking collectives, shards(): lax.all_to_all(total, 'coil', split_axis=0, concat_axis=0, tiled=True)  14.2 us
    all_to_all x1, starting transfers between devices, shards(): lax.all_to_all(back_z.reshape(slabs * groups, z_part, LANES), ('slab', 'c...  13 us
    ppermute x1, starting transfers between devices, maps_by_readout(): got = lax.ppermute(other, 'coil', [(i, i ^ 1) for i in devices])  6.21 us
    pallas_call x1, Pallas kernels, shards(): call(z_work, 'z_work', jax.ShapeDtypeStruct((slabs, readout, z_lo, LANES)...  4.62 us
  transfers between devices with their start and end apart: 10, of which 4 were waited for; matrix products, arithmetic and copies ran while one was open for 0% of the time, Pallas kernels for 0%

profile of v2, /device:TPU:1, one launch (start us, length us, event | category | flops | bytes accessed | tf_op | source)
XLA Modules:
  0.0 173.1 jit_solution(3080962131550484069)
XLA Ops:
  0.0 0.0 copy-start
  0.0 1.0 copy-done
  1.0 0.0 copy-start.3
  1.0 1.0 copy-done.3
  2.1 0.0 copy-start.4
  2.1 1.0 copy-done.4
  3.1 0.0 copy-start.6
  3.1 1.0 copy-done.6
  4.2 0.0 copy-start.8
  4.2 3.5 %forward_y.1 = bf16[32,16,1024]{2,1,0:T(8,128)(2,1)} custom-call(bf16[2,2,8,16,512]{4,3,2,1,0:T(8,128)(2,1)S(1)} %copy-done, bf16[2,2,8,16,512]{4,3,2,1,0:T(8,128)(2,1)S(1)} %copy-done.3, bf16[512,512]{1,0:T(8,128)(2,1)S(1)} %copy-done.6, bf16[512,512]{1,0:T(8,128)(2,1)S(1)} %copy-done.4), custom_call_target="tpu_custom_call" | custom-call | flops 1073741824 | bytes 3145728 | tf_op jit(solution)/shard_map/forward_y/pallas_call | solution.py:218
  7.7 0.0 copy-start.2
  7.7 0.0 copy-start.5
  7.7 0.0 copy-start.7
  7.7 18.6 %all-to-all-start = ((bf16[32,16,1024]{2,1,0:T(8,128)(2,1)}), bf16[32,16,1024]{2,1,0:T(8,128)(2,1)S(1)}, u32[]{:S(2)}, u32[]{:S(2)}) async-start(bf16[32,16,1024]{2,1,0:T(8,128)(2,1)} %forward_y.1), calls=%async_computation | async-start | bytes 2097152 | tf_op jit(solution)/shard_map/all_to_all | solution.py:232
  26.3 0.0 copy-done.8
  26.4 0.1 reshape.28.weight_ref
  26.5 53.0 %all-to-all-done = bf16[32,16,1024]{2,1,0:T(8,128)(2,1)S(1)} async-done(((bf16[32,16,1024]{2,1,0:T(8,128)(2,1)}), bf16[32,16,1024]{2,1,0:T(8,128)(2,1)S(1)}, u32[]{:S(2)}, u32[]{:S(2)}) %all-to-all-start) | async-done | bytes 1048608 | tf_op jit(solution)/shard_map/all_to_all | solution.py:232
  79.5 0.0 copy-done.2
  79.5 0.0 copy-done.5
  79.5 0.0 copy-done.7
  79.5 4.6 %z_work.1 = bf16[32,8,16,128]{3,2,1,0:T(8,128)(2,1)} custom-call(bf16[512,1024]{1,0:T(8,128)(2,1)S(1)} %bitcast.53, bf16[2,2,8,2,16,512]{5,4,3,2,1,0:T(8,128)(2,1)S(1)} %copy-done.2, f32[4,128]{1,0:T(4,128)S(1)} %reshape.28.weight_ref, bf16[512,512]{1,0:T(8,128)(2,1)S(1)} %copy-done.7, bf16[512,512]{1,0:T(8,128)(2,1)S(1)} %copy-done.5), custom_call_target="tpu_custom_call" | custom-call | flops 2147483648 | bytes 4194304 | tf_op jit(solution)/shard_map/z_work/pallas_call | solution.py:237
  84.1 0.0 copy-start.1
  84.1 13.0 %all-to-all-start.1 = ((bf16[512,8,128]{2,1,0:T(8,128)(2,1)}), bf16[512,8,128]{2,1,0:T(8,128)(2,1)S(1)}, u32[]{:S(2)}, u32[]{:S(2)}) async-start(bf16[512,8,128]{2,1,0:T(8,128)(2,1)} %bitcast.4), calls=%async_computation.1 | async-start | bytes 2097152 | tf_op jit(solution)/shard_map/all_to_all | solution.py:264
  97.2 0.0 copy-done.1
  97.3 6.2 %collective-permute-start = (bf16[2,2,8,8,512]{4,3,1,0,2:T(8,128)(2,1)S(1)}, bf16[2,2,8,8,512]{4,3,1,0,2:T(8,128)(2,1)S(1)}, u32[]{:S(2)}, u32[]{:S(2)}) collective-permute-start(bf16[2,2,8,8,512]{4,3,1,0,2:T(8,128)(2,1)S(1)} %bitcast.62), channel_id=1, source_target_pairs={{0,1},{1,0},{2,3},{3,2},{4,5},{5,4},{6,7},{7,6},{8,9},{9,8},{10,11... | collective-permute-start | bytes 786440 | tf_op jit(solution)/shard_map/ppermute | solution.py:184
  103.6 0.1 pad_add_fusion.place_ref
  103.7 0.9 collective-permute-done
  104.6 1.9 %collective-permute-start.6 = (bf16[2,2,2,8,512]{4,3,2,1,0:T(8,128)(2,1)S(1)}, bf16[2,2,2,8,512]{4,3,2,1,0:T(8,128)(2,1)S(1)}, u32[]{:S(2)}, u32[]{:S(2)}) collective-permute-start(bf16[2,2,2,8,512]{4,3,2,1,0:T(8,128)(2,1)S(1)} %fusion.8), channel_id=1, source_target_pairs={{0,12},{1,13},{2,14},{3,15},{4,8},{5,9},{6,10},{7,11},{8,4},{9,5},... | collective-permute-start | bytes 196616 | tf_op jit(solution)/shard_map/ppermute | solution.py:190
  106.6 0.1 fusion.14
  106.6 1.9 %collective-permute-start.7 = (bf16[2,2,2,8,512]{4,3,2,1,0:T(8,128)(2,1)S(1)}, bf16[2,2,2,8,512]{4,3,2,1,0:T(8,128)(2,1)S(1)}, u32[]{:S(2)}, u32[]{:S(2)}) collective-permute-start(bf16[2,2,2,8,512]{4,3,2,1,0:T(8,128)(2,1)S(1)} %get-tuple-element.9), channel_id=1, source_target_pairs={{0,14},{1,15},{2,12},{3,13},{4,10},{5,11},{6,8},{7,9},{8,6},{9,7},... | collective-permute-start | bytes 196616 | tf_op jit(solution)/shard_map/ppermute | solution.py:190
  108.5 5.7 %collective-permute-start.1 = (bf16[2,2,2,8,512]{4,3,2,1,0:T(8,128)(2,1)S(1)}, bf16[2,2,2,8,512]{4,3,2,1,0:T(8,128)(2,1)S(1)}, u32[]{:S(2)}, u32[]{:S(2)}) collective-permute-start(bf16[2,2,2,8,512]{4,3,2,1,0:T(8,128)(2,1)S(1)} %get-tuple-element.10), channel_id=1, source_target_pairs={{0,2},{1,3},{2,0},{3,1},{4,6},{5,7},{6,4},{7,5},{8,10},{9,11},{10,... | collective-permute-start | bytes 196616 | tf_op jit(solution)/shard_map/ppermute | solution.py:190
  114.3 1.9 %collective-permute-start.2 = (bf16[2,2,2,8,512]{4,3,2,1,0:T(8,128)(2,1)S(1)}, bf16[2,2,2,8,512]{4,3,2,1,0:T(8,128)(2,1)S(1)}, u32[]{:S(2)}, u32[]{:S(2)}) collective-permute-start(bf16[2,2,2,8,512]{4,3,2,1,0:T(8,128)(2,1)S(1)} %get-tuple-element.11), channel_id=1, source_target_pairs={{0,4},{1,5},{2,6},{3,7},{4,0},{5,1},{6,2},{7,3},{8,12},{9,13},{10,... | collective-permute-start | bytes 196616 | tf_op jit(solution)/shard_map/ppermute | solution.py:190
  116.2 3.1 %collective-permute-start.3 = (bf16[2,2,2,8,512]{4,3,2,1,0:T(8,128)(2,1)S(1)}, bf16[2,2,2,8,512]{4,3,2,1,0:T(8,128)(2,1)S(1)}, u32[]{:S(2)}, u32[]{:S(2)}) collective-permute-start(bf16[2,2,2,8,512]{4,3,2,1,0:T(8,128)(2,1)S(1)} %get-tuple-element.12), channel_id=1, source_target_pairs={{0,6},{1,7},{2,4},{3,5},{4,2},{5,3},{6,0},{7,1},{8,14},{9,15},{10,... | collective-permute-start | bytes 196616 | tf_op jit(solution)/shard_map/ppermute | solution.py:190
  119.3 0.0 collective-permute-done.1
  119.3 1.9 %collective-permute-start.4 = (bf16[2,2,2,8,512]{4,3,2,1,0:T(8,128)(2,1)S(1)}, bf16[2,2,2,8,512]{4,3,2,1,0:T(8,128)(2,1)S(1)}, u32[]{:S(2)}, u32[]{:S(2)}) collective-permute-start(bf16[2,2,2,8,512]{4,3,2,1,0:T(8,128)(2,1)S(1)} %get-tuple-element.13), channel_id=1, source_target_pairs={{0,8},{1,9},{2,10},{3,11},{4,12},{5,13},{6,14},{7,15},{8,0},{9,1},... | collective-permute-start | bytes 196616 | tf_op jit(solution)/shard_map/ppermute | solution.py:190
  121.3 0.0 collective-permute-done.2
  121.3 6.0 %collective-permute-start.5 = (bf16[2,2,2,8,512]{4,3,2,1,0:T(8,128)(2,1)S(1)}, bf16[2,2,2,8,512]{4,3,2,1,0:T(8,128)(2,1)S(1)}, u32[]{:S(2)}, u32[]{:S(2)}) collective-permute-start(bf16[2,2,2,8,512]{4,3,2,1,0:T(8,128)(2,1)S(1)} %get-tuple-element.14), channel_id=1, source_target_pairs={{0,10},{1,11},{2,8},{3,9},{4,14},{5,15},{6,12},{7,13},{8,2},{9,3},... | collective-permute-start | bytes 196616 | tf_op jit(solution)/shard_map/ppermute | solution.py:190
  127.4 0.0 collective-permute-done.3
  127.4 0.0 collective-permute-done.4
  127.4 2.1 %collective-permute-done.5 = bf16[2,2,2,8,512]{4,3,2,1,0:T(8,128)(2,1)S(1)} collective-permute-done((bf16[2,2,2,8,512]{4,3,2,1,0:T(8,128)(2,1)S(1)}, bf16[2,2,2,8,512]{4,3,2,1,0:T(8,128)(2,1)S(1)}, u32[]{:S(2)}, u32[]{:S(2)}) %collective-permute-start.5) | collective-permute-done | bytes 65568 | tf_op jit(solution)/shard_map/ppermute | solution.py:190
  129.5 0.0 collective-permute-done.6
  129.6 0.0 collective-permute-done.7
  129.6 24.2 %all-to-all-done.1 = bf16[512,8,128]{2,1,0:T(8,128)(2,1)S(1)} async-done(((bf16[512,8,128]{2,1,0:T(8,128)(2,1)}), bf16[512,8,128]{2,1,0:T(8,128)(2,1)S(1)}, u32[]{:S(2)}, u32[]{:S(2)}) %all-to-all-start.1) | async-done | bytes 1048608 | tf_op jit(solution)/shard_map/all_to_all | solution.py:264
  153.8 4.0 %backward_y.1 = bf16[16,32,512]{2,1,0:T(8,128)(2,1)S(1)} custom-call(s32[2]{0:T(128)S(1)} %pad_add_fusion.place_ref, bf16[32,8,16,128]{3,2,1,0:T(8,128)(2,1)S(1)} %bitcast.52, bf16[8,2,2,2,8,512]{5,4,3,2,1,0:T(8,128)(2,1)S(1)} %bitcast_dynamic-update-slice_fusion.maps_ref, bf16[512,512]{1,0:T(8,128)(2,1)S(1)} %copy-done.7, bf16[512,512]{1,0:T(8,128)(2,1)S(1)} %copy-done.5), custom_call_target="tpu_custom_call" | custom-call | flops 1073741824 | bytes 3145728 | tf_op jit(solution)/shard_map/backward_y/pallas_call | solution.py:274
  157.8 14.2 %all_to_all.15 = bf16[16,32,512]{2,1,0:T(8,128)(2,1)S(1)} all-to-all(bf16[16,32,512]{2,1,0:T(8,128)(2,1)S(1)} %backward_y.1), channel_id=1, replica_groups=mesh['slab'=32,'coil'=16] {'coil'}, dimensions={0} | all-to-all | bytes 1048576 | tf_op jit(solution)/shard_map/all_to_all | solution.py:299
  172.0 1.1 copy_bitcast_fusion
  (15 shorter events, 0.2 us)
Async XLA Ops:
  0.0 1.0 copy-start
  1.0 1.0 copy-start.3
  2.1 1.0 copy-start.4
  3.1 1.0 copy-start.6
  4.2 22.2 %copy-start.8 = (s32[2,16,4]{1,2,0:T(4,128)S(1)}, s32[2,16,4]{1,2,0:T(4,128)}, u32[]{:S(2)}) copy-start(s32[2,16,4]{1,2,0:T(4,128)} %param.9) | copy-start | bytes 1540
  7.7 71.8 %copy-start.2 = (bf16[2,2,8,2,16,512]{5,4,3,2,1,0:T(8,128)(2,1)S(1)}, bf16[2,2,8,2,16,512]{5,4,3,2,1,0:T(8,128)(2,1)}, u32[]{:S(2)}) copy-start(bf16[2,2,8,2,16,512]{5,4,3,2,1,0:T(8,128)(2,1)} %measured_ref.1) | copy-start | bytes 3145732
  7.7 71.8 %copy-start.5 = (bf16[512,512]{1,0:T(8,128)(2,1)S(1)}, bf16[512,512]{1,0:T(8,128)(2,1)}, u32[]{:S(2)}) copy-start(bf16[512,512]{1,0:T(8,128)(2,1)} %constant.70.clone.sin_ref) | copy-start | bytes 1572868
  7.7 71.8 %copy-start.7 = (bf16[512,512]{1,0:T(8,128)(2,1)S(1)}, bf16[512,512]{1,0:T(8,128)(2,1)}, u32[]{:S(2)}) copy-start(bf16[512,512]{1,0:T(8,128)(2,1)} %constant.69.clone.cos_ref) | copy-start | bytes 1572868
  7.7 71.8 %all-to-all-start = ((bf16[32,16,1024]{2,1,0:T(8,128)(2,1)}), bf16[32,16,1024]{2,1,0:T(8,128)(2,1)S(1)}, u32[]{:S(2)}, u32[]{:S(2)}) async-start(bf16[32,16,1024]{2,1,0:T(8,128)(2,1)} %forward_y.1), calls=%async_computation | async-start | bytes 2097152 | tf_op jit(solution)/shard_map/all_to_all | solution.py:232
  84.1 13.1 %copy-start.1 = (bf16[2,2,8,16,512]{4,3,2,1,0:T(8,128)(2,1)S(1)}, bf16[2,2,8,16,512]{4,3,2,1,0:T(8,128)(2,1)}, u32[]{:S(2)}) copy-start(bf16[2,2,8,16,512]{4,3,2,1,0:T(8,128)(2,1)} %maps_ref.1) | copy-start | bytes 1572868
  84.1 69.7 %all-to-all-start.1 = ((bf16[512,8,128]{2,1,0:T(8,128)(2,1)}), bf16[512,8,128]{2,1,0:T(8,128)(2,1)S(1)}, u32[]{:S(2)}, u32[]{:S(2)}) async-start(bf16[512,8,128]{2,1,0:T(8,128)(2,1)} %bitcast.4), calls=%async_computation.1 | async-start | bytes 2097152 | tf_op jit(solution)/shard_map/all_to_all | solution.py:264
  97.3 7.4 %collective-permute-start = (bf16[2,2,8,8,512]{4,3,1,0,2:T(8,128)(2,1)S(1)}, bf16[2,2,8,8,512]{4,3,1,0,2:T(8,128)(2,1)S(1)}, u32[]{:S(2)}, u32[]{:S(2)}) collective-permute-start(bf16[2,2,8,8,512]{4,3,1,0,2:T(8,128)(2,1)S(1)} %bitcast.62), channel_id=1, source_target_pairs={{0,1},{1,0},{2,3},{3,2},{4,5},{5,4},{6,7},{7,6},{8,9},{9,8},{10,11... | collective-permute-start | bytes 786440 | tf_op jit(solution)/shard_map/ppermute | solution.py:184
  104.6 24.9 %collective-permute-start.6 = (bf16[2,2,2,8,512]{4,3,2,1,0:T(8,128)(2,1)S(1)}, bf16[2,2,2,8,512]{4,3,2,1,0:T(8,128)(2,1)S(1)}, u32[]{:S(2)}, u32[]{:S(2)}) collective-permute-start(bf16[2,2,2,8,512]{4,3,2,1,0:T(8,128)(2,1)S(1)} %fusion.8), channel_id=1, source_target_pairs={{0,12},{1,13},{2,14},{3,15},{4,8},{5,9},{6,10},{7,11},{8,4},{9,5},... | collective-permute-start | bytes 196616 | tf_op jit(solution)/shard_map/ppermute | solution.py:190
  106.6 23.0 %collective-permute-start.7 = (bf16[2,2,2,8,512]{4,3,2,1,0:T(8,128)(2,1)S(1)}, bf16[2,2,2,8,512]{4,3,2,1,0:T(8,128)(2,1)S(1)}, u32[]{:S(2)}, u32[]{:S(2)}) collective-permute-start(bf16[2,2,2,8,512]{4,3,2,1,0:T(8,128)(2,1)S(1)} %get-tuple-element.9), channel_id=1, source_target_pairs={{0,14},{1,15},{2,12},{3,13},{4,10},{5,11},{6,8},{7,9},{8,6},{9,7},... | collective-permute-start | bytes 196616 | tf_op jit(solution)/shard_map/ppermute | solution.py:190
  108.5 10.8 %collective-permute-start.1 = (bf16[2,2,2,8,512]{4,3,2,1,0:T(8,128)(2,1)S(1)}, bf16[2,2,2,8,512]{4,3,2,1,0:T(8,128)(2,1)S(1)}, u32[]{:S(2)}, u32[]{:S(2)}) collective-permute-start(bf16[2,2,2,8,512]{4,3,2,1,0:T(8,128)(2,1)S(1)} %get-tuple-element.10), channel_id=1, source_target_pairs={{0,2},{1,3},{2,0},{3,1},{4,6},{5,7},{6,4},{7,5},{8,10},{9,11},{10,... | collective-permute-start | bytes 196616 | tf_op jit(solution)/shard_map/ppermute | solution.py:190
  114.3 7.0 %collective-permute-start.2 = (bf16[2,2,2,8,512]{4,3,2,1,0:T(8,128)(2,1)S(1)}, bf16[2,2,2,8,512]{4,3,2,1,0:T(8,128)(2,1)S(1)}, u32[]{:S(2)}, u32[]{:S(2)}) collective-permute-start(bf16[2,2,2,8,512]{4,3,2,1,0:T(8,128)(2,1)S(1)} %get-tuple-element.11), channel_id=1, source_target_pairs={{0,4},{1,5},{2,6},{3,7},{4,0},{5,1},{6,2},{7,3},{8,12},{9,13},{10,... | collective-permute-start | bytes 196616 | tf_op jit(solution)/shard_map/ppermute | solution.py:190
  116.2 11.1 %collective-permute-start.3 = (bf16[2,2,2,8,512]{4,3,2,1,0:T(8,128)(2,1)S(1)}, bf16[2,2,2,8,512]{4,3,2,1,0:T(8,128)(2,1)S(1)}, u32[]{:S(2)}, u32[]{:S(2)}) collective-permute-start(bf16[2,2,2,8,512]{4,3,2,1,0:T(8,128)(2,1)S(1)} %get-tuple-element.12), channel_id=1, source_target_pairs={{0,6},{1,7},{2,4},{3,5},{4,2},{5,3},{6,0},{7,1},{8,14},{9,15},{10,... | collective-permute-start | bytes 196616 | tf_op jit(solution)/shard_map/ppermute | solution.py:190
  119.3 8.0 %collective-permute-start.4 = (bf16[2,2,2,8,512]{4,3,2,1,0:T(8,128)(2,1)S(1)}, bf16[2,2,2,8,512]{4,3,2,1,0:T(8,128)(2,1)S(1)}, u32[]{:S(2)}, u32[]{:S(2)}) collective-permute-start(bf16[2,2,2,8,512]{4,3,2,1,0:T(8,128)(2,1)S(1)} %get-tuple-element.13), channel_id=1, source_target_pairs={{0,8},{1,9},{2,10},{3,11},{4,12},{5,13},{6,14},{7,15},{8,0},{9,1},... | collective-permute-start | bytes 196616 | tf_op jit(solution)/shard_map/ppermute | solution.py:190
  121.3 8.2 %collective-permute-start.5 = (bf16[2,2,2,8,512]{4,3,2,1,0:T(8,128)(2,1)S(1)}, bf16[2,2,2,8,512]{4,3,2,1,0:T(8,128)(2,1)S(1)}, u32[]{:S(2)}, u32[]{:S(2)}) collective-permute-start(bf16[2,2,2,8,512]{4,3,2,1,0:T(8,128)(2,1)S(1)} %get-tuple-element.14), channel_id=1, source_target_pairs={{0,10},{1,11},{2,8},{3,9},{4,14},{5,15},{6,12},{7,13},{8,2},{9,3},... | collective-permute-start | bytes 196616 | tf_op jit(solution)/shard_map/ppermute | solution.py:190

commit v3 on v0

v3 whole, which is shorter than its diff:
```python
import math

import jax
import jax.numpy as jnp
import ml_dtypes
import numpy as np
from jax import lax
from jax.experimental import pallas as pl
from jax.experimental.pallas import tpu as pltpu
from jax.sharding import PartitionSpec as P

LANES = 128
VMEM_SOME = 40 * 1024 * 1024
VMEM_ALL = 62 * 1024 * 1024


def dft_tables(length):
    indices = np.arange(length)
    angles = (indices[:, None] * indices[None, :] % length) * (2.0 * math.pi / length)
    cosine = (np.cos(angles) / math.sqrt(length)).astype(ml_dtypes.bfloat16)
    sine = (np.sin(angles) / math.sqrt(length)).astype(ml_dtypes.bfloat16)
    return cosine, sine


def swap_runs(blocks, run):
    count = len(blocks)
    rows, lanes = blocks[0].shape
    position = lax.broadcasted_iota(jnp.int32, (rows, lanes), 1) // run
    moved = [pltpu.roll(b, i * run, 1) if i else b for i, b in enumerate(blocks)]
    moved = [moved[-k % count] for k in range(count)]
    step = 1
    while step < count:
        chosen = (position & step) != 0
        moved = [jnp.where(chosen, moved[(k - step) % count], moved[k]) for k in range(count)]
        step *= 2
    return [pltpu.roll(b, lanes - j * run, 1) if j else b for j, b in enumerate(moved)]


def forward_y(maps_ref, image_ref, cos_ref, sin_ref, out_ref, lhs):
    _, coils, readout, z_lo, len_y = maps_ref.shape
    frames = image_ref.shape[1]
    steps = lhs.shape[0]
    part = readout // steps
    group = part * frames * coils
    half = group * z_lo
    run = LANES // group
    for i in range(steps):
        for x in range(part):
            for f in range(frames):
                image_re = image_ref[0, f, i * part + x].astype(jnp.float32)
                image_im = image_ref[1, f, i * part + x].astype(jnp.float32)
                for c in range(coils):
                    map_re = maps_ref[0, c, i * part + x].astype(jnp.float32)
                    map_im = maps_ref[1, c, i * part + x].astype(jnp.float32)
                    row = ((x * frames + f) * coils + c) * z_lo
                    coil_re = map_re * image_re - map_im * image_im
                    coil_im = map_re * image_im + map_im * image_re
                    lhs[i, row : row + z_lo] = coil_re.astype(jnp.bfloat16)
                    lhs[i, row + half : row + half + z_lo] = coil_im.astype(jnp.bfloat16)
        by_cos = jnp.dot(lhs[i], cos_ref[...], preferred_element_type=jnp.float32)
        by_sin = jnp.dot(lhs[i], sin_ref[...], preferred_element_type=jnp.float32)
        for p, along in enumerate((by_cos[:half] + by_sin[half:], by_cos[half:] - by_sin[:half])):
            lane = (2 * i + p) * LANES
            for t in range(len_y // LANES):
                block = along[:, t * LANES : (t + 1) * LANES]
                block = [block[u * z_lo : (u + 1) * z_lo] for u in range(group)]
                for u, rows in enumerate(swap_runs(block, run)):
                    out_ref[t * group + u, :, lane : lane + LANES] = rows.astype(jnp.bfloat16)


def z_work(arrived_ref, measured_ref, weight_ref, cos_ref, sin_ref, out_ref, residual):
    _, frames, readout, coils, ky_lo, len_z = measured_ref.shape
    blocks = weight_ref.shape[0]
    width = weight_ref.shape[1]
    depth = len_z // blocks
    steps = arrived_ref.shape[1] // (2 * width)
    part = readout // steps
    slabs, _, z_lo, _ = out_ref.shape
    for i in range(steps):
        mid, end = (2 * i + 1) * width, (2 * i + 2) * width
        arrived = arrived_ref[:, mid - width : end]
        by_cos = jnp.dot(cos_ref[...], arrived, preferred_element_type=jnp.float32)
        by_sin = jnp.dot(sin_ref[...], arrived, preferred_element_type=jnp.float32)
        target = []
        for p in range(2):
            lines = [
                measured_ref[p, f, i * part + x].reshape(coils * ky_lo, len_z)
                for x in range(part)
                for f in range(frames)
            ]
            target.append(jnp.concatenate(lines, axis=0).T.astype(jnp.float32))
        spectrum_re = by_cos[:, :width] + by_sin[:, width:]
        spectrum_im = by_cos[:, width:] - by_sin[:, :width]
        for b in range(blocks):
            rows = slice(b * depth, (b + 1) * depth)
            weight = weight_ref[b : b + 1, :]
            resid_re = weight * (spectrum_re[rows] - target[0][rows])
            resid_im = weight * (spectrum_im[rows] - target[1][rows])
            residual[rows, mid - width : mid] = resid_re.astype(jnp.bfloat16)
            residual[rows, mid:end] = resid_im.astype(jnp.bfloat16)
    run = width // part
    lower = lax.broadcasted_iota(jnp.int32, (len_z, width), 1) < run
    for i in range(steps):
        rows = residual[:, 2 * i * width : (2 * i + 2) * width]
        by_cos = jnp.dot(cos_ref[...], rows, preferred_element_type=jnp.float32)
        by_sin = jnp.dot(sin_ref[...], rows, preferred_element_type=jnp.float32)
        back_re = by_cos[:, :width] - by_sin[:, width:]
        back_im = by_cos[:, width:] + by_sin[:, :width]
        sent = (
            jnp.where(lower, back_re, pltpu.roll(back_im, run, 1)),
            jnp.where(lower, pltpu.roll(back_re, run, 1), back_im),
        )
        for x in range(part):
            out_ref[:, i * part + x] = sent[x].reshape(slabs, z_lo, width).astype(jnp.bfloat16)


def backward_y(place_ref, returned_ref, maps_ref, cos_ref, sin_ref, out_ref, lhs):
    chip, core = place_ref[0], place_ref[1]
    _, chips, rows, _ = returned_ref.shape
    _, cores, _, coils, z_part, len_y = maps_ref.shape
    steps, height, _ = lhs.shape
    pair = chips // steps
    half = height // 2
    frames = half // (pair * coils * rows)
    group = 2 * frames * coils
    run = LANES // group
    zero = jnp.zeros((z_part, len_y), jnp.float32)
    sums = [[zero, zero] for _ in range(frames)]
    for i in range(steps):
        for q in range(pair):
            for t in range(len_y // LANES):
                block = returned_ref[t * group : (t + 1) * group, i * pair + q].astype(jnp.float32)
                block = swap_runs([block[u] for u in range(group)], run)
                for p in range(2):
                    for f in range(frames):
                        for c in range(coils):
                            row = p * half + ((f * pair + q) * coils + c) * rows
                            lhs[i, row : row + rows, t * LANES : (t + 1) * LANES] = block[
                                (p * frames + f) * coils + c
                            ].astype(jnp.bfloat16)
        by_cos = jnp.dot(lhs[i], cos_ref[...], preferred_element_type=jnp.float32)
        by_sin = jnp.dot(lhs[i], sin_ref[...], preferred_element_type=jnp.float32)
        back_re = by_cos[:half] - by_sin[half:]
        back_im = by_cos[half:] + by_sin[:half]
        for q in range(pair):
            source = (i * pair + q) ^ chip
            for k in range(cores):
                for c in range(coils):
                    map_re = maps_ref[source, k ^ core, 0, c].astype(jnp.float32)
                    map_im = maps_ref[source, k ^ core, 1, c].astype(jnp.float32)
                    for f in range(frames):
                        row = ((f * pair + q) * coils + c) * rows + k * z_part
                        re, im = back_re[row : row + z_part], back_im[row : row + z_part]
                        sums[f][0] = sums[f][0] + (map_re * re + map_im * im)
                        sums[f][1] = sums[f][1] + (map_re * im - map_im * re)
    whole = jnp.concatenate([sums[f][p] for p in range(2) for f in range(frames)], axis=0)
    out_ref[...] = jnp.broadcast_to(whole.astype(jnp.bfloat16)[None], out_ref.shape)


def call(kernel, name, out_shape, in_spaces, out_space, scratch, flops, bytes_accessed, vmem):
    return pl.pallas_call(
        kernel,
        name=name,
        out_shape=out_shape,
        in_specs=[pl.BlockSpec(memory_space=space) for space in in_spaces],
        out_specs=pl.BlockSpec(memory_space=out_space),
        scratch_shapes=scratch,
        compiler_params=pltpu.CompilerParams(vmem_limit_bytes=vmem),
        cost_estimate=pl.CostEstimate(
            flops=flops, bytes_accessed=bytes_accessed, transcendentals=0
        ),
    )


def maps_by_readout(coil_maps, place):
    cores = 2
    chips = lax.axis_size("coil") // cores
    chip, core = place[0], place[1]
    _, coils, readout, z_lo, len_y = coil_maps.shape
    halves = coil_maps.reshape(2, coils, readout, cores, z_lo // cores, len_y)
    own = lax.dynamic_index_in_dim(halves, core, 3, keepdims=False)
    other = lax.dynamic_index_in_dim(halves, 1 - core, 3, keepdims=False)
    devices = range(chips * cores)
    got = lax.ppermute(other, "coil", [(i, i ^ 1) for i in devices])
    both = jnp.stack([own, got])
    pieces = []
    for k in range(chips):
        piece = lax.dynamic_index_in_dim(both, chip ^ k, 3, keepdims=False)
        if k:
            piece = lax.ppermute(piece, "coil", [(i, i ^ (cores * k)) for i in devices])
        pieces.append(piece)
    return jnp.stack(pieces)


def send_forward(coil_maps, image_estimate, cosine, sine, slabs):
    _, frames, readout, z_lo, len_y = image_estimate.shape
    coils = coil_maps.shape[1]
    group = LANES // (len_y // slabs)
    part = group // (coils * frames)
    steps = readout // part
    half = group * z_lo
    return call(
        forward_y,
        "forward_y",
        jax.ShapeDtypeStruct((slabs, z_lo, steps * 2 * LANES), jnp.bfloat16),
        [pltpu.VMEM] * 4,
        pltpu.VMEM,
        [pltpu.VMEM((steps, 2 * half, len_y), jnp.bfloat16)],
        8 * steps * half * len_y * len_y,
        8 * steps * half * len_y + 4 * len_y * len_y,
        VMEM_ALL,
    )(coil_maps, image_estimate, cosine, sine)


def send_back(arrived, measured, sampled_blocks, cosine, sine):
    slabs, z_lo, lanes = arrived.shape
    _, frames, readout, coils, ky_lo, len_z = measured.shape
    block_count = sampled_blocks.shape[2]
    steps = lanes // (2 * LANES)
    part = readout // steps
    weight = jnp.transpose(sampled_blocks.astype(jnp.float32), (2, 0, 1))[:, None, :, None, :]
    weight = jnp.broadcast_to(weight, (block_count, part, frames, coils, ky_lo))
    return call(
        z_work,
        "z_work",
        jax.ShapeDtypeStruct((slabs, readout, z_lo, LANES), jnp.bfloat16),
        [pltpu.VMEM] * 5,
        pltpu.VMEM,
        [pltpu.VMEM((len_z, lanes), jnp.bfloat16)],
        8 * lanes * len_z * len_z,
        6 * lanes * len_z + 4 * len_z * len_z,
        VMEM_SOME,
    )(
        arrived.reshape(len_z, lanes),
        measured,
        weight.reshape(block_count, LANES),
        cosine,
        sine,
    )


def combine(returned, own_maps, place, cosine, sine):
    slabs, chips, z_lo, _ = returned.shape
    _, cores, _, coils, z_part, len_y = own_maps.shape
    frames = LANES // (len_y // slabs * 2 * coils)
    pair = 2
    steps = chips // pair
    height = 2 * frames * pair * coils * z_lo
    return call(
        backward_y,
        "backward_y",
        jax.ShapeDtypeStruct((chips * cores, 2 * frames * z_part, len_y), jnp.bfloat16),
        [pltpu.SMEM] + [pltpu.VMEM] * 4,
        pltpu.VMEM,
        [pltpu.VMEM((steps, height, len_y), jnp.bfloat16)],
        4 * steps * height * len_y * len_y,
        4 * steps * height * len_y + 4 * len_y * len_y,
        VMEM_SOME,
    )(place, returned, own_maps, cosine, sine)


def shards(image_estimate, coil_maps, measured, sampled_blocks, cosine, sine):
    slabs = lax.axis_size("slab")
    groups = lax.axis_size("coil")
    _, frames, readout, z_lo, len_y = image_estimate.shape
    cores = 2
    z_part = z_lo // cores
    me = lax.axis_index("coil")
    place = jnp.stack([me // cores, me % cores]).astype(jnp.int32)

    outgoing = send_forward(coil_maps, image_estimate, cosine, sine, slabs)
    outgoing, late_maps = lax.optimization_barrier((outgoing, coil_maps))
    arrived = lax.all_to_all(outgoing, "slab", split_axis=0, concat_axis=0, tiled=True)
    own_maps = maps_by_readout(late_maps, place)
    back_z = send_back(arrived, measured, sampled_blocks, cosine, sine)
    returned = lax.all_to_all(
        back_z.reshape(slabs * groups, z_part, LANES),
        ("slab", "coil"),
        split_axis=0,
        concat_axis=0,
        tiled=True,
    )
    total = combine(
        returned.reshape(slabs, groups // cores, z_lo, LANES), own_maps, place, cosine, sine
    )
    whole = lax.all_to_all(total, "coil", split_axis=0, concat_axis=0, tiled=True)
    whole = whole.reshape(readout, cores, 2, frames, z_part, len_y)
    whole = jnp.transpose(whole, (2, 3, 0, 1, 4, 5)).astype(jnp.float32)
    return whole.reshape(2, frames, readout, z_lo, len_y)


def solution(mesh):
    body = jax.shard_map(
        shards,
        mesh=mesh,
        in_specs=(
            P(None, None, None, "slab", None),
            P(None, "coil", None, "slab", None),
            P(None, None, None, "coil", "slab", None),
            P(None, "slab", None),
            P(None, None),
            P(None, None),
        ),
        out_specs=P(None, None, None, "slab", None),
        check_vma=False,
    )

    def run(image_estimate, coil_maps, measured, sampled_blocks):
        cosine, sine = dft_tables(image_estimate.shape[4])
        return body(
            image_estimate, coil_maps, measured, sampled_blocks, jnp.asarray(cosine), jnp.asarray(sine)
        )

    return run
```

time: 357 us -> 167 us (0.47)
  waiting for transfers between devices: 175 us -> 80.3 us
  blocking collectives: 59.9 us -> 14.2 us
  local copies, waits for them, and re-layouts: 42.2 us -> 0.25 us
  starting transfers between devices: 18.5 us -> 60.4 us
  matrix products: 31.3 us -> 0 us
  other arithmetic: 15.3 us -> 1.25 us
  between operations: 13.5 us -> 0.38 us
  Pallas kernels: 0 us -> 9.91 us
    psum x1 -> x0, waiting for transfers between devices: 129 us -> none  [shards(): return lax.psum(partial_sum, 'coil')]
    all_to_all x1, blocking collectives: 59.9 us -> 14.2 us  [shards(): lax.all_to_all(total, 'coil', split_axis=0, concat_axis=0, tiled=True)]
    dot_general x4 -> x0, matrix products: 31.3 us -> none  [the longest x1 10.9 us: z_work(): jnp.einsum('qfxclk,qkphz->fxcphlz', residual, table_zi.reshape(2, len_z,...]
    all_to_all x1 -> x2, waiting for transfers between devices: 46.6 us -> 77.2 us  [the longest x1 53 us: shards(): lax.all_to_all(outgoing, 'slab', split_axis=0, concat_axis=0, tiled=True)]
    ppermute x0 -> x8, starting transfers between devices: none -> 28.8 us  [the longest x7 22.5 us: maps_by_readout(): piece = lax.ppermute(piece, 'coil', [(i, i ^ cores * k) for i in devices])]
    convert_element_type x3 -> x0, local copies, waits for them, and re-layouts: 24.4 us -> none  [the longest x1 12.9 us: z_work(): back_z.astype(jnp.bfloat16)]
    all_to_all x1 -> x2, starting transfers between devices: 18.5 us -> 31.7 us  [the longest x1 18.6 us: shards(): lax.all_to_all(outgoing, 'slab', split_axis=0, concat_axis=0, tiled=True)]
    another operation x4 -> x1, other arithmetic: 12.6 us -> 0.08 us  [shards(): place = jnp.stack([me // cores, me % cores]).astype(jnp.int32)]
  transfers between devices with their start and end apart: 2 -> 10, of which waited for: 2 -> 4; matrix products, arithmetic and copies ran while one was open for 2% -> 0% of each run, Pallas kernels for 0% -> 0%
where the time goes in v3:
time: 167 us
  waiting for transfers between devices  80.3 us (48%)
  starting transfers between devices  60.4 us (36%)
  blocking collectives  14.2 us (9%)
  Pallas kernels  9.91 us (6%)
    all_to_all x1, waiting for transfers between devices, shards(): lax.all_to_all(outgoing, 'slab', split_axis=0, concat_axis=0, tiled=True)  53 us
    all_to_all x1, waiting for transfers between devices, shards(): lax.all_to_all(back_z.reshape(slabs * groups, z_part, LANES), ('slab', 'c...  24.2 us
    ppermute x7, starting transfers between devices, maps_by_readout(): piece = lax.ppermute(piece, 'coil', [(i, i ^ cores * k) for i in devices])  22.5 us
    all_to_all x1, starting transfers between devices, shards(): lax.all_to_all(outgoing, 'slab', split_axis=0, concat_axis=0, tiled=True)  18.6 us
    all_to_all x1, blocking collectives, shards(): lax.all_to_all(total, 'coil', split_axis=0, concat_axis=0, tiled=True)  14.2 us
    all_to_all x1, starting transfers between devices, shards(): lax.all_to_all(back_z.reshape(slabs * groups, z_part, LANES), ('slab', 'c...  13 us
    ppermute x1, starting transfers between devices, maps_by_readout(): got = lax.ppermute(other, 'coil', [(i, i ^ 1) for i in devices])  6.21 us
    pallas_call x1, Pallas kernels, send_forward(): call(forward_y, 'forward_y', jax.ShapeDtypeStruct((slabs, z_lo, steps * 2...  4.02 us
  transfers between devices with their start and end apart: 10, of which 4 were waited for; matrix products, arithmetic and copies ran while one was open for 0% of the time, Pallas kernels for 0%

profile of v3, /device:TPU:1, one launch (start us, length us, event | category | flops | bytes accessed | tf_op | source)
XLA Modules:
  0.0 166.8 jit_solution(11784905661048258931)
XLA Ops:
  0.0 0.0 copy-start.4
  0.0 4.0 %forward_y.1 = bf16[32,16,1024]{2,1,0:T(8,128)(2,1)} custom-call(bf16[2,2,8,16,512]{4,3,2,1,0:T(8,128)(2,1)} %maps_ref.1, bf16[2,2,8,16,512]{4,3,2,1,0:T(8,128)(2,1)} %image_ref.1, bf16[512,512]{1,0:T(8,128)(2,1)} %constant.69.clone.cos_ref, bf16[512,512]{1,0:T(8,128)(2,1)} %constant.70.clone.sin_ref), custom_call_target="tpu_custom_call" | custom-call | flops 1073741824 | bytes 3145728 | tf_op jit(solution)/shard_map/forward_y/pallas_call | solution.py:202
  4.0 0.0 copy-start
  4.0 0.0 copy-start.1
  4.0 0.0 copy-start.2
  4.0 18.6 %all-to-all-start = ((bf16[32,16,1024]{2,1,0:T(8,128)(2,1)}), bf16[32,16,1024]{2,1,0:T(8,128)(2,1)S(1)}, u32[]{:S(2)}, u32[]{:S(2)}) async-start(bf16[32,16,1024]{2,1,0:T(8,128)(2,1)} %forward_y.1), calls=%async_computation | async-start | bytes 2097152 | tf_op jit(solution)/shard_map/all_to_all | solution.py:273
  22.7 0.0 copy-done.4
  22.7 0.1 reshape.28.weight_ref
  22.8 53.0 %all-to-all-done = bf16[32,16,1024]{2,1,0:T(8,128)(2,1)S(1)} async-done(((bf16[32,16,1024]{2,1,0:T(8,128)(2,1)}), bf16[32,16,1024]{2,1,0:T(8,128)(2,1)S(1)}, u32[]{:S(2)}, u32[]{:S(2)}) %all-to-all-start) | async-done | bytes 1048608 | tf_op jit(solution)/shard_map/all_to_all | solution.py:273
  75.8 0.0 copy-done
  75.8 0.0 copy-done.1
  75.8 0.0 copy-done.2
  75.8 3.5 %z_work.1 = bf16[32,8,16,128]{3,2,1,0:T(8,128)(2,1)} custom-call(bf16[512,1024]{1,0:T(8,128)(2,1)S(1)} %bitcast.53, bf16[2,2,8,2,16,512]{5,4,3,2,1,0:T(8,128)(2,1)S(1)} %copy-done, f32[4,128]{1,0:T(4,128)S(1)} %reshape.28.weight_ref, bf16[512,512]{1,0:T(8,128)(2,1)S(1)} %copy-done.2, bf16[512,512]{1,0:T(8,128)(2,1)S(1)} %copy-done.1), custom_call_target="tpu_custom_call" | custom-call | flops 2147483648 | bytes 4194304 | tf_op jit(solution)/shard_map/z_work/pallas_call | solution.py:223
  79.3 0.0 copy-start.3
  79.3 13.0 %all-to-all-start.1 = ((bf16[512,8,128]{2,1,0:T(8,128)(2,1)}), bf16[512,8,128]{2,1,0:T(8,128)(2,1)S(1)}, u32[]{:S(2)}, u32[]{:S(2)}) async-start(bf16[512,8,128]{2,1,0:T(8,128)(2,1)} %bitcast.4), calls=%async_computation.1 | async-start | bytes 2097152 | tf_op jit(solution)/shard_map/all_to_all | solution.py:276
  92.4 0.0 copy-done.3
  92.4 6.2 %collective-permute-start = (bf16[2,2,8,8,512]{4,3,1,0,2:T(8,128)(2,1)S(1)}, bf16[2,2,8,8,512]{4,3,1,0,2:T(8,128)(2,1)S(1)}, u32[]{:S(2)}, u32[]{:S(2)}) collective-permute-start(bf16[2,2,8,8,512]{4,3,1,0,2:T(8,128)(2,1)S(1)} %bitcast.62), channel_id=1, source_target_pairs={{0,1},{1,0},{2,3},{3,2},{4,5},{5,4},{6,7},{7,6},{8,9},{9,8},{10,11... | collective-permute-start | bytes 786440 | tf_op jit(solution)/shard_map/ppermute | solution.py:184
  98.8 0.1 pad_add_fusion.place_ref
  98.9 0.9 collective-permute-done
  99.8 1.9 %collective-permute-start.6 = (bf16[2,2,2,8,512]{4,3,2,1,0:T(8,128)(2,1)S(1)}, bf16[2,2,2,8,512]{4,3,2,1,0:T(8,128)(2,1)S(1)}, u32[]{:S(2)}, u32[]{:S(2)}) collective-permute-start(bf16[2,2,2,8,512]{4,3,2,1,0:T(8,128)(2,1)S(1)} %fusion.8), channel_id=1, source_target_pairs={{0,12},{1,13},{2,14},{3,15},{4,8},{5,9},{6,10},{7,11},{8,4},{9,5},... | collective-permute-start | bytes 196616 | tf_op jit(solution)/shard_map/ppermute | solution.py:190
  101.7 0.1 fusion.14
  101.8 1.9 %collective-permute-start.7 = (bf16[2,2,2,8,512]{4,3,2,1,0:T(8,128)(2,1)S(1)}, bf16[2,2,2,8,512]{4,3,2,1,0:T(8,128)(2,1)S(1)}, u32[]{:S(2)}, u32[]{:S(2)}) collective-permute-start(bf16[2,2,2,8,512]{4,3,2,1,0:T(8,128)(2,1)S(1)} %get-tuple-element.9), channel_id=1, source_target_pairs={{0,14},{1,15},{2,12},{3,13},{4,10},{5,11},{6,8},{7,9},{8,6},{9,7},... | collective-permute-start | bytes 196616 | tf_op jit(solution)/shard_map/ppermute | solution.py:190
  103.7 5.7 %collective-permute-start.1 = (bf16[2,2,2,8,512]{4,3,2,1,0:T(8,128)(2,1)S(1)}, bf16[2,2,2,8,512]{4,3,2,1,0:T(8,128)(2,1)S(1)}, u32[]{:S(2)}, u32[]{:S(2)}) collective-permute-start(bf16[2,2,2,8,512]{4,3,2,1,0:T(8,128)(2,1)S(1)} %get-tuple-element.10), channel_id=1, source_target_pairs={{0,2},{1,3},{2,0},{3,1},{4,6},{5,7},{6,4},{7,5},{8,10},{9,11},{10,... | collective-permute-start | bytes 196616 | tf_op jit(solution)/shard_map/ppermute | solution.py:190
  109.5 1.9 %collective-permute-start.2 = (bf16[2,2,2,8,512]{4,3,2,1,0:T(8,128)(2,1)S(1)}, bf16[2,2,2,8,512]{4,3,2,1,0:T(8,128)(2,1)S(1)}, u32[]{:S(2)}, u32[]{:S(2)}) collective-permute-start(bf16[2,2,2,8,512]{4,3,2,1,0:T(8,128)(2,1)S(1)} %get-tuple-element.11), channel_id=1, source_target_pairs={{0,4},{1,5},{2,6},{3,7},{4,0},{5,1},{6,2},{7,3},{8,12},{9,13},{10,... | collective-permute-start | bytes 196616 | tf_op jit(solution)/shard_map/ppermute | solution.py:190
  111.4 3.1 %collective-permute-start.3 = (bf16[2,2,2,8,512]{4,3,2,1,0:T(8,128)(2,1)S(1)}, bf16[2,2,2,8,512]{4,3,2,1,0:T(8,128)(2,1)S(1)}, u32[]{:S(2)}, u32[]{:S(2)}) collective-permute-start(bf16[2,2,2,8,512]{4,3,2,1,0:T(8,128)(2,1)S(1)} %get-tuple-element.12), channel_id=1, source_target_pairs={{0,6},{1,7},{2,4},{3,5},{4,2},{5,3},{6,0},{7,1},{8,14},{9,15},{10,... | collective-permute-start | bytes 196616 | tf_op jit(solution)/shard_map/ppermute | solution.py:190
  114.5 0.0 collective-permute-done.1
  114.5 1.9 %collective-permute-start.4 = (bf16[2,2,2,8,512]{4,3,2,1,0:T(8,128)(2,1)S(1)}, bf16[2,2,2,8,512]{4,3,2,1,0:T(8,128)(2,1)S(1)}, u32[]{:S(2)}, u32[]{:S(2)}) collective-permute-start(bf16[2,2,2,8,512]{4,3,2,1,0:T(8,128)(2,1)S(1)} %get-tuple-element.13), channel_id=1, source_target_pairs={{0,8},{1,9},{2,10},{3,11},{4,12},{5,13},{6,14},{7,15},{8,0},{9,1},... | collective-permute-start | bytes 196616 | tf_op jit(solution)/shard_map/ppermute | solution.py:190
  116.5 0.0 collective-permute-done.2
  116.5 6.0 %collective-permute-start.5 = (bf16[2,2,2,8,512]{4,3,2,1,0:T(8,128)(2,1)S(1)}, bf16[2,2,2,8,512]{4,3,2,1,0:T(8,128)(2,1)S(1)}, u32[]{:S(2)}, u32[]{:S(2)}) collective-permute-start(bf16[2,2,2,8,512]{4,3,2,1,0:T(8,128)(2,1)S(1)} %get-tuple-element.14), channel_id=1, source_target_pairs={{0,10},{1,11},{2,8},{3,9},{4,14},{5,15},{6,12},{7,13},{8,2},{9,3},... | collective-permute-start | bytes 196616 | tf_op jit(solution)/shard_map/ppermute | solution.py:190
  122.5 0.0 collective-permute-done.3
  122.6 0.0 collective-permute-done.4
  122.6 2.1 %collective-permute-done.5 = bf16[2,2,2,8,512]{4,3,2,1,0:T(8,128)(2,1)S(1)} collective-permute-done((bf16[2,2,2,8,512]{4,3,2,1,0:T(8,128)(2,1)S(1)}, bf16[2,2,2,8,512]{4,3,2,1,0:T(8,128)(2,1)S(1)}, u32[]{:S(2)}, u32[]{:S(2)}) %collective-permute-start.5) | collective-permute-done | bytes 65568 | tf_op jit(solution)/shard_map/ppermute | solution.py:190
  124.7 0.0 collective-permute-done.6
  124.7 0.0 collective-permute-done.7
  124.8 24.2 %all-to-all-done.1 = bf16[512,8,128]{2,1,0:T(8,128)(2,1)S(1)} async-done(((bf16[512,8,128]{2,1,0:T(8,128)(2,1)}), bf16[512,8,128]{2,1,0:T(8,128)(2,1)S(1)}, u32[]{:S(2)}, u32[]{:S(2)}) %all-to-all-start.1) | async-done | bytes 1048608 | tf_op jit(solution)/shard_map/all_to_all | solution.py:276
  149.0 2.4 %backward_y.1 = bf16[16,32,512]{2,1,0:T(8,128)(2,1)S(1)} custom-call(s32[2]{0:T(128)S(1)} %pad_add_fusion.place_ref, bf16[32,8,16,128]{3,2,1,0:T(8,128)(2,1)S(1)} %bitcast.52, bf16[8,2,2,2,8,512]{5,4,3,2,1,0:T(8,128)(2,1)S(1)} %bitcast_dynamic-update-slice_fusion.maps_ref, bf16[512,512]{1,0:T(8,128)(2,1)S(1)} %copy-done.2, bf16[512,512]{1,0:T(8,128)(2,1)S(1)} %copy-done.1), custom_call_target="tpu_custom_call" | custom-call | flops 1073741824 | bytes 3145728 | tf_op jit(solution)/shard_map/backward_y/pallas_call | solution.py:249
  151.4 14.2 %all_to_all.15 = bf16[16,32,512]{2,1,0:T(8,128)(2,1)S(1)} all-to-all(bf16[16,32,512]{2,1,0:T(8,128)(2,1)S(1)} %backward_y.1), channel_id=1, replica_groups=mesh['slab'=32,'coil'=16] {'coil'}, dimensions={0} | all-to-all | bytes 1048576 | tf_op jit(solution)/shard_map/all_to_all | solution.py:286
  165.7 1.1 copy_bitcast_fusion
  (15 shorter events, 0.2 us)
Async XLA Ops:
  0.0 22.7 %copy-start.4 = (s32[2,16,4]{1,2,0:T(4,128)S(1)}, s32[2,16,4]{1,2,0:T(4,128)}, u32[]{:S(2)}) copy-start(s32[2,16,4]{1,2,0:T(4,128)} %param.9) | copy-start | bytes 1540
  4.0 71.8 %copy-start = (bf16[2,2,8,2,16,512]{5,4,3,2,1,0:T(8,128)(2,1)S(1)}, bf16[2,2,8,2,16,512]{5,4,3,2,1,0:T(8,128)(2,1)}, u32[]{:S(2)}) copy-start(bf16[2,2,8,2,16,512]{5,4,3,2,1,0:T(8,128)(2,1)} %measured_ref.1) | copy-start | bytes 3145732
  4.0 71.8 %copy-start.1 = (bf16[512,512]{1,0:T(8,128)(2,1)S(1)}, bf16[512,512]{1,0:T(8,128)(2,1)}, u32[]{:S(2)}) copy-start(bf16[512,512]{1,0:T(8,128)(2,1)} %constant.70.clone.sin_ref) | copy-start | bytes 1572868
  4.0 71.8 %copy-start.2 = (bf16[512,512]{1,0:T(8,128)(2,1)S(1)}, bf16[512,512]{1,0:T(8,128)(2,1)}, u32[]{:S(2)}) copy-start(bf16[512,512]{1,0:T(8,128)(2,1)} %constant.69.clone.cos_ref) | copy-start | bytes 1572868
  4.0 71.8 %all-to-all-start = ((bf16[32,16,1024]{2,1,0:T(8,128)(2,1)}), bf16[32,16,1024]{2,1,0:T(8,128)(2,1)S(1)}, u32[]{:S(2)}, u32[]{:S(2)}) async-start(bf16[32,16,1024]{2,1,0:T(8,128)(2,1)} %forward_y.1), calls=%async_computation | async-start | bytes 2097152 | tf_op jit(solution)/shard_map/all_to_all | solution.py:273
  79.3 13.1 %copy-start.3 = (bf16[2,2,8,16,512]{4,3,2,1,0:T(8,128)(2,1)S(1)}, bf16[2,2,8,16,512]{4,3,2,1,0:T(8,128)(2,1)}, u32[]{:S(2)}) copy-start(bf16[2,2,8,16,512]{4,3,2,1,0:T(8,128)(2,1)} %maps_ref.1) | copy-start | bytes 1572868
  79.3 69.7 %all-to-all-start.1 = ((bf16[512,8,128]{2,1,0:T(8,128)(2,1)}), bf16[512,8,128]{2,1,0:T(8,128)(2,1)S(1)}, u32[]{:S(2)}, u32[]{:S(2)}) async-start(bf16[512,8,128]{2,1,0:T(8,128)(2,1)} %bitcast.4), calls=%async_computation.1 | async-start | bytes 2097152 | tf_op jit(solution)/shard_map/all_to_all | solution.py:276
  92.4 7.4 %collective-permute-start = (bf16[2,2,8,8,512]{4,3,1,0,2:T(8,128)(2,1)S(1)}, bf16[2,2,8,8,512]{4,3,1,0,2:T(8,128)(2,1)S(1)}, u32[]{:S(2)}, u32[]{:S(2)}) collective-permute-start(bf16[2,2,8,8,512]{4,3,1,0,2:T(8,128)(2,1)S(1)} %bitcast.62), channel_id=1, source_target_pairs={{0,1},{1,0},{2,3},{3,2},{4,5},{5,4},{6,7},{7,6},{8,9},{9,8},{10,11... | collective-permute-start | bytes 786440 | tf_op jit(solution)/shard_map/ppermute | solution.py:184
  99.8 24.9 %collective-permute-start.6 = (bf16[2,2,2,8,512]{4,3,2,1,0:T(8,128)(2,1)S(1)}, bf16[2,2,2,8,512]{4,3,2,1,0:T(8,128)(2,1)S(1)}, u32[]{:S(2)}, u32[]{:S(2)}) collective-permute-start(bf16[2,2,2,8,512]{4,3,2,1,0:T(8,128)(2,1)S(1)} %fusion.8), channel_id=1, source_target_pairs={{0,12},{1,13},{2,14},{3,15},{4,8},{5,9},{6,10},{7,11},{8,4},{9,5},... | collective-permute-start | bytes 196616 | tf_op jit(solution)/shard_map/ppermute | solution.py:190
  101.8 23.0 %collective-permute-start.7 = (bf16[2,2,2,8,512]{4,3,2,1,0:T(8,128)(2,1)S(1)}, bf16[2,2,2,8,512]{4,3,2,1,0:T(8,128)(2,1)S(1)}, u32[]{:S(2)}, u32[]{:S(2)}) collective-permute-start(bf16[2,2,2,8,512]{4,3,2,1,0:T(8,128)(2,1)S(1)} %get-tuple-element.9), channel_id=1, source_target_pairs={{0,14},{1,15},{2,12},{3,13},{4,10},{5,11},{6,8},{7,9},{8,6},{9,7},... | collective-permute-start | bytes 196616 | tf_op jit(solution)/shard_map/ppermute | solution.py:190
  103.7 10.8 %collective-permute-start.1 = (bf16[2,2,2,8,512]{4,3,2,1,0:T(8,128)(2,1)S(1)}, bf16[2,2,2,8,512]{4,3,2,1,0:T(8,128)(2,1)S(1)}, u32[]{:S(2)}, u32[]{:S(2)}) collective-permute-start(bf16[2,2,2,8,512]{4,3,2,1,0:T(8,128)(2,1)S(1)} %get-tuple-element.10), channel_id=1, source_target_pairs={{0,2},{1,3},{2,0},{3,1},{4,6},{5,7},{6,4},{7,5},{8,10},{9,11},{10,... | collective-permute-start | bytes 196616 | tf_op jit(solution)/shard_map/ppermute | solution.py:190
  109.5 7.0 %collective-permute-start.2 = (bf16[2,2,2,8,512]{4,3,2,1,0:T(8,128)(2,1)S(1)}, bf16[2,2,2,8,512]{4,3,2,1,0:T(8,128)(2,1)S(1)}, u32[]{:S(2)}, u32[]{:S(2)}) collective-permute-start(bf16[2,2,2,8,512]{4,3,2,1,0:T(8,128)(2,1)S(1)} %get-tuple-element.11), channel_id=1, source_target_pairs={{0,4},{1,5},{2,6},{3,7},{4,0},{5,1},{6,2},{7,3},{8,12},{9,13},{10,... | collective-permute-start | bytes 196616 | tf_op jit(solution)/shard_map/ppermute | solution.py:190
  111.4 11.1 %collective-permute-start.3 = (bf16[2,2,2,8,512]{4,3,2,1,0:T(8,128)(2,1)S(1)}, bf16[2,2,2,8,512]{4,3,2,1,0:T(8,128)(2,1)S(1)}, u32[]{:S(2)}, u32[]{:S(2)}) collective-permute-start(bf16[2,2,2,8,512]{4,3,2,1,0:T(8,128)(2,1)S(1)} %get-tuple-element.12), channel_id=1, source_target_pairs={{0,6},{1,7},{2,4},{3,5},{4,2},{5,3},{6,0},{7,1},{8,14},{9,15},{10,... | collective-permute-start | bytes 196616 | tf_op jit(solution)/shard_map/ppermute | solution.py:190
  114.5 8.0 %collective-permute-start.4 = (bf16[2,2,2,8,512]{4,3,2,1,0:T(8,128)(2,1)S(1)}, bf16[2,2,2,8,512]{4,3,2,1,0:T(8,128)(2,1)S(1)}, u32[]{:S(2)}, u32[]{:S(2)}) collective-permute-start(bf16[2,2,2,8,512]{4,3,2,1,0:T(8,128)(2,1)S(1)} %get-tuple-element.13), channel_id=1, source_target_pairs={{0,8},{1,9},{2,10},{3,11},{4,12},{5,13},{6,14},{7,15},{8,0},{9,1},... | collective-permute-start | bytes 196616 | tf_op jit(solution)/shard_map/ppermute | solution.py:190
  116.5 8.2 %collective-permute-start.5 = (bf16[2,2,2,8,512]{4,3,2,1,0:T(8,128)(2,1)S(1)}, bf16[2,2,2,8,512]{4,3,2,1,0:T(8,128)(2,1)S(1)}, u32[]{:S(2)}, u32[]{:S(2)}) collective-permute-start(bf16[2,2,2,8,512]{4,3,2,1,0:T(8,128)(2,1)S(1)} %get-tuple-element.14), channel_id=1, source_target_pairs={{0,10},{1,11},{2,8},{3,9},{4,14},{5,15},{6,12},{7,13},{8,2},{9,3},... | collective-permute-start | bytes 196616 | tf_op jit(solution)/shard_map/ppermute | solution.py:190

commit v4 on v3

--- a/solution.py
+++ b/solution.py
@@ -14,12 +14,46 @@
 VMEM_ALL = 62 * 1024 * 1024
 
 
-def dft_tables(length):
+def dft_tables(length, run):
     indices = np.arange(length)
     angles = (indices[:, None] * indices[None, :] % length) * (2.0 * math.pi / length)
     cosine = (np.cos(angles) / math.sqrt(length)).astype(ml_dtypes.bfloat16)
     sine = (np.sin(angles) / math.sqrt(length)).astype(ml_dtypes.bfloat16)
-    return cosine, sine
+    middle = length // 2
+    turned = indices.reshape(-1, run).copy()
+    turned[middle // run :] = turned[middle // run :, ::-1]
+    turned = turned.reshape(-1)
+    half_cos = cosine[:, :middle]
+    half_sin = sine[:, :middle].copy()
+    half_sin[:, 0] = cosine[:, middle]
+    tables = (
+        np.concatenate([half_cos, half_sin]),
+        np.concatenate([half_cos.T, half_sin.T]),
+        np.concatenate([cosine[turned], sine[turned]]),
+    )
+    return tuple(np.ascontiguousarray(table) for table in tables)
+
+
+def mirror(values, axis):
+    middle = values.shape[axis] // 2
+    first = lax.slice_in_dim(values, 0, middle + 1, axis=axis)
+    last = lax.slice_in_dim(values, middle + 1, 2 * middle, axis=axis)
+    return lax.concatenate([first, lax.rev(last, (axis,))], axis)
+
+
+def split_ends(by_cos, by_sin, axis):
+    edge = (8, LANES)[axis]
+    cos_edge = lax.slice_in_dim(by_cos, 0, edge, axis=axis)
+    sin_edge = lax.slice_in_dim(by_sin, 0, edge, axis=axis)
+    first = lax.broadcasted_iota(jnp.int32, cos_edge.shape, axis) == 0
+    joined = []
+    for edge_values, values in (
+        (jnp.where(first, sin_edge, cos_edge), by_cos),
+        (jnp.where(first, jnp.zeros_like(sin_edge), sin_edge), by_sin),
+    ):
+        rest = lax.slice_in_dim(values, edge, values.shape[axis], axis=axis)
+        joined.append(jnp.concatenate([edge_values, rest], axis=axis))
+    return joined
 
 
 def swap_runs(blocks, run):
@@ -36,7 +70,7 @@
     return [pltpu.roll(b, lanes - j * run, 1) if j else b for j, b in enumerate(moved)]
 
 
-def forward_y(maps_ref, image_ref, cos_ref, sin_ref, out_ref, lhs):
+def forward_y(maps_ref, image_ref, table_ref, out_ref, lhs):
     _, coils, readout, z_lo, len_y = maps_ref.shape
     frames = image_ref.shape[1]
     steps = lhs.shape[0]
@@ -57,30 +91,55 @@
                     coil_im = map_re * image_im + map_im * image_re
                     lhs[i, row : row + z_lo] = coil_re.astype(jnp.bfloat16)
                     lhs[i, row + half : row + half + z_lo] = coil_im.astype(jnp.bfloat16)
-        by_cos = jnp.dot(lhs[i], cos_ref[...], preferred_element_type=jnp.float32)
-        by_sin = jnp.dot(lhs[i], sin_ref[...], preferred_element_type=jnp.float32)
-        for p, along in enumerate((by_cos[:half] + by_sin[half:], by_cos[half:] - by_sin[:half])):
+        by_cos = jnp.dot(lhs[i], table_ref[:len_y], preferred_element_type=jnp.float32)
+        by_sin = jnp.dot(lhs[i], table_ref[len_y:], preferred_element_type=jnp.float32)
+        middle = by_cos.shape[1]
+        other_cos, by_sin = split_ends(by_cos, by_sin, 1)
+        lower = (by_cos[:half] + by_sin[half:], by_cos[half:] - by_sin[:half])
+        upper = (other_cos[:half] - by_sin[half:], other_cos[half:] + by_sin[:half])
+        final = lax.broadcasted_iota(jnp.int32, (half, LANES), 1) == LANES - 1
+        for p in range(2):
             lane = (2 * i + p) * LANES
-            for t in range(len_y // LANES):
-                block = along[:, t * LANES : (t + 1) * LANES]
+            blocks = [lower[p][:, t * LANES : (t + 1) * LANES] for t in range(middle // LANES)]
+            moved = [
+                pltpu.roll(upper[p][:, t * LANES : (t + 1) * LANES], LANES - 1, 1)
+                for t in range(middle // LANES)
+            ]
+            for t in range(len(moved)):
+                blocks.append(jnp.where(final, moved[(t + 1) % len(moved)], moved[t]))
+            for t, block in enumerate(blocks):
                 block = [block[u * z_lo : (u + 1) * z_lo] for u in range(group)]
                 for u, rows in enumerate(swap_runs(block, run)):
-                    out_ref[t * group + u, :, lane : lane + LANES] = rows.astype(jnp.bfloat16)
-
-
-def z_work(arrived_ref, measured_ref, weight_ref, cos_ref, sin_ref, out_ref, residual):
+                    slab = t * group + u
+                    if t >= len(moved):
+                        slab = out_ref.shape[0] - 1 - (t - len(moved)) * group - u
+                    out_ref[slab, :, lane : lane + LANES] = rows.astype(jnp.bfloat16)
+
+
+def z_work(
+    arrived_ref,
+    measured_ref,
+    weight_ref,
+    columns_ref,
+    rows_ref,
+    out_ref,
+    table,
+    residual,
+    out,
+    leave,
+):
     _, frames, readout, coils, ky_lo, len_z = measured_ref.shape
-    blocks = weight_ref.shape[0]
     width = weight_ref.shape[1]
-    depth = len_z // blocks
+    middle = len_z // 2
     steps = arrived_ref.shape[1] // (2 * width)
     part = readout // steps
     slabs, _, z_lo, _ = out_ref.shape
     for i in range(steps):
-        mid, end = (2 * i + 1) * width, (2 * i + 2) * width
-        arrived = arrived_ref[:, mid - width : end]
-        by_cos = jnp.dot(cos_ref[...], arrived, preferred_element_type=jnp.float32)
-        by_sin = jnp.dot(sin_ref[...], arrived, preferred_element_type=jnp.float32)
+        start, mid, end = 2 * i * width, (2 * i + 1) * width, (2 * i + 2) * width
+        arrived = arrived_ref[:, start:end]
+        by_cos = jnp.dot(rows_ref[:middle], arrived, preferred_element_type=jnp.float32)
+        by_sin = jnp.dot(rows_ref[middle:], arrived, preferred_element_type=jnp.float32)
+        other_cos, by_sin = split_ends(by_cos, by_sin, 0)
         target = []
         for p in range(2):
             lines = [
@@ -89,21 +148,34 @@
                 for f in range(frames)
             ]
             target.append(jnp.concatenate(lines, axis=0).T.astype(jnp.float32))
-        spectrum_re = by_cos[:, :width] + by_sin[:, width:]
-        spectrum_im = by_cos[:, width:] - by_sin[:, :width]
-        for b in range(blocks):
-            rows = slice(b * depth, (b + 1) * depth)
-            weight = weight_ref[b : b + 1, :]
-            resid_re = weight * (spectrum_re[rows] - target[0][rows])
-            resid_im = weight * (spectrum_im[rows] - target[1][rows])
-            residual[rows, mid - width : mid] = resid_re.astype(jnp.bfloat16)
-            residual[rows, mid:end] = resid_im.astype(jnp.bfloat16)
+        for rows, spectrum_re, spectrum_im in (
+            (
+                slice(0, middle),
+                by_cos[:, :width] + by_sin[:, width:],
+                by_cos[:, width:] - by_sin[:, :width],
+            ),
+            (
+                slice(middle, len_z),
+                other_cos[:, :width] - by_sin[:, width:],
+                other_cos[:, width:] + by_sin[:, :width],
+            ),
+        ):
+            weight = weight_ref[rows]
+            residual[rows, start:mid] = (weight * (spectrum_re - target[0][rows])).astype(jnp.bfloat16)
+            residual[rows, mid:end] = (weight * (spectrum_im - target[1][rows])).astype(jnp.bfloat16)
     run = width // part
     lower = lax.broadcasted_iota(jnp.int32, (len_z, width), 1) < run
+    half_cos, half_sin = columns_ref[:len_z], columns_ref[len_z:]
+    other_cos, half_sin = split_ends(half_cos, half_sin, 1)
+    table[:len_z, :middle] = half_cos
+    table[:len_z, middle:] = other_cos
+    table[len_z:, :middle] = half_sin
+    table[len_z:, middle:] = -half_sin
+    copies = []
     for i in range(steps):
         rows = residual[:, 2 * i * width : (2 * i + 2) * width]
-        by_cos = jnp.dot(cos_ref[...], rows, preferred_element_type=jnp.float32)
-        by_sin = jnp.dot(sin_ref[...], rows, preferred_element_type=jnp.float32)
+        by_cos = jnp.dot(table[:len_z], rows, preferred_element_type=jnp.float32)
+        by_sin = jnp.dot(table[len_z:], rows, preferred_element_type=jnp.float32)
         back_re = by_cos[:, :width] - by_sin[:, width:]
         back_im = by_cos[:, width:] + by_sin[:, :width]
         sent = (
@@ -111,10 +183,15 @@
             jnp.where(lower, pltpu.roll(back_re, run, 1), back_im),
         )
         for x in range(part):
-            out_ref[:, i * part + x] = sent[x].reshape(slabs, z_lo, width).astype(jnp.bfloat16)
-
-
-def backward_y(place_ref, returned_ref, maps_ref, cos_ref, sin_ref, out_ref, lhs):
+            out[:, i * part + x] = sent[x].reshape(slabs, z_lo, width).astype(jnp.bfloat16)
+        here = pl.ds(i * part, part)
+        copies.append(pltpu.make_async_copy(out.at[:, here], out_ref.at[:, here], leave.at[i]))
+        copies[-1].start()
+    for copy in copies:
+        copy.wait()
+
+
+def backward_y(place_ref, returned_ref, maps_ref, table_ref, out_ref, lhs):
     chip, core = place_ref[0], place_ref[1]
     _, chips, rows, _ = returned_ref.shape
     _, cores, _, coils, z_part, len_y = maps_ref.shape
@@ -138,8 +215,8 @@
                             lhs[i, row : row + rows, t * LANES : (t + 1) * LANES] = block[
                                 (p * frames + f) * coils + c
                             ].astype(jnp.bfloat16)
-        by_cos = jnp.dot(lhs[i], cos_ref[...], preferred_element_type=jnp.float32)
-        by_sin = jnp.dot(lhs[i], sin_ref[...], preferred_element_type=jnp.float32)
+        by_cos = jnp.dot(lhs[i], table_ref[:len_y], preferred_element_type=jnp.float32)
+        by_sin = jnp.dot(lhs[i], table_ref[len_y:], preferred_element_type=jnp.float32)
         back_re = by_cos[:half] - by_sin[half:]
         back_im = by_cos[half:] + by_sin[:half]
         for q in range(pair):
@@ -192,7 +269,7 @@
     return jnp.stack(pieces)
 
 
-def send_forward(coil_maps, image_estimate, cosine, sine, slabs):
+def send_forward(coil_maps, image_estimate, table, slabs):
     _, frames, readout, z_lo, len_y = image_estimate.shape
     coils = coil_maps.shape[1]
     group = LANES // (len_y // slabs)
@@ -203,16 +280,16 @@
         forward_y,
         "forward_y",
         jax.ShapeDtypeStruct((slabs, z_lo, steps * 2 * LANES), jnp.bfloat16),
-        [pltpu.VMEM] * 4,
+        [pltpu.VMEM] * 3,
         pltpu.VMEM,
         [pltpu.VMEM((steps, 2 * half, len_y), jnp.bfloat16)],
-        8 * steps * half * len_y * len_y,
-        8 * steps * half * len_y + 4 * len_y * len_y,
+        4 * steps * half * len_y * len_y,
+        8 * steps * half * len_y + 2 * len_y * len_y,
         VMEM_ALL,
-    )(coil_maps, image_estimate, cosine, sine)
-
-
-def send_back(arrived, measured, sampled_blocks, cosine, sine):
+    )(coil_maps, image_estimate, table)
+
+
+def send_back(arrived, measured, sampled_blocks, columns, rows):
     slabs, z_lo, lanes = arrived.shape
     _, frames, readout, coils, ky_lo, len_z = measured.shape
     block_count = sampled_blocks.shape[2]
@@ -220,26 +297,26 @@
     part = readout // steps
     weight = jnp.transpose(sampled_blocks.astype(jnp.float32), (2, 0, 1))[:, None, :, None, :]
     weight = jnp.broadcast_to(weight, (block_count, part, frames, coils, ky_lo))
+    weight = jnp.repeat(weight.reshape(block_count, LANES), len_z // block_count, axis=0)
     return call(
         z_work,
         "z_work",
         jax.ShapeDtypeStruct((slabs, readout, z_lo, LANES), jnp.bfloat16),
         [pltpu.VMEM] * 5,
-        pltpu.VMEM,
-        [pltpu.VMEM((len_z, lanes), jnp.bfloat16)],
-        8 * lanes * len_z * len_z,
+        pl.ANY,
+        [
+            pltpu.VMEM((2 * len_z, len_z), jnp.bfloat16),
+            pltpu.VMEM((len_z, lanes), jnp.bfloat16),
+            pltpu.VMEM((slabs, readout, z_lo, LANES), jnp.bfloat16),
+            pltpu.SemaphoreType.DMA((steps,)),
+        ],
+        6 * lanes * len_z * len_z,
         6 * lanes * len_z + 4 * len_z * len_z,
         VMEM_SOME,
-    )(
-        arrived.reshape(len_z, lanes),
-        measured,
-        weight.reshape(block_count, LANES),
-        cosine,
-        sine,
-    )
-
-
-def combine(returned, own_maps, place, cosine, sine):
+    )(arrived.reshape(len_z, lanes), measured, mirror(weight, 0), columns, rows)
+
+
+def combine(returned, own_maps, place, table):
     slabs, chips, z_lo, _ = returned.shape
     _, cores, _, coils, z_part, len_y = own_maps.shape
     frames = LANES // (len_y // slabs * 2 * coils)
@@ -250,16 +327,16 @@
         backward_y,
         "backward_y",
         jax.ShapeDtypeStruct((chips * cores, 2 * frames * z_part, len_y), jnp.bfloat16),
-        [pltpu.SMEM] + [pltpu.VMEM] * 4,
+        [pltpu.SMEM] + [pltpu.VMEM] * 3,
         pltpu.VMEM,
         [pltpu.VMEM((steps, height, len_y), jnp.bfloat16)],
         4 * steps * height * len_y * len_y,
         4 * steps * height * len_y + 4 * len_y * len_y,
         VMEM_SOME,
-    )(place, returned, own_maps, cosine, sine)
-
-
-def shards(image_estimate, coil_maps, measured, sampled_blocks, cosine, sine):
+    )(place, returned, own_maps, table)
+
+
+def shards(image_estimate, coil_maps, measured, sampled_blocks, *tables):
     slabs = lax.axis_size("slab")
     groups = lax.axis_size("coil")
     _, frames, readout, z_lo, len_y = image_estimate.shape
@@ -268,11 +345,16 @@
     me = lax.axis_index("coil")
     place = jnp.stack([me // cores, me % cores]).astype(jnp.int32)
 
-    outgoing = send_forward(coil_maps, image_estimate, cosine, sine, slabs)
-    outgoing, late_maps = lax.optimization_barrier((outgoing, coil_maps))
+    outgoing = send_forward(coil_maps, image_estimate, tables[0], slabs)
+    outgoing, coil_maps, measured, sampled_blocks = lax.optimization_barrier(
+        (outgoing, coil_maps, measured, sampled_blocks)
+    )
     arrived = lax.all_to_all(outgoing, "slab", split_axis=0, concat_axis=0, tiled=True)
-    own_maps = maps_by_readout(late_maps, place)
-    back_z = send_back(arrived, measured, sampled_blocks, cosine, sine)
+    own_maps = maps_by_readout(coil_maps, place)
+    upper = lax.axis_index("slab") >= slabs // 2
+    measured = jnp.where(upper, lax.rev(measured, (4,)), measured)
+    sampled_blocks = jnp.where(upper, lax.rev(sampled_blocks, (1,)), sampled_blocks)
+    back_z = send_back(arrived, mirror(measured, 5), sampled_blocks, *tables[:2])
     returned = lax.all_to_all(
         back_z.reshape(slabs * groups, z_part, LANES),
         ("slab", "coil"),
@@ -281,7 +363,7 @@
         tiled=True,
     )
     total = combine(
-        returned.reshape(slabs, groups // cores, z_lo, LANES), own_maps, place, cosine, sine
+        returned.reshape(slabs, groups // cores, z_lo, LANES), own_maps, place, tables[2]
     )
     whole = lax.all_to_all(total, "coil", split_axis=0, concat_axis=0, tiled=True)
     whole = whole.reshape(readout, cores, 2, frames, z_part, len_y)
@@ -298,17 +380,15 @@
             P(None, "coil", None, "slab", None),
             P(None, None, None, "coil", "slab", None),
             P(None, "slab", None),
-            P(None, None),
-            P(None, None),
+            *[P(None, None)] * 3,
         ),
         out_specs=P(None, None, None, "slab", None),
         check_vma=False,
     )
 
     def run(image_estimate, coil_maps, measured, sampled_blocks):
-        cosine, sine = dft_tables(image_estimate.shape[4])
-        return body(
-            image_estimate, coil_maps, measured, sampled_blocks, jnp.asarray(cosine), jnp.asarray(sine)
-        )
+        slabs, len_y = mesh.shape["slab"], image_estimate.shape[4]
+        tables = [jnp.asarray(table) for table in dft_tables(len_y, len_y // slabs)]
+        return body(image_estimate, coil_maps, measured, sampled_blocks, *tables)
 
     return run

time: 167 us -> 166 us (level)
  waiting for transfers between devices: 80.3 us -> 74.5 us
  local copies, waits for them, and re-layouts: 0.25 us -> 4.04 us
  other arithmetic: 1.25 us -> 3.06 us
    all_to_all x1, waiting for transfers between devices: 53 us -> 47.3 us  [shards(): lax.all_to_all(outgoing, 'slab', split_axis=0, concat_axis=0, tiled=True)]
    concatenate x0 -> x2, other arithmetic: none -> 1.7 us  [mirror(): return lax.concatenate([first, lax.rev(last, (axis,))], axis)]
  transfers between devices with their start and end apart: 10 -> 10, of which waited for: 4 -> 4; matrix products, arithmetic and copies ran while one was open for 0% -> 4% of each run, Pallas kernels for 0% -> 0%
where the time goes in v4:
time: 166 us
  waiting for transfers between devices  74.5 us (45%)
  starting transfers between devices  60.6 us (37%)
  blocking collectives  14.2 us (9%)
  Pallas kernels  8.84 us (5%)
  local copies, waits for them, and re-layouts  4.04 us (2%)
  other arithmetic  3.06 us (2%)
    all_to_all x1, waiting for transfers between devices, shards(): lax.all_to_all(outgoing, 'slab', split_axis=0, concat_axis=0, tiled=True)  47.3 us
    all_to_all x1, waiting for transfers between devices, shards(): lax.all_to_all(back_z.reshape(slabs * groups, z_part, LANES), ('slab', 'c...  24.2 us
    ppermute x7, starting transfers between devices, maps_by_readout(): piece = lax.ppermute(piece, 'coil', [(i, i ^ cores * k) for i in devices])  22.7 us
    all_to_all x1, starting transfers between devices, shards(): lax.all_to_all(outgoing, 'slab', split_axis=0, concat_axis=0, tiled=True)  18.6 us
    all_to_all x1, blocking collectives, shards(): lax.all_to_all(total, 'coil', split_axis=0, concat_axis=0, tiled=True)  14.2 us
    all_to_all x1, starting transfers between devices, shards(): lax.all_to_all(back_z.reshape(slabs * groups, z_part, LANES), ('slab', 'c...  13.1 us
    ppermute x1, starting transfers between devices, maps_by_readout(): got = lax.ppermute(other, 'coil', [(i, i ^ 1) for i in devices])  6.21 us
    pallas_call x1, Pallas kernels, send_forward(): call(forward_y, 'forward_y', jax.ShapeDtypeStruct((slabs, z_lo, steps * 2...  3.71 us
  transfers between devices with their start and end apart: 10, of which 4 were waited for; matrix products, arithmetic and copies ran while one was open for 4% of the time, Pallas kernels for 0%

profile of v4, /device:TPU:1, one launch (start us, length us, event | category | flops | bytes accessed | tf_op | source)
XLA Modules:
  0.0 165.7 jit_solution(14633529650715293327)
XLA Ops:
  0.0 3.7 %forward_y.1 = bf16[32,16,1024]{2,1,0:T(8,128)(2,1)} custom-call(bf16[2,2,8,16,512]{4,3,2,1,0:T(8,128)(2,1)} %maps_ref.1, bf16[2,2,8,16,512]{4,3,2,1,0:T(8,128)(2,1)} %image_ref.1, bf16[1024,256]{1,0:T(8,128)(2,1)} %constant.78.clone.table_ref.columns_ref), custom_call_target="tpu_custom_call" | custom-call | flops 536870912 | bytes 2621440 | tf_op jit(solution)/shard_map/forward_y/pallas_call | solution.py:279
  3.7 0.0 copy-start.3
  3.7 18.6 %all-to-all-start = ((bf16[32,16,1024]{2,1,0:T(8,128)(2,1)}), bf16[32,16,1024]{2,1,0:T(8,128)(2,1)S(1)}, u32[]{:S(2)}, u32[]{:S(2)}) async-start(bf16[32,16,1024]{2,1,0:T(8,128)(2,1)} %forward_y.1), calls=%async_computation | async-start | bytes 2097152 | tf_op jit(solution)/shard_map/all_to_all | solution.py:352
  22.3 0.0 copy-done.3
  22.4 0.7 rev.12
  23.1 0.1 broadcast_select_fusion
  23.2 0.2 slice.17
  23.4 0.0 copy-start.5
  23.4 1.0 slice.16
  24.4 0.0 copy-done.5
  24.4 0.1 rev.14
  24.6 0.1 reshape.31
  24.7 0.5 reverse
  25.2 1.1 slice.20
  26.3 0.2 rev.15
  26.5 0.0 copy-start
  26.5 0.0 copy-start.2
  26.5 1.7 %pad_maximum_fusion.measured_ref = bf16[2,2,8,2,16,512]{5,4,3,2,1,0:T(8,128)(2,1)S(1)} fusion(bf16[2,2,8,2,16,255]{5,4,3,2,1,0:T(8,128)(2,1)} %slice.20, bf16[2,2,8,2,16,257]{5,4,3,2,1,0:T(8,128)(2,1)} %slice.16), kind=kLoop, calls=%fused_computation | loop fusion | flops 2097152 | bytes 2097152 | tf_op jit(solution)/shard_map/concatenate | solution.py:41
  28.2 47.3 %all-to-all-done = bf16[32,16,1024]{2,1,0:T(8,128)(2,1)S(1)} async-done(((bf16[32,16,1024]{2,1,0:T(8,128)(2,1)}), bf16[32,16,1024]{2,1,0:T(8,128)(2,1)S(1)}, u32[]{:S(2)}, u32[]{:S(2)}) %all-to-all-start) | async-done | bytes 1048608 | tf_op jit(solution)/shard_map/all_to_all | solution.py:352
  75.5 0.0 copy-done
  75.5 0.0 copy-done.2
  75.5 2.7 %z_work.1 = bf16[32,8,16,128]{3,2,1,0:T(8,128)(2,1)} custom-call(bf16[512,1024]{1,0:T(8,128)(2,1)S(1)} %bitcast.55, bf16[2,2,8,2,16,512]{5,4,3,2,1,0:T(8,128)(2,1)S(1)} %pad_maximum_fusion.measured_ref, f32[512,128]{1,0:T(8,128)S(1)} %pad_maximum_fusion.1.weight_ref, bf16[1024,256]{1,0:T(8,128)(2,1)S(1)} %copy-done, bf16[512,512]{1,0:T(8,128)(2,1)S(1)} %copy-done.2), custom_call_target="tpu_custom_call" | custom-call | flops 1610612736 | bytes 4194304 | tf_op jit(solution)/shard_map/z_work/pallas_call | solution.py:301
  78.2 0.0 copy-start.4
  78.2 13.1 %all-to-all-start.1 = ((bf16[512,8,128]{2,1,0:T(8,128)(2,1)}), bf16[512,8,128]{2,1,0:T(8,128)(2,1)S(1)}, u32[]{:S(2)}, u32[]{:S(2)}) async-start(bf16[512,8,128]{2,1,0:T(8,128)(2,1)} %bitcast.5), calls=%async_computation.1 | async-start | bytes 2097152 | tf_op jit(solution)/shard_map/all_to_all | solution.py:358
  91.3 0.0 copy-done.4
  91.4 6.2 %collective-permute-start = (bf16[2,2,8,8,512]{4,3,1,0,2:T(8,128)(2,1)S(1)}, bf16[2,2,8,8,512]{4,3,1,0,2:T(8,128)(2,1)S(1)}, u32[]{:S(2)}, u32[]{:S(2)}) collective-permute-start(bf16[2,2,8,8,512]{4,3,1,0,2:T(8,128)(2,1)S(1)} %bitcast.67), channel_id=1, source_target_pairs={{0,1},{1,0},{2,3},{3,2},{4,5},{5,4},{6,7},{7,6},{8,9},{9,8},{10,11... | collective-permute-start | bytes 786440 | tf_op jit(solution)/shard_map/ppermute | solution.py:261
  97.7 0.1 pad_add_fusion.place_ref
  97.8 0.9 collective-permute-done
  98.8 1.9 %collective-permute-start.1 = (bf16[2,2,2,8,512]{4,3,2,1,0:T(8,128)(2,1)S(1)}, bf16[2,2,2,8,512]{4,3,2,1,0:T(8,128)(2,1)S(1)}, u32[]{:S(2)}, u32[]{:S(2)}) collective-permute-start(bf16[2,2,2,8,512]{4,3,2,1,0:T(8,128)(2,1)S(1)} %get-tuple-element.14), channel_id=1, source_target_pairs={{0,2},{1,3},{2,0},{3,1},{4,6},{5,7},{6,4},{7,5},{8,10},{9,11},{10,... | collective-permute-start | bytes 196616 | tf_op jit(solution)/shard_map/ppermute | solution.py:267
  100.7 1.9 %collective-permute-start.2 = (bf16[2,2,2,8,512]{4,3,2,1,0:T(8,128)(2,1)S(1)}, bf16[2,2,2,8,512]{4,3,2,1,0:T(8,128)(2,1)S(1)}, u32[]{:S(2)}, u32[]{:S(2)}) collective-permute-start(bf16[2,2,2,8,512]{4,3,2,1,0:T(8,128)(2,1)S(1)} %get-tuple-element.15), channel_id=1, source_target_pairs={{0,4},{1,5},{2,6},{3,7},{4,0},{5,1},{6,2},{7,3},{8,12},{9,13},{10,... | collective-permute-start | bytes 196616 | tf_op jit(solution)/shard_map/ppermute | solution.py:267
  102.6 4.5 %collective-permute-start.3 = (bf16[2,2,2,8,512]{4,3,2,1,0:T(8,128)(2,1)S(1)}, bf16[2,2,2,8,512]{4,3,2,1,0:T(8,128)(2,1)S(1)}, u32[]{:S(2)}, u32[]{:S(2)}) collective-permute-start(bf16[2,2,2,8,512]{4,3,2,1,0:T(8,128)(2,1)S(1)} %get-tuple-element.16), channel_id=1, source_target_pairs={{0,6},{1,7},{2,4},{3,5},{4,2},{5,3},{6,0},{7,1},{8,14},{9,15},{10,... | collective-permute-start | bytes 196616 | tf_op jit(solution)/shard_map/ppermute | solution.py:267
  107.2 1.9 %collective-permute-start.4 = (bf16[2,2,2,8,512]{4,3,2,1,0:T(8,128)(2,1)S(1)}, bf16[2,2,2,8,512]{4,3,2,1,0:T(8,128)(2,1)S(1)}, u32[]{:S(2)}, u32[]{:S(2)}) collective-permute-start(bf16[2,2,2,8,512]{4,3,2,1,0:T(8,128)(2,1)S(1)} %get-tuple-element.17), channel_id=1, source_target_pairs={{0,8},{1,9},{2,10},{3,11},{4,12},{5,13},{6,14},{7,15},{8,0},{9,1},... | collective-permute-start | bytes 196616 | tf_op jit(solution)/shard_map/ppermute | solution.py:267
  109.1 0.0 copy-start.1
  109.1 4.7 %collective-permute-start.5 = (bf16[2,2,2,8,512]{4,3,2,1,0:T(8,128)(2,1)S(1)}, bf16[2,2,2,8,512]{4,3,2,1,0:T(8,128)(2,1)S(1)}, u32[]{:S(2)}, u32[]{:S(2)}) collective-permute-start(bf16[2,2,2,8,512]{4,3,2,1,0:T(8,128)(2,1)S(1)} %get-tuple-element.18), channel_id=1, source_target_pairs={{0,10},{1,11},{2,8},{3,9},{4,14},{5,15},{6,12},{7,13},{8,2},{9,3},... | collective-permute-start | bytes 196616 | tf_op jit(solution)/shard_map/ppermute | solution.py:267
  113.9 0.0 collective-permute-done.1
  113.9 1.9 %collective-permute-start.6 = (bf16[2,2,2,8,512]{4,3,2,1,0:T(8,128)(2,1)S(1)}, bf16[2,2,2,8,512]{4,3,2,1,0:T(8,128)(2,1)S(1)}, u32[]{:S(2)}, u32[]{:S(2)}) collective-permute-start(bf16[2,2,2,8,512]{4,3,2,1,0:T(8,128)(2,1)S(1)} %fusion.8), channel_id=1, source_target_pairs={{0,12},{1,13},{2,14},{3,15},{4,8},{5,9},{6,10},{7,11},{8,4},{9,5},... | collective-permute-start | bytes 196616 | tf_op jit(solution)/shard_map/ppermute | solution.py:267
  115.8 0.0 collective-permute-done.2
  115.8 5.7 %collective-permute-start.7 = (bf16[2,2,2,8,512]{4,3,2,1,0:T(8,128)(2,1)S(1)}, bf16[2,2,2,8,512]{4,3,2,1,0:T(8,128)(2,1)S(1)}, u32[]{:S(2)}, u32[]{:S(2)}) collective-permute-start(bf16[2,2,2,8,512]{4,3,2,1,0:T(8,128)(2,1)S(1)} %get-tuple-element.13), channel_id=1, source_target_pairs={{0,14},{1,15},{2,12},{3,13},{4,10},{5,11},{6,8},{7,9},{8,6},{9,7},... | collective-permute-start | bytes 196616 | tf_op jit(solution)/shard_map/ppermute | solution.py:267
  121.6 0.0 collective-permute-done.3
  121.6 0.0 collective-permute-done.4
  121.7 0.0 collective-permute-done.5
  121.7 0.0 collective-permute-done.6
  121.7 2.0 %collective-permute-done.7 = bf16[2,2,2,8,512]{4,3,2,1,0:T(8,128)(2,1)S(1)} collective-permute-done((bf16[2,2,2,8,512]{4,3,2,1,0:T(8,128)(2,1)S(1)}, bf16[2,2,2,8,512]{4,3,2,1,0:T(8,128)(2,1)S(1)}, u32[]{:S(2)}, u32[]{:S(2)}) %collective-permute-start.7) | collective-permute-done | bytes 65568 | tf_op jit(solution)/shard_map/ppermute | solution.py:267
  123.7 24.2 %all-to-all-done.1 = bf16[512,8,128]{2,1,0:T(8,128)(2,1)S(1)} async-done(((bf16[512,8,128]{2,1,0:T(8,128)(2,1)}), bf16[512,8,128]{2,1,0:T(8,128)(2,1)S(1)}, u32[]{:S(2)}, u32[]{:S(2)}) %all-to-all-start.1) | async-done | bytes 1048608 | tf_op jit(solution)/shard_map/all_to_all | solution.py:358
  147.9 0.0 copy-done.1
  147.9 2.4 %backward_y.1 = bf16[16,32,512]{2,1,0:T(8,128)(2,1)S(1)} custom-call(s32[2]{0:T(128)S(1)} %pad_add_fusion.place_ref, bf16[32,8,16,128]{3,2,1,0:T(8,128)(2,1)S(1)} %bitcast.54, bf16[8,2,2,2,8,512]{5,4,3,2,1,0:T(8,128)(2,1)S(1)} %bitcast_dynamic-update-slice_fusion.maps_ref, bf16[1024,512]{1,0:T(8,128)(2,1)S(1)} %copy-done.1), custom_call_target="tpu_custom_call" | custom-call | flops 1073741824 | bytes 3145728 | tf_op jit(solution)/shard_map/backward_y/pallas_call | solution.py:326
  150.4 14.2 %all_to_all.15 = bf16[16,32,512]{2,1,0:T(8,128)(2,1)S(1)} all-to-all(bf16[16,32,512]{2,1,0:T(8,128)(2,1)S(1)} %backward_y.1), channel_id=1, replica_groups=mesh['slab'=32,'coil'=16] {'coil'}, dimensions={0} | all-to-all | bytes 1048576 | tf_op jit(solution)/shard_map/all_to_all | solution.py:368
  164.6 1.1 copy_bitcast_fusion
  (20 shorter events, 0.3 us)
Async XLA Ops:
  3.7 18.6 %copy-start.3 = (bf16[2,2,8,2,16,512]{5,4,3,2,1,0:T(8,128)(2,1)S(1)}, bf16[2,2,8,2,16,512]{5,4,3,2,1,0:T(8,128)(2,1)}, u32[]{:S(2)}) copy-start(bf16[2,2,8,2,16,512]{5,4,3,2,1,0:T(8,128)(2,1)} %param.9) | copy-start | bytes 3145732
  3.7 71.8 %all-to-all-start = ((bf16[32,16,1024]{2,1,0:T(8,128)(2,1)}), bf16[32,16,1024]{2,1,0:T(8,128)(2,1)S(1)}, u32[]{:S(2)}, u32[]{:S(2)}) async-start(bf16[32,16,1024]{2,1,0:T(8,128)(2,1)} %forward_y.1), calls=%async_computation | async-start | bytes 2097152 | tf_op jit(solution)/shard_map/all_to_all | solution.py:352
  23.4 1.0 copy-start.5
  26.5 49.0 %copy-start = (bf16[1024,256]{1,0:T(8,128)(2,1)S(1)}, bf16[1024,256]{1,0:T(8,128)(2,1)}, u32[]{:S(2)}) copy-start(bf16[1024,256]{1,0:T(8,128)(2,1)} %constant.78.clone.table_ref.columns_ref) | copy-start | bytes 1572868
  26.5 49.0 %copy-start.2 = (bf16[512,512]{1,0:T(8,128)(2,1)S(1)}, bf16[512,512]{1,0:T(8,128)(2,1)}, u32[]{:S(2)}) copy-start(bf16[512,512]{1,0:T(8,128)(2,1)} %constant.79.clone.rows_ref) | copy-start | bytes 1572868
  78.2 13.1 %copy-start.4 = (bf16[2,2,8,16,512]{4,3,2,1,0:T(8,128)(2,1)S(1)}, bf16[2,2,8,16,512]{4,3,2,1,0:T(8,128)(2,1)}, u32[]{:S(2)}) copy-start(bf16[2,2,8,16,512]{4,3,2,1,0:T(8,128)(2,1)} %maps_ref.1) | copy-start | bytes 1572868
  78.2 69.7 %all-to-all-start.1 = ((bf16[512,8,128]{2,1,0:T(8,128)(2,1)}), bf16[512,8,128]{2,1,0:T(8,128)(2,1)S(1)}, u32[]{:S(2)}, u32[]{:S(2)}) async-start(bf16[512,8,128]{2,1,0:T(8,128)(2,1)} %bitcast.5), calls=%async_computation.1 | async-start | bytes 2097152 | tf_op jit(solution)/shard_map/all_to_all | solution.py:358
  91.4 7.4 %collective-permute-start = (bf16[2,2,8,8,512]{4,3,1,0,2:T(8,128)(2,1)S(1)}, bf16[2,2,8,8,512]{4,3,1,0,2:T(8,128)(2,1)S(1)}, u32[]{:S(2)}, u32[]{:S(2)}) collective-permute-start(bf16[2,2,8,8,512]{4,3,1,0,2:T(8,128)(2,1)S(1)} %bitcast.67), channel_id=1, source_target_pairs={{0,1},{1,0},{2,3},{3,2},{4,5},{5,4},{6,7},{7,6},{8,9},{9,8},{10,11... | collective-permute-start | bytes 786440 | tf_op jit(solution)/shard_map/ppermute | solution.py:261
  98.8 15.1 %collective-permute-start.1 = (bf16[2,2,2,8,512]{4,3,2,1,0:T(8,128)(2,1)S(1)}, bf16[2,2,2,8,512]{4,3,2,1,0:T(8,128)(2,1)S(1)}, u32[]{:S(2)}, u32[]{:S(2)}) collective-permute-start(bf16[2,2,2,8,512]{4,3,2,1,0:T(8,128)(2,1)S(1)} %get-tuple-element.14), channel_id=1, source_target_pairs={{0,2},{1,3},{2,0},{3,1},{4,6},{5,7},{6,4},{7,5},{8,10},{9,11},{10,... | collective-permute-start | bytes 196616 | tf_op jit(solution)/shard_map/ppermute | solution.py:267
  100.7 15.1 %collective-permute-start.2 = (bf16[2,2,2,8,512]{4,3,2,1,0:T(8,128)(2,1)S(1)}, bf16[2,2,2,8,512]{4,3,2,1,0:T(8,128)(2,1)S(1)}, u32[]{:S(2)}, u32[]{:S(2)}) collective-permute-start(bf16[2,2,2,8,512]{4,3,2,1,0:T(8,128)(2,1)S(1)} %get-tuple-element.15), channel_id=1, source_target_pairs={{0,4},{1,5},{2,6},{3,7},{4,0},{5,1},{6,2},{7,3},{8,12},{9,13},{10,... | collective-permute-start | bytes 196616 | tf_op jit(solution)/shard_map/ppermute | solution.py:267
  102.6 19.0 %collective-permute-start.3 = (bf16[2,2,2,8,512]{4,3,2,1,0:T(8,128)(2,1)S(1)}, bf16[2,2,2,8,512]{4,3,2,1,0:T(8,128)(2,1)S(1)}, u32[]{:S(2)}, u32[]{:S(2)}) collective-permute-start(bf16[2,2,2,8,512]{4,3,2,1,0:T(8,128)(2,1)S(1)} %get-tuple-element.16), channel_id=1, source_target_pairs={{0,6},{1,7},{2,4},{3,5},{4,2},{5,3},{6,0},{7,1},{8,14},{9,15},{10,... | collective-permute-start | bytes 196616 | tf_op jit(solution)/shard_map/ppermute | solution.py:267
  107.2 14.5 %collective-permute-start.4 = (bf16[2,2,2,8,512]{4,3,2,1,0:T(8,128)(2,1)S(1)}, bf16[2,2,2,8,512]{4,3,2,1,0:T(8,128)(2,1)S(1)}, u32[]{:S(2)}, u32[]{:S(2)}) collective-permute-start(bf16[2,2,2,8,512]{4,3,2,1,0:T(8,128)(2,1)S(1)} %get-tuple-element.17), channel_id=1, source_target_pairs={{0,8},{1,9},{2,10},{3,11},{4,12},{5,13},{6,14},{7,15},{8,0},{9,1},... | collective-permute-start | bytes 196616 | tf_op jit(solution)/shard_map/ppermute | solution.py:267
  109.1 38.8 %copy-start.1 = (bf16[1024,512]{1,0:T(8,128)(2,1)S(1)}, bf16[1024,512]{1,0:T(8,128)(2,1)}, u32[]{:S(2)}) copy-start(bf16[1024,512]{1,0:T(8,128)(2,1)} %constant.80.clone.table_ref) | copy-start | bytes 3145732
  109.1 12.6 %collective-permute-start.5 = (bf16[2,2,2,8,512]{4,3,2,1,0:T(8,128)(2,1)S(1)}, bf16[2,2,2,8,512]{4,3,2,1,0:T(8,128)(2,1)S(1)}, u32[]{:S(2)}, u32[]{:S(2)}) collective-permute-start(bf16[2,2,2,8,512]{4,3,2,1,0:T(8,128)(2,1)S(1)} %get-tuple-element.18), channel_id=1, source_target_pairs={{0,10},{1,11},{2,8},{3,9},{4,14},{5,15},{6,12},{7,13},{8,2},{9,3},... | collective-permute-start | bytes 196616 | tf_op jit(solution)/shard_map/ppermute | solution.py:267
  113.9 7.8 %collective-permute-start.6 = (bf16[2,2,2,8,512]{4,3,2,1,0:T(8,128)(2,1)S(1)}, bf16[2,2,2,8,512]{4,3,2,1,0:T(8,128)(2,1)S(1)}, u32[]{:S(2)}, u32[]{:S(2)}) collective-permute-start(bf16[2,2,2,8,512]{4,3,2,1,0:T(8,128)(2,1)S(1)} %fusion.8), channel_id=1, source_target_pairs={{0,12},{1,13},{2,14},{3,15},{4,8},{5,9},{6,10},{7,11},{8,4},{9,5},... | collective-permute-start | bytes 196616 | tf_op jit(solution)/shard_map/ppermute | solution.py:267
  115.8 7.9 %collective-permute-start.7 = (bf16[2,2,2,8,512]{4,3,2,1,0:T(8,128)(2,1)S(1)}, bf16[2,2,2,8,512]{4,3,2,1,0:T(8,128)(2,1)S(1)}, u32[]{:S(2)}, u32[]{:S(2)}) collective-permute-start(bf16[2,2,2,8,512]{4,3,2,1,0:T(8,128)(2,1)S(1)} %get-tuple-element.13), channel_id=1, source_target_pairs={{0,14},{1,15},{2,12},{3,13},{4,10},{5,11},{6,8},{7,9},{8,6},{9,7},... | collective-permute-start | bytes 196616 | tf_op jit(solution)/shard_map/ppermute | solution.py:267

commit v5 on v4

--- a/solution.py
+++ b/solution.py
@@ -70,7 +70,9 @@
     return [pltpu.roll(b, lanes - j * run, 1) if j else b for j, b in enumerate(moved)]
 
 
-def forward_y(maps_ref, image_ref, table_ref, out_ref, lhs):
+def forward_y(
+    maps_ref, image_ref, table_ref, out_ref, maps, image, table, lhs, out, arrive, leave
+):
     _, coils, readout, z_lo, len_y = maps_ref.shape
     frames = image_ref.shape[1]
     steps = lhs.shape[0]
@@ -78,28 +80,39 @@
     group = part * frames * coils
     half = group * z_lo
     run = LANES // group
+    inputs = [
+        pltpu.make_async_copy(source, held, arrive.at[k])
+        for k, (source, held) in enumerate(((maps_ref, maps), (image_ref, image), (table_ref, table)))
+    ]
+    for copy in inputs:
+        copy.start()
+    inputs[0].wait()
+    inputs[1].wait()
     for i in range(steps):
         for x in range(part):
             for f in range(frames):
-                image_re = image_ref[0, f, i * part + x].astype(jnp.float32)
-                image_im = image_ref[1, f, i * part + x].astype(jnp.float32)
+                image_re = image[0, f, i * part + x].astype(jnp.float32)
+                image_im = image[1, f, i * part + x].astype(jnp.float32)
                 for c in range(coils):
-                    map_re = maps_ref[0, c, i * part + x].astype(jnp.float32)
-                    map_im = maps_ref[1, c, i * part + x].astype(jnp.float32)
+                    map_re = maps[0, c, i * part + x].astype(jnp.float32)
+                    map_im = maps[1, c, i * part + x].astype(jnp.float32)
                     row = ((x * frames + f) * coils + c) * z_lo
                     coil_re = map_re * image_re - map_im * image_im
                     coil_im = map_re * image_im + map_im * image_re
                     lhs[i, row : row + z_lo] = coil_re.astype(jnp.bfloat16)
                     lhs[i, row + half : row + half + z_lo] = coil_im.astype(jnp.bfloat16)
-        by_cos = jnp.dot(lhs[i], table_ref[:len_y], preferred_element_type=jnp.float32)
-        by_sin = jnp.dot(lhs[i], table_ref[len_y:], preferred_element_type=jnp.float32)
+    inputs[2].wait()
+    results = []
+    for i in range(steps):
+        by_cos = jnp.dot(lhs[i], table[:len_y], preferred_element_type=jnp.float32)
+        by_sin = jnp.dot(lhs[i], table[len_y:], preferred_element_type=jnp.float32)
         middle = by_cos.shape[1]
         other_cos, by_sin = split_ends(by_cos, by_sin, 1)
         lower = (by_cos[:half] + by_sin[half:], by_cos[half:] - by_sin[:half])
         upper = (other_cos[:half] - by_sin[half:], other_cos[half:] + by_sin[:half])
         final = lax.broadcasted_iota(jnp.int32, (half, LANES), 1) == LANES - 1
         for p in range(2):
-            lane = (2 * i + p) * LANES
+            lane = p * LANES
             blocks = [lower[p][:, t * LANES : (t + 1) * LANES] for t in range(middle // LANES)]
             moved = [
                 pltpu.roll(upper[p][:, t * LANES : (t + 1) * LANES], LANES - 1, 1)
@@ -112,8 +125,13 @@
                 for u, rows in enumerate(swap_runs(block, run)):
                     slab = t * group + u
                     if t >= len(moved):
-                        slab = out_ref.shape[0] - 1 - (t - len(moved)) * group - u
-                    out_ref[slab, :, lane : lane + LANES] = rows.astype(jnp.bfloat16)
+                        slab = out.shape[1] - 1 - (t - len(moved)) * group - u
+                    out[i, slab, :, lane : lane + LANES] = rows.astype(jnp.bfloat16)
+        lanes = pl.ds(2 * i * LANES, 2 * LANES)
+        results.append(pltpu.make_async_copy(out.at[i], out_ref.at[:, :, lanes], leave.at[i]))
+        results[-1].start()
+    for copy in results:
+        copy.wait()
 
 
 def z_work(
@@ -280,9 +298,17 @@
         forward_y,
         "forward_y",
         jax.ShapeDtypeStruct((slabs, z_lo, steps * 2 * LANES), jnp.bfloat16),
-        [pltpu.VMEM] * 3,
-        pltpu.VMEM,
-        [pltpu.VMEM((steps, 2 * half, len_y), jnp.bfloat16)],
+        [pl.ANY] * 3,
+        pl.ANY,
+        [
+            pltpu.VMEM(coil_maps.shape, jnp.bfloat16),
+            pltpu.VMEM(image_estimate.shape, jnp.bfloat16),
+            pltpu.VMEM(table.shape, jnp.bfloat16),
+            pltpu.VMEM((steps, 2 * half, len_y), jnp.bfloat16),
+            pltpu.VMEM((steps, slabs, z_lo, 2 * LANES), jnp.bfloat16),
+            pltpu.SemaphoreType.DMA((3,)),
+            pltpu.SemaphoreType.DMA((steps,)),
+        ],
         4 * steps * half * len_y * len_y,
         8 * steps * half * len_y + 2 * len_y * len_y,
         VMEM_ALL,

time: 166 us -> 166 us (level)
  no operation moved by 1% of the time
where the time goes in v5:
time: 166 us
  waiting for transfers between devices  74.5 us (45%)
  starting transfers between devices  60.6 us (37%)
  blocking collectives  14.3 us (9%)
  Pallas kernels  8.65 us (5%)
  local copies, waits for them, and re-layouts  4.04 us (2%)
  other arithmetic  3.06 us (2%)
    all_to_all x1, waiting for transfers between devices, shards(): lax.all_to_all(outgoing, 'slab', split_axis=0, concat_axis=0, tiled=True)  47.3 us
    all_to_all x1, waiting for transfers between devices, shards(): lax.all_to_all(back_z.reshape(slabs * groups, z_part, LANES), ('slab', 'c...  24.2 us
    ppermute x7, starting transfers between devices, maps_by_readout(): piece = lax.ppermute(piece, 'coil', [(i, i ^ cores * k) for i in devices])  22.7 us
    all_to_all x1, starting transfers between devices, shards(): lax.all_to_all(outgoing, 'slab', split_axis=0, concat_axis=0, tiled=True)  18.6 us
    all_to_all x1, blocking collectives, shards(): lax.all_to_all(total, 'coil', split_axis=0, concat_axis=0, tiled=True)  14.3 us
    all_to_all x1, starting transfers between devices, shards(): lax.all_to_all(back_z.reshape(slabs * groups, z_part, LANES), ('slab', 'c...  13 us
    ppermute x1, starting transfers between devices, maps_by_readout(): got = lax.ppermute(other, 'coil', [(i, i ^ 1) for i in devices])  6.21 us
    pallas_call x1, Pallas kernels, send_forward(): call(forward_y, 'forward_y', jax.ShapeDtypeStruct((slabs, z_lo, steps * 2...  3.53 us
  transfers between devices with their start and end apart: 10, of which 4 were waited for; matrix products, arithmetic and copies ran while one was open for 4% of the time, Pallas kernels for 0%

profile of v5, /device:TPU:1, one launch (start us, length us, event | category | flops | bytes accessed | tf_op | source)
XLA Modules:
  0.0 165.6 jit_solution(14175246550580104422)
XLA Ops:
  0.0 3.5 %forward_y.1 = bf16[32,16,1024]{2,1,0:T(8,128)(2,1)} custom-call(bf16[2,2,8,16,512]{4,3,2,1,0:T(8,128)(2,1)} %maps_ref.1, bf16[2,2,8,16,512]{4,3,2,1,0:T(8,128)(2,1)} %image_ref.1, bf16[1024,256]{1,0:T(8,128)(2,1)} %constant.78.clone.table_ref.columns_ref), custom_call_target="tpu_custom_call" | custom-call | flops 536870912 | bytes 2621440 | tf_op jit(solution)/shard_map/forward_y/pallas_call | solution.py:297
  3.5 0.0 copy-start.3
  3.5 18.6 %all-to-all-start = ((bf16[32,16,1024]{2,1,0:T(8,128)(2,1)}), bf16[32,16,1024]{2,1,0:T(8,128)(2,1)S(1)}, u32[]{:S(2)}, u32[]{:S(2)}) async-start(bf16[32,16,1024]{2,1,0:T(8,128)(2,1)} %forward_y.1), calls=%async_computation | async-start | bytes 2097152 | tf_op jit(solution)/shard_map/all_to_all | solution.py:378
  22.2 0.0 copy-done.3
  22.2 0.7 rev.12
  22.9 0.1 broadcast_select_fusion
  23.0 0.2 slice.17
  23.3 0.0 copy-start.5
  23.3 1.0 slice.16
  24.3 0.0 copy-done.5
  24.3 0.1 rev.14
  24.4 0.1 reshape.31
  24.6 0.5 reverse
  25.1 1.1 slice.20
  26.1 0.2 rev.15
  26.3 0.0 copy-start
  26.3 0.0 copy-start.2
  26.3 1.7 %pad_maximum_fusion.measured_ref = bf16[2,2,8,2,16,512]{5,4,3,2,1,0:T(8,128)(2,1)S(1)} fusion(bf16[2,2,8,2,16,255]{5,4,3,2,1,0:T(8,128)(2,1)} %slice.20, bf16[2,2,8,2,16,257]{5,4,3,2,1,0:T(8,128)(2,1)} %slice.16), kind=kLoop, calls=%fused_computation | loop fusion | flops 2097152 | bytes 2097152 | tf_op jit(solution)/shard_map/concatenate | solution.py:41
  28.0 47.3 %all-to-all-done = bf16[32,16,1024]{2,1,0:T(8,128)(2,1)S(1)} async-done(((bf16[32,16,1024]{2,1,0:T(8,128)(2,1)}), bf16[32,16,1024]{2,1,0:T(8,128)(2,1)S(1)}, u32[]{:S(2)}, u32[]{:S(2)}) %all-to-all-start) | async-done | bytes 1048608 | tf_op jit(solution)/shard_map/all_to_all | solution.py:378
  75.3 0.0 copy-done
  75.3 0.0 copy-done.2
  75.3 2.7 %z_work.1 = bf16[32,8,16,128]{3,2,1,0:T(8,128)(2,1)} custom-call(bf16[512,1024]{1,0:T(8,128)(2,1)S(1)} %bitcast.55, bf16[2,2,8,2,16,512]{5,4,3,2,1,0:T(8,128)(2,1)S(1)} %pad_maximum_fusion.measured_ref, f32[512,128]{1,0:T(8,128)S(1)} %pad_maximum_fusion.1.weight_ref, bf16[1024,256]{1,0:T(8,128)(2,1)S(1)} %copy-done, bf16[512,512]{1,0:T(8,128)(2,1)S(1)} %copy-done.2), custom_call_target="tpu_custom_call" | custom-call | flops 1610612736 | bytes 4194304 | tf_op jit(solution)/shard_map/z_work/pallas_call | solution.py:327
  78.0 0.0 copy-start.4
  78.0 13.0 %all-to-all-start.1 = ((bf16[512,8,128]{2,1,0:T(8,128)(2,1)}), bf16[512,8,128]{2,1,0:T(8,128)(2,1)S(1)}, u32[]{:S(2)}, u32[]{:S(2)}) async-start(bf16[512,8,128]{2,1,0:T(8,128)(2,1)} %bitcast.5), calls=%async_computation.1 | async-start | bytes 2097152 | tf_op jit(solution)/shard_map/all_to_all | solution.py:384
  91.1 0.0 copy-done.4
  91.2 6.2 %collective-permute-start = (bf16[2,2,8,8,512]{4,3,1,0,2:T(8,128)(2,1)S(1)}, bf16[2,2,8,8,512]{4,3,1,0,2:T(8,128)(2,1)S(1)}, u32[]{:S(2)}, u32[]{:S(2)}) collective-permute-start(bf16[2,2,8,8,512]{4,3,1,0,2:T(8,128)(2,1)S(1)} %bitcast.67), channel_id=1, source_target_pairs={{0,1},{1,0},{2,3},{3,2},{4,5},{5,4},{6,7},{7,6},{8,9},{9,8},{10,11... | collective-permute-start | bytes 786440 | tf_op jit(solution)/shard_map/ppermute | solution.py:279
  97.5 0.1 pad_add_fusion.place_ref
  97.6 0.9 collective-permute-done
  98.6 1.9 %collective-permute-start.1 = (bf16[2,2,2,8,512]{4,3,2,1,0:T(8,128)(2,1)S(1)}, bf16[2,2,2,8,512]{4,3,2,1,0:T(8,128)(2,1)S(1)}, u32[]{:S(2)}, u32[]{:S(2)}) collective-permute-start(bf16[2,2,2,8,512]{4,3,2,1,0:T(8,128)(2,1)S(1)} %get-tuple-element.14), channel_id=1, source_target_pairs={{0,2},{1,3},{2,0},{3,1},{4,6},{5,7},{6,4},{7,5},{8,10},{9,11},{10,... | collective-permute-start | bytes 196616 | tf_op jit(solution)/shard_map/ppermute | solution.py:285
  100.5 1.9 %collective-permute-start.2 = (bf16[2,2,2,8,512]{4,3,2,1,0:T(8,128)(2,1)S(1)}, bf16[2,2,2,8,512]{4,3,2,1,0:T(8,128)(2,1)S(1)}, u32[]{:S(2)}, u32[]{:S(2)}) collective-permute-start(bf16[2,2,2,8,512]{4,3,2,1,0:T(8,128)(2,1)S(1)} %get-tuple-element.15), channel_id=1, source_target_pairs={{0,4},{1,5},{2,6},{3,7},{4,0},{5,1},{6,2},{7,3},{8,12},{9,13},{10,... | collective-permute-start | bytes 196616 | tf_op jit(solution)/shard_map/ppermute | solution.py:285
  102.5 4.5 %collective-permute-start.3 = (bf16[2,2,2,8,512]{4,3,2,1,0:T(8,128)(2,1)S(1)}, bf16[2,2,2,8,512]{4,3,2,1,0:T(8,128)(2,1)S(1)}, u32[]{:S(2)}, u32[]{:S(2)}) collective-permute-start(bf16[2,2,2,8,512]{4,3,2,1,0:T(8,128)(2,1)S(1)} %get-tuple-element.16), channel_id=1, source_target_pairs={{0,6},{1,7},{2,4},{3,5},{4,2},{5,3},{6,0},{7,1},{8,14},{9,15},{10,... | collective-permute-start | bytes 196616 | tf_op jit(solution)/shard_map/ppermute | solution.py:285
  107.0 1.9 %collective-permute-start.4 = (bf16[2,2,2,8,512]{4,3,2,1,0:T(8,128)(2,1)S(1)}, bf16[2,2,2,8,512]{4,3,2,1,0:T(8,128)(2,1)S(1)}, u32[]{:S(2)}, u32[]{:S(2)}) collective-permute-start(bf16[2,2,2,8,512]{4,3,2,1,0:T(8,128)(2,1)S(1)} %get-tuple-element.17), channel_id=1, source_target_pairs={{0,8},{1,9},{2,10},{3,11},{4,12},{5,13},{6,14},{7,15},{8,0},{9,1},... | collective-permute-start | bytes 196616 | tf_op jit(solution)/shard_map/ppermute | solution.py:285
  108.9 0.0 copy-start.1
  108.9 4.7 %collective-permute-start.5 = (bf16[2,2,2,8,512]{4,3,2,1,0:T(8,128)(2,1)S(1)}, bf16[2,2,2,8,512]{4,3,2,1,0:T(8,128)(2,1)S(1)}, u32[]{:S(2)}, u32[]{:S(2)}) collective-permute-start(bf16[2,2,2,8,512]{4,3,2,1,0:T(8,128)(2,1)S(1)} %get-tuple-element.18), channel_id=1, source_target_pairs={{0,10},{1,11},{2,8},{3,9},{4,14},{5,15},{6,12},{7,13},{8,2},{9,3},... | collective-permute-start | bytes 196616 | tf_op jit(solution)/shard_map/ppermute | solution.py:285
  113.7 0.0 collective-permute-done.1
  113.7 1.9 %collective-permute-start.6 = (bf16[2,2,2,8,512]{4,3,2,1,0:T(8,128)(2,1)S(1)}, bf16[2,2,2,8,512]{4,3,2,1,0:T(8,128)(2,1)S(1)}, u32[]{:S(2)}, u32[]{:S(2)}) collective-permute-start(bf16[2,2,2,8,512]{4,3,2,1,0:T(8,128)(2,1)S(1)} %fusion.8), channel_id=1, source_target_pairs={{0,12},{1,13},{2,14},{3,15},{4,8},{5,9},{6,10},{7,11},{8,4},{9,5},... | collective-permute-start | bytes 196616 | tf_op jit(solution)/shard_map/ppermute | solution.py:285
  115.7 0.0 collective-permute-done.2
  115.7 5.7 %collective-permute-start.7 = (bf16[2,2,2,8,512]{4,3,2,1,0:T(8,128)(2,1)S(1)}, bf16[2,2,2,8,512]{4,3,2,1,0:T(8,128)(2,1)S(1)}, u32[]{:S(2)}, u32[]{:S(2)}) collective-permute-start(bf16[2,2,2,8,512]{4,3,2,1,0:T(8,128)(2,1)S(1)} %get-tuple-element.13), channel_id=1, source_target_pairs={{0,14},{1,15},{2,12},{3,13},{4,10},{5,11},{6,8},{7,9},{8,6},{9,7},... | collective-permute-start | bytes 196616 | tf_op jit(solution)/shard_map/ppermute | solution.py:285
  121.4 0.0 collective-permute-done.3
  121.5 0.0 collective-permute-done.4
  121.5 0.0 collective-permute-done.5
  121.5 0.0 collective-permute-done.6
  121.6 2.0 %collective-permute-done.7 = bf16[2,2,2,8,512]{4,3,2,1,0:T(8,128)(2,1)S(1)} collective-permute-done((bf16[2,2,2,8,512]{4,3,2,1,0:T(8,128)(2,1)S(1)}, bf16[2,2,2,8,512]{4,3,2,1,0:T(8,128)(2,1)S(1)}, u32[]{:S(2)}, u32[]{:S(2)}) %collective-permute-start.7) | collective-permute-done | bytes 65568 | tf_op jit(solution)/shard_map/ppermute | solution.py:285
  123.6 24.2 %all-to-all-done.1 = bf16[512,8,128]{2,1,0:T(8,128)(2,1)S(1)} async-done(((bf16[512,8,128]{2,1,0:T(8,128)(2,1)}), bf16[512,8,128]{2,1,0:T(8,128)(2,1)S(1)}, u32[]{:S(2)}, u32[]{:S(2)}) %all-to-all-start.1) | async-done | bytes 1048608 | tf_op jit(solution)/shard_map/all_to_all | solution.py:384
  147.8 0.0 copy-done.1
  147.8 2.4 %backward_y.1 = bf16[16,32,512]{2,1,0:T(8,128)(2,1)S(1)} custom-call(s32[2]{0:T(128)S(1)} %pad_add_fusion.place_ref, bf16[32,8,16,128]{3,2,1,0:T(8,128)(2,1)S(1)} %bitcast.54, bf16[8,2,2,2,8,512]{5,4,3,2,1,0:T(8,128)(2,1)S(1)} %bitcast_dynamic-update-slice_fusion.maps_ref, bf16[1024,512]{1,0:T(8,128)(2,1)S(1)} %copy-done.1), custom_call_target="tpu_custom_call" | custom-call | flops 1073741824 | bytes 3145728 | tf_op jit(solution)/shard_map/backward_y/pallas_call | solution.py:352
  150.2 14.3 %all_to_all.15 = bf16[16,32,512]{2,1,0:T(8,128)(2,1)S(1)} all-to-all(bf16[16,32,512]{2,1,0:T(8,128)(2,1)S(1)} %backward_y.1), channel_id=1, replica_groups=mesh['slab'=32,'coil'=16] {'coil'}, dimensions={0} | all-to-all | bytes 1048576 | tf_op jit(solution)/shard_map/all_to_all | solution.py:394
  164.5 1.1 copy_bitcast_fusion
  (20 shorter events, 0.3 us)
Async XLA Ops:
  3.5 18.7 %copy-start.3 = (bf16[2,2,8,2,16,512]{5,4,3,2,1,0:T(8,128)(2,1)S(1)}, bf16[2,2,8,2,16,512]{5,4,3,2,1,0:T(8,128)(2,1)}, u32[]{:S(2)}) copy-start(bf16[2,2,8,2,16,512]{5,4,3,2,1,0:T(8,128)(2,1)} %param.9) | copy-start | bytes 3145732
  3.5 71.8 %all-to-all-start = ((bf16[32,16,1024]{2,1,0:T(8,128)(2,1)}), bf16[32,16,1024]{2,1,0:T(8,128)(2,1)S(1)}, u32[]{:S(2)}, u32[]{:S(2)}) async-start(bf16[32,16,1024]{2,1,0:T(8,128)(2,1)} %forward_y.1), calls=%async_computation | async-start | bytes 2097152 | tf_op jit(solution)/shard_map/all_to_all | solution.py:378
  23.3 1.0 copy-start.5
  26.3 49.0 %copy-start = (bf16[1024,256]{1,0:T(8,128)(2,1)S(1)}, bf16[1024,256]{1,0:T(8,128)(2,1)}, u32[]{:S(2)}) copy-start(bf16[1024,256]{1,0:T(8,128)(2,1)} %constant.78.clone.table_ref.columns_ref) | copy-start | bytes 1572868
  26.3 49.0 %copy-start.2 = (bf16[512,512]{1,0:T(8,128)(2,1)S(1)}, bf16[512,512]{1,0:T(8,128)(2,1)}, u32[]{:S(2)}) copy-start(bf16[512,512]{1,0:T(8,128)(2,1)} %constant.79.clone.rows_ref) | copy-start | bytes 1572868
  78.0 13.1 %copy-start.4 = (bf16[2,2,8,16,512]{4,3,2,1,0:T(8,128)(2,1)S(1)}, bf16[2,2,8,16,512]{4,3,2,1,0:T(8,128)(2,1)}, u32[]{:S(2)}) copy-start(bf16[2,2,8,16,512]{4,3,2,1,0:T(8,128)(2,1)} %maps_ref.1) | copy-start | bytes 1572868
  78.0 69.7 %all-to-all-start.1 = ((bf16[512,8,128]{2,1,0:T(8,128)(2,1)}), bf16[512,8,128]{2,1,0:T(8,128)(2,1)S(1)}, u32[]{:S(2)}, u32[]{:S(2)}) async-start(bf16[512,8,128]{2,1,0:T(8,128)(2,1)} %bitcast.5), calls=%async_computation.1 | async-start | bytes 2097152 | tf_op jit(solution)/shard_map/all_to_all | solution.py:384
  91.2 7.4 %collective-permute-start = (bf16[2,2,8,8,512]{4,3,1,0,2:T(8,128)(2,1)S(1)}, bf16[2,2,8,8,512]{4,3,1,0,2:T(8,128)(2,1)S(1)}, u32[]{:S(2)}, u32[]{:S(2)}) collective-permute-start(bf16[2,2,8,8,512]{4,3,1,0,2:T(8,128)(2,1)S(1)} %bitcast.67), channel_id=1, source_target_pairs={{0,1},{1,0},{2,3},{3,2},{4,5},{5,4},{6,7},{7,6},{8,9},{9,8},{10,11... | collective-permute-start | bytes 786440 | tf_op jit(solution)/shard_map/ppermute | solution.py:279
  98.6 15.1 %collective-permute-start.1 = (bf16[2,2,2,8,512]{4,3,2,1,0:T(8,128)(2,1)S(1)}, bf16[2,2,2,8,512]{4,3,2,1,0:T(8,128)(2,1)S(1)}, u32[]{:S(2)}, u32[]{:S(2)}) collective-permute-start(bf16[2,2,2,8,512]{4,3,2,1,0:T(8,128)(2,1)S(1)} %get-tuple-element.14), channel_id=1, source_target_pairs={{0,2},{1,3},{2,0},{3,1},{4,6},{5,7},{6,4},{7,5},{8,10},{9,11},{10,... | collective-permute-start | bytes 196616 | tf_op jit(solution)/shard_map/ppermute | solution.py:285
  100.5 15.1 %collective-permute-start.2 = (bf16[2,2,2,8,512]{4,3,2,1,0:T(8,128)(2,1)S(1)}, bf16[2,2,2,8,512]{4,3,2,1,0:T(8,128)(2,1)S(1)}, u32[]{:S(2)}, u32[]{:S(2)}) collective-permute-start(bf16[2,2,2,8,512]{4,3,2,1,0:T(8,128)(2,1)S(1)} %get-tuple-element.15), channel_id=1, source_target_pairs={{0,4},{1,5},{2,6},{3,7},{4,0},{5,1},{6,2},{7,3},{8,12},{9,13},{10,... | collective-permute-start | bytes 196616 | tf_op jit(solution)/shard_map/ppermute | solution.py:285
  102.5 19.0 %collective-permute-start.3 = (bf16[2,2,2,8,512]{4,3,2,1,0:T(8,128)(2,1)S(1)}, bf16[2,2,2,8,512]{4,3,2,1,0:T(8,128)(2,1)S(1)}, u32[]{:S(2)}, u32[]{:S(2)}) collective-permute-start(bf16[2,2,2,8,512]{4,3,2,1,0:T(8,128)(2,1)S(1)} %get-tuple-element.16), channel_id=1, source_target_pairs={{0,6},{1,7},{2,4},{3,5},{4,2},{5,3},{6,0},{7,1},{8,14},{9,15},{10,... | collective-permute-start | bytes 196616 | tf_op jit(solution)/shard_map/ppermute | solution.py:285
  107.0 14.5 %collective-permute-start.4 = (bf16[2,2,2,8,512]{4,3,2,1,0:T(8,128)(2,1)S(1)}, bf16[2,2,2,8,512]{4,3,2,1,0:T(8,128)(2,1)S(1)}, u32[]{:S(2)}, u32[]{:S(2)}) collective-permute-start(bf16[2,2,2,8,512]{4,3,2,1,0:T(8,128)(2,1)S(1)} %get-tuple-element.17), channel_id=1, source_target_pairs={{0,8},{1,9},{2,10},{3,11},{4,12},{5,13},{6,14},{7,15},{8,0},{9,1},... | collective-permute-start | bytes 196616 | tf_op jit(solution)/shard_map/ppermute | solution.py:285
  108.9 38.8 %copy-start.1 = (bf16[1024,512]{1,0:T(8,128)(2,1)S(1)}, bf16[1024,512]{1,0:T(8,128)(2,1)}, u32[]{:S(2)}) copy-start(bf16[1024,512]{1,0:T(8,128)(2,1)} %constant.80.clone.table_ref) | copy-start | bytes 3145732
  108.9 12.6 %collective-permute-start.5 = (bf16[2,2,2,8,512]{4,3,2,1,0:T(8,128)(2,1)S(1)}, bf16[2,2,2,8,512]{4,3,2,1,0:T(8,128)(2,1)S(1)}, u32[]{:S(2)}, u32[]{:S(2)}) collective-permute-start(bf16[2,2,2,8,512]{4,3,2,1,0:T(8,128)(2,1)S(1)} %get-tuple-element.18), channel_id=1, source_target_pairs={{0,10},{1,11},{2,8},{3,9},{4,14},{5,15},{6,12},{7,13},{8,2},{9,3},... | collective-permute-start | bytes 196616 | tf_op jit(solution)/shard_map/ppermute | solution.py:285
  113.7 7.8 %collective-permute-start.6 = (bf16[2,2,2,8,512]{4,3,2,1,0:T(8,128)(2,1)S(1)}, bf16[2,2,2,8,512]{4,3,2,1,0:T(8,128)(2,1)S(1)}, u32[]{:S(2)}, u32[]{:S(2)}) collective-permute-start(bf16[2,2,2,8,512]{4,3,2,1,0:T(8,128)(2,1)S(1)} %fusion.8), channel_id=1, source_target_pairs={{0,12},{1,13},{2,14},{3,15},{4,8},{5,9},{6,10},{7,11},{8,4},{9,5},... | collective-permute-start | bytes 196616 | tf_op jit(solution)/shard_map/ppermute | solution.py:285
  115.7 7.9 %collective-permute-start.7 = (bf16[2,2,2,8,512]{4,3,2,1,0:T(8,128)(2,1)S(1)}, bf16[2,2,2,8,512]{4,3,2,1,0:T(8,128)(2,1)S(1)}, u32[]{:S(2)}, u32[]{:S(2)}) collective-permute-start(bf16[2,2,2,8,512]{4,3,2,1,0:T(8,128)(2,1)S(1)} %get-tuple-element.13), channel_id=1, source_target_pairs={{0,14},{1,15},{2,12},{3,13},{4,10},{5,11},{6,8},{7,9},{8,6},{9,7},... | collective-permute-start | bytes 196616 | tf_op jit(solution)/shard_map/ppermute | solution.py:285

commit v6 on v5

--- a/solution.py
+++ b/solution.py
@@ -80,15 +80,19 @@
     group = part * frames * coils
     half = group * z_lo
     run = LANES // group
+    halves = [pl.ds(0, readout // 2), pl.ds(readout // 2, readout // 2)]
     inputs = [
-        pltpu.make_async_copy(source, held, arrive.at[k])
-        for k, (source, held) in enumerate(((maps_ref, maps), (image_ref, image), (table_ref, table)))
+        pltpu.make_async_copy(source.at[:, :, here], held.at[:, :, here], arrive.at[2 * k + n])
+        for k, here in enumerate(halves)
+        for n, (source, held) in enumerate(((maps_ref, maps), (image_ref, image)))
     ]
-    for copy in inputs:
+    fetch_table = pltpu.make_async_copy(table_ref, table, arrive.at[4])
+    for copy in inputs + [fetch_table]:
         copy.start()
-    inputs[0].wait()
-    inputs[1].wait()
     for i in range(steps):
+        if i * 2 % steps == 0:
+            for copy in inputs[4 * i // steps : 4 * i // steps + 2]:
+                copy.wait()
         for x in range(part):
             for f in range(frames):
                 image_re = image[0, f, i * part + x].astype(jnp.float32)
@@ -101,7 +105,7 @@
                     coil_im = map_re * image_im + map_im * image_re
                     lhs[i, row : row + z_lo] = coil_re.astype(jnp.bfloat16)
                     lhs[i, row + half : row + half + z_lo] = coil_im.astype(jnp.bfloat16)
-    inputs[2].wait()
+    fetch_table.wait()
     results = []
     for i in range(steps):
         by_cos = jnp.dot(lhs[i], table[:len_y], preferred_element_type=jnp.float32)
@@ -306,7 +310,7 @@
             pltpu.VMEM(table.shape, jnp.bfloat16),
             pltpu.VMEM((steps, 2 * half, len_y), jnp.bfloat16),
             pltpu.VMEM((steps, slabs, z_lo, 2 * LANES), jnp.bfloat16),
-            pltpu.SemaphoreType.DMA((3,)),
+            pltpu.SemaphoreType.DMA((5,)),
             pltpu.SemaphoreType.DMA((steps,)),
         ],
         4 * steps * half * len_y * len_y,

time: 166 us -> 166 us (level)
  no operation moved by 1% of the time
where the time goes in v6:
time: 166 us; the launch traced here: 165 us
  waiting for transfers between devices  74.5 us (45%)
  starting transfers between devices  60.6 us (37%)
  blocking collectives  14.3 us (9%)
  Pallas kernels  8.55 us (5%)
  local copies, waits for them, and re-layouts  4.04 us (2%)
  other arithmetic  3.06 us (2%)
    all_to_all x1, waiting for transfers between devices, shards(): lax.all_to_all(outgoing, 'slab', split_axis=0, concat_axis=0, tiled=True)  47.3 us
    all_to_all x1, waiting for transfers between devices, shards(): lax.all_to_all(back_z.reshape(slabs * groups, z_part, LANES), ('slab', 'c...  24.2 us
    ppermute x7, starting transfers between devices, maps_by_readout(): piece = lax.ppermute(piece, 'coil', [(i, i ^ cores * k) for i in devices])  22.7 us
    all_to_all x1, starting transfers between devices, shards(): lax.all_to_all(outgoing, 'slab', split_axis=0, concat_axis=0, tiled=True)  18.6 us
    all_to_all x1, blocking collectives, shards(): lax.all_to_all(total, 'coil', split_axis=0, concat_axis=0, tiled=True)  14.3 us
    all_to_all x1, starting transfers between devices, shards(): lax.all_to_all(back_z.reshape(slabs * groups, z_part, LANES), ('slab', 'c...  13.1 us
    ppermute x1, starting transfers between devices, maps_by_readout(): got = lax.ppermute(other, 'coil', [(i, i ^ 1) for i in devices])  6.21 us
    pallas_call x1, Pallas kernels, send_forward(): call(forward_y, 'forward_y', jax.ShapeDtypeStruct((slabs, z_lo, steps * 2...  3.43 us
  transfers between devices with their start and end apart: 10, of which 4 were waited for; matrix products, arithmetic and copies ran while one was open for 4% of the time, Pallas kernels for 0%

profile of v6, /device:TPU:1, one launch (start us, length us, event | category | flops | bytes accessed | tf_op | source)
XLA Modules:
  0.0 165.5 jit_solution(3674201233876587246)
XLA Ops:
  0.0 3.4 %forward_y.1 = bf16[32,16,1024]{2,1,0:T(8,128)(2,1)} custom-call(bf16[2,2,8,16,512]{4,3,2,1,0:T(8,128)(2,1)} %maps_ref.1, bf16[2,2,8,16,512]{4,3,2,1,0:T(8,128)(2,1)} %image_ref.1, bf16[1024,256]{1,0:T(8,128)(2,1)} %constant.78.clone.table_ref.columns_ref), custom_call_target="tpu_custom_call" | custom-call | flops 536870912 | bytes 2621440 | tf_op jit(solution)/shard_map/forward_y/pallas_call | solution.py:301
  3.4 0.0 copy-start.3
  3.4 18.6 %all-to-all-start = ((bf16[32,16,1024]{2,1,0:T(8,128)(2,1)}), bf16[32,16,1024]{2,1,0:T(8,128)(2,1)S(1)}, u32[]{:S(2)}, u32[]{:S(2)}) async-start(bf16[32,16,1024]{2,1,0:T(8,128)(2,1)} %forward_y.1), calls=%async_computation | async-start | bytes 2097152 | tf_op jit(solution)/shard_map/all_to_all | solution.py:382
  22.1 0.0 copy-done.3
  22.1 0.7 rev.12
  22.8 0.1 broadcast_select_fusion
  22.9 0.2 slice.17
  23.2 0.0 copy-start.5
  23.2 1.0 slice.16
  24.2 0.0 copy-done.5
  24.2 0.1 rev.14
  24.3 0.1 reshape.31
  24.5 0.5 reverse
  25.0 1.1 slice.20
  26.0 0.2 rev.15
  26.2 0.0 copy-start
  26.2 0.0 copy-start.2
  26.2 1.7 %pad_maximum_fusion.measured_ref = bf16[2,2,8,2,16,512]{5,4,3,2,1,0:T(8,128)(2,1)S(1)} fusion(bf16[2,2,8,2,16,255]{5,4,3,2,1,0:T(8,128)(2,1)} %slice.20, bf16[2,2,8,2,16,257]{5,4,3,2,1,0:T(8,128)(2,1)} %slice.16), kind=kLoop, calls=%fused_computation | loop fusion | flops 2097152 | bytes 2097152 | tf_op jit(solution)/shard_map/concatenate | solution.py:41
  27.9 47.3 %all-to-all-done = bf16[32,16,1024]{2,1,0:T(8,128)(2,1)S(1)} async-done(((bf16[32,16,1024]{2,1,0:T(8,128)(2,1)}), bf16[32,16,1024]{2,1,0:T(8,128)(2,1)S(1)}, u32[]{:S(2)}, u32[]{:S(2)}) %all-to-all-start) | async-done | bytes 1048608 | tf_op jit(solution)/shard_map/all_to_all | solution.py:382
  75.2 0.0 copy-done
  75.2 0.0 copy-done.2
  75.2 2.7 %z_work.1 = bf16[32,8,16,128]{3,2,1,0:T(8,128)(2,1)} custom-call(bf16[512,1024]{1,0:T(8,128)(2,1)S(1)} %bitcast.55, bf16[2,2,8,2,16,512]{5,4,3,2,1,0:T(8,128)(2,1)S(1)} %pad_maximum_fusion.measured_ref, f32[512,128]{1,0:T(8,128)S(1)} %pad_maximum_fusion.1.weight_ref, bf16[1024,256]{1,0:T(8,128)(2,1)S(1)} %copy-done, bf16[512,512]{1,0:T(8,128)(2,1)S(1)} %copy-done.2), custom_call_target="tpu_custom_call" | custom-call | flops 1610612736 | bytes 4194304 | tf_op jit(solution)/shard_map/z_work/pallas_call | solution.py:331
  77.9 0.0 copy-start.4
  77.9 13.1 %all-to-all-start.1 = ((bf16[512,8,128]{2,1,0:T(8,128)(2,1)}), bf16[512,8,128]{2,1,0:T(8,128)(2,1)S(1)}, u32[]{:S(2)}, u32[]{:S(2)}) async-start(bf16[512,8,128]{2,1,0:T(8,128)(2,1)} %bitcast.5), calls=%async_computation.1 | async-start | bytes 2097152 | tf_op jit(solution)/shard_map/all_to_all | solution.py:388
  91.0 0.0 copy-done.4
  91.1 6.2 %collective-permute-start = (bf16[2,2,8,8,512]{4,3,1,0,2:T(8,128)(2,1)S(1)}, bf16[2,2,8,8,512]{4,3,1,0,2:T(8,128)(2,1)S(1)}, u32[]{:S(2)}, u32[]{:S(2)}) collective-permute-start(bf16[2,2,8,8,512]{4,3,1,0,2:T(8,128)(2,1)S(1)} %bitcast.67), channel_id=1, source_target_pairs={{0,1},{1,0},{2,3},{3,2},{4,5},{5,4},{6,7},{7,6},{8,9},{9,8},{10,11... | collective-permute-start | bytes 786440 | tf_op jit(solution)/shard_map/ppermute | solution.py:283
  97.4 0.1 pad_add_fusion.place_ref
  97.5 0.9 collective-permute-done
  98.5 1.9 %collective-permute-start.1 = (bf16[2,2,2,8,512]{4,3,2,1,0:T(8,128)(2,1)S(1)}, bf16[2,2,2,8,512]{4,3,2,1,0:T(8,128)(2,1)S(1)}, u32[]{:S(2)}, u32[]{:S(2)}) collective-permute-start(bf16[2,2,2,8,512]{4,3,2,1,0:T(8,128)(2,1)S(1)} %get-tuple-element.14), channel_id=1, source_target_pairs={{0,2},{1,3},{2,0},{3,1},{4,6},{5,7},{6,4},{7,5},{8,10},{9,11},{10,... | collective-permute-start | bytes 196616 | tf_op jit(solution)/shard_map/ppermute | solution.py:289
  100.4 1.9 %collective-permute-start.2 = (bf16[2,2,2,8,512]{4,3,2,1,0:T(8,128)(2,1)S(1)}, bf16[2,2,2,8,512]{4,3,2,1,0:T(8,128)(2,1)S(1)}, u32[]{:S(2)}, u32[]{:S(2)}) collective-permute-start(bf16[2,2,2,8,512]{4,3,2,1,0:T(8,128)(2,1)S(1)} %get-tuple-element.15), channel_id=1, source_target_pairs={{0,4},{1,5},{2,6},{3,7},{4,0},{5,1},{6,2},{7,3},{8,12},{9,13},{10,... | collective-permute-start | bytes 196616 | tf_op jit(solution)/shard_map/ppermute | solution.py:289
  102.4 4.5 %collective-permute-start.3 = (bf16[2,2,2,8,512]{4,3,2,1,0:T(8,128)(2,1)S(1)}, bf16[2,2,2,8,512]{4,3,2,1,0:T(8,128)(2,1)S(1)}, u32[]{:S(2)}, u32[]{:S(2)}) collective-permute-start(bf16[2,2,2,8,512]{4,3,2,1,0:T(8,128)(2,1)S(1)} %get-tuple-element.16), channel_id=1, source_target_pairs={{0,6},{1,7},{2,4},{3,5},{4,2},{5,3},{6,0},{7,1},{8,14},{9,15},{10,... | collective-permute-start | bytes 196616 | tf_op jit(solution)/shard_map/ppermute | solution.py:289
  106.9 1.9 %collective-permute-start.4 = (bf16[2,2,2,8,512]{4,3,2,1,0:T(8,128)(2,1)S(1)}, bf16[2,2,2,8,512]{4,3,2,1,0:T(8,128)(2,1)S(1)}, u32[]{:S(2)}, u32[]{:S(2)}) collective-permute-start(bf16[2,2,2,8,512]{4,3,2,1,0:T(8,128)(2,1)S(1)} %get-tuple-element.17), channel_id=1, source_target_pairs={{0,8},{1,9},{2,10},{3,11},{4,12},{5,13},{6,14},{7,15},{8,0},{9,1},... | collective-permute-start | bytes 196616 | tf_op jit(solution)/shard_map/ppermute | solution.py:289
  108.8 0.0 copy-start.1
  108.8 4.7 %collective-permute-start.5 = (bf16[2,2,2,8,512]{4,3,2,1,0:T(8,128)(2,1)S(1)}, bf16[2,2,2,8,512]{4,3,2,1,0:T(8,128)(2,1)S(1)}, u32[]{:S(2)}, u32[]{:S(2)}) collective-permute-start(bf16[2,2,2,8,512]{4,3,2,1,0:T(8,128)(2,1)S(1)} %get-tuple-element.18), channel_id=1, source_target_pairs={{0,10},{1,11},{2,8},{3,9},{4,14},{5,15},{6,12},{7,13},{8,2},{9,3},... | collective-permute-start | bytes 196616 | tf_op jit(solution)/shard_map/ppermute | solution.py:289
  113.6 0.0 collective-permute-done.1
  113.6 1.9 %collective-permute-start.6 = (bf16[2,2,2,8,512]{4,3,2,1,0:T(8,128)(2,1)S(1)}, bf16[2,2,2,8,512]{4,3,2,1,0:T(8,128)(2,1)S(1)}, u32[]{:S(2)}, u32[]{:S(2)}) collective-permute-start(bf16[2,2,2,8,512]{4,3,2,1,0:T(8,128)(2,1)S(1)} %fusion.8), channel_id=1, source_target_pairs={{0,12},{1,13},{2,14},{3,15},{4,8},{5,9},{6,10},{7,11},{8,4},{9,5},... | collective-permute-start | bytes 196616 | tf_op jit(solution)/shard_map/ppermute | solution.py:289
  115.6 0.0 collective-permute-done.2
  115.6 5.7 %collective-permute-start.7 = (bf16[2,2,2,8,512]{4,3,2,1,0:T(8,128)(2,1)S(1)}, bf16[2,2,2,8,512]{4,3,2,1,0:T(8,128)(2,1)S(1)}, u32[]{:S(2)}, u32[]{:S(2)}) collective-permute-start(bf16[2,2,2,8,512]{4,3,2,1,0:T(8,128)(2,1)S(1)} %get-tuple-element.13), channel_id=1, source_target_pairs={{0,14},{1,15},{2,12},{3,13},{4,10},{5,11},{6,8},{7,9},{8,6},{9,7},... | collective-permute-start | bytes 196616 | tf_op jit(solution)/shard_map/ppermute | solution.py:289
  121.3 0.0 collective-permute-done.3
  121.4 0.0 collective-permute-done.4
  121.4 0.0 collective-permute-done.5
  121.4 0.0 collective-permute-done.6
  121.5 2.0 %collective-permute-done.7 = bf16[2,2,2,8,512]{4,3,2,1,0:T(8,128)(2,1)S(1)} collective-permute-done((bf16[2,2,2,8,512]{4,3,2,1,0:T(8,128)(2,1)S(1)}, bf16[2,2,2,8,512]{4,3,2,1,0:T(8,128)(2,1)S(1)}, u32[]{:S(2)}, u32[]{:S(2)}) %collective-permute-start.7) | collective-permute-done | bytes 65568 | tf_op jit(solution)/shard_map/ppermute | solution.py:289
  123.5 24.2 %all-to-all-done.1 = bf16[512,8,128]{2,1,0:T(8,128)(2,1)S(1)} async-done(((bf16[512,8,128]{2,1,0:T(8,128)(2,1)}), bf16[512,8,128]{2,1,0:T(8,128)(2,1)S(1)}, u32[]{:S(2)}, u32[]{:S(2)}) %all-to-all-start.1) | async-done | bytes 1048608 | tf_op jit(solution)/shard_map/all_to_all | solution.py:388
  147.7 0.0 copy-done.1
  147.7 2.4 %backward_y.1 = bf16[16,32,512]{2,1,0:T(8,128)(2,1)S(1)} custom-call(s32[2]{0:T(128)S(1)} %pad_add_fusion.place_ref, bf16[32,8,16,128]{3,2,1,0:T(8,128)(2,1)S(1)} %bitcast.54, bf16[8,2,2,2,8,512]{5,4,3,2,1,0:T(8,128)(2,1)S(1)} %bitcast_dynamic-update-slice_fusion.maps_ref, bf16[1024,512]{1,0:T(8,128)(2,1)S(1)} %copy-done.1), custom_call_target="tpu_custom_call" | custom-call | flops 1073741824 | bytes 3145728 | tf_op jit(solution)/shard_map/backward_y/pallas_call | solution.py:356
  150.1 14.3 %all_to_all.15 = bf16[16,32,512]{2,1,0:T(8,128)(2,1)S(1)} all-to-all(bf16[16,32,512]{2,1,0:T(8,128)(2,1)S(1)} %backward_y.1), channel_id=1, replica_groups=mesh['slab'=32,'coil'=16] {'coil'}, dimensions={0} | all-to-all | bytes 1048576 | tf_op jit(solution)/shard_map/all_to_all | solution.py:398
  164.4 1.1 copy_bitcast_fusion
  (20 shorter events, 0.3 us)
Async XLA Ops:
  3.4 18.7 %copy-start.3 = (bf16[2,2,8,2,16,512]{5,4,3,2,1,0:T(8,128)(2,1)S(1)}, bf16[2,2,8,2,16,512]{5,4,3,2,1,0:T(8,128)(2,1)}, u32[]{:S(2)}) copy-start(bf16[2,2,8,2,16,512]{5,4,3,2,1,0:T(8,128)(2,1)} %param.9) | copy-start | bytes 3145732
  3.4 71.8 %all-to-all-start = ((bf16[32,16,1024]{2,1,0:T(8,128)(2,1)}), bf16[32,16,1024]{2,1,0:T(8,128)(2,1)S(1)}, u32[]{:S(2)}, u32[]{:S(2)}) async-start(bf16[32,16,1024]{2,1,0:T(8,128)(2,1)} %forward_y.1), calls=%async_computation | async-start | bytes 2097152 | tf_op jit(solution)/shard_map/all_to_all | solution.py:382
  23.2 1.0 copy-start.5
  26.2 49.0 %copy-start = (bf16[1024,256]{1,0:T(8,128)(2,1)S(1)}, bf16[1024,256]{1,0:T(8,128)(2,1)}, u32[]{:S(2)}) copy-start(bf16[1024,256]{1,0:T(8,128)(2,1)} %constant.78.clone.table_ref.columns_ref) | copy-start | bytes 1572868
  26.2 49.0 %copy-start.2 = (bf16[512,512]{1,0:T(8,128)(2,1)S(1)}, bf16[512,512]{1,0:T(8,128)(2,1)}, u32[]{:S(2)}) copy-start(bf16[512,512]{1,0:T(8,128)(2,1)} %constant.79.clone.rows_ref) | copy-start | bytes 1572868
  77.9 13.1 %copy-start.4 = (bf16[2,2,8,16,512]{4,3,2,1,0:T(8,128)(2,1)S(1)}, bf16[2,2,8,16,512]{4,3,2,1,0:T(8,128)(2,1)}, u32[]{:S(2)}) copy-start(bf16[2,2,8,16,512]{4,3,2,1,0:T(8,128)(2,1)} %maps_ref.1) | copy-start | bytes 1572868
  77.9 69.7 %all-to-all-start.1 = ((bf16[512,8,128]{2,1,0:T(8,128)(2,1)}), bf16[512,8,128]{2,1,0:T(8,128)(2,1)S(1)}, u32[]{:S(2)}, u32[]{:S(2)}) async-start(bf16[512,8,128]{2,1,0:T(8,128)(2,1)} %bitcast.5), calls=%async_computation.1 | async-start | bytes 2097152 | tf_op jit(solution)/shard_map/all_to_all | solution.py:388
  91.1 7.4 %collective-permute-start = (bf16[2,2,8,8,512]{4,3,1,0,2:T(8,128)(2,1)S(1)}, bf16[2,2,8,8,512]{4,3,1,0,2:T(8,128)(2,1)S(1)}, u32[]{:S(2)}, u32[]{:S(2)}) collective-permute-start(bf16[2,2,8,8,512]{4,3,1,0,2:T(8,128)(2,1)S(1)} %bitcast.67), channel_id=1, source_target_pairs={{0,1},{1,0},{2,3},{3,2},{4,5},{5,4},{6,7},{7,6},{8,9},{9,8},{10,11... | collective-permute-start | bytes 786440 | tf_op jit(solution)/shard_map/ppermute | solution.py:283
  98.5 15.1 %collective-permute-start.1 = (bf16[2,2,2,8,512]{4,3,2,1,0:T(8,128)(2,1)S(1)}, bf16[2,2,2,8,512]{4,3,2,1,0:T(8,128)(2,1)S(1)}, u32[]{:S(2)}, u32[]{:S(2)}) collective-permute-start(bf16[2,2,2,8,512]{4,3,2,1,0:T(8,128)(2,1)S(1)} %get-tuple-element.14), channel_id=1, source_target_pairs={{0,2},{1,3},{2,0},{3,1},{4,6},{5,7},{6,4},{7,5},{8,10},{9,11},{10,... | collective-permute-start | bytes 196616 | tf_op jit(solution)/shard_map/ppermute | solution.py:289
  100.4 15.1 %collective-permute-start.2 = (bf16[2,2,2,8,512]{4,3,2,1,0:T(8,128)(2,1)S(1)}, bf16[2,2,2,8,512]{4,3,2,1,0:T(8,128)(2,1)S(1)}, u32[]{:S(2)}, u32[]{:S(2)}) collective-permute-start(bf16[2,2,2,8,512]{4,3,2,1,0:T(8,128)(2,1)S(1)} %get-tuple-element.15), channel_id=1, source_target_pairs={{0,4},{1,5},{2,6},{3,7},{4,0},{5,1},{6,2},{7,3},{8,12},{9,13},{10,... | collective-permute-start | bytes 196616 | tf_op jit(solution)/shard_map/ppermute | solution.py:289
  102.4 19.0 %collective-permute-start.3 = (bf16[2,2,2,8,512]{4,3,2,1,0:T(8,128)(2,1)S(1)}, bf16[2,2,2,8,512]{4,3,2,1,0:T(8,128)(2,1)S(1)}, u32[]{:S(2)}, u32[]{:S(2)}) collective-permute-start(bf16[2,2,2,8,512]{4,3,2,1,0:T(8,128)(2,1)S(1)} %get-tuple-element.16), channel_id=1, source_target_pairs={{0,6},{1,7},{2,4},{3,5},{4,2},{5,3},{6,0},{7,1},{8,14},{9,15},{10,... | collective-permute-start | bytes 196616 | tf_op jit(solution)/shard_map/ppermute | solution.py:289
  106.9 14.5 %collective-permute-start.4 = (bf16[2,2,2,8,512]{4,3,2,1,0:T(8,128)(2,1)S(1)}, bf16[2,2,2,8,512]{4,3,2,1,0:T(8,128)(2,1)S(1)}, u32[]{:S(2)}, u32[]{:S(2)}) collective-permute-start(bf16[2,2,2,8,512]{4,3,2,1,0:T(8,128)(2,1)S(1)} %get-tuple-element.17), channel_id=1, source_target_pairs={{0,8},{1,9},{2,10},{3,11},{4,12},{5,13},{6,14},{7,15},{8,0},{9,1},... | collective-permute-start | bytes 196616 | tf_op jit(solution)/shard_map/ppermute | solution.py:289
  108.8 38.8 %copy-start.1 = (bf16[1024,512]{1,0:T(8,128)(2,1)S(1)}, bf16[1024,512]{1,0:T(8,128)(2,1)}, u32[]{:S(2)}) copy-start(bf16[1024,512]{1,0:T(8,128)(2,1)} %constant.80.clone.table_ref) | copy-start | bytes 3145732
  108.8 12.6 %collective-permute-start.5 = (bf16[2,2,2,8,512]{4,3,2,1,0:T(8,128)(2,1)S(1)}, bf16[2,2,2,8,512]{4,3,2,1,0:T(8,128)(2,1)S(1)}, u32[]{:S(2)}, u32[]{:S(2)}) collective-permute-start(bf16[2,2,2,8,512]{4,3,2,1,0:T(8,128)(2,1)S(1)} %get-tuple-element.18), channel_id=1, source_target_pairs={{0,10},{1,11},{2,8},{3,9},{4,14},{5,15},{6,12},{7,13},{8,2},{9,3},... | collective-permute-start | bytes 196616 | tf_op jit(solution)/shard_map/ppermute | solution.py:289
  113.6 7.8 %collective-permute-start.6 = (bf16[2,2,2,8,512]{4,3,2,1,0:T(8,128)(2,1)S(1)}, bf16[2,2,2,8,512]{4,3,2,1,0:T(8,128)(2,1)S(1)}, u32[]{:S(2)}, u32[]{:S(2)}) collective-permute-start(bf16[2,2,2,8,512]{4,3,2,1,0:T(8,128)(2,1)S(1)} %fusion.8), channel_id=1, source_target_pairs={{0,12},{1,13},{2,14},{3,15},{4,8},{5,9},{6,10},{7,11},{8,4},{9,5},... | collective-permute-start | bytes 196616 | tf_op jit(solution)/shard_map/ppermute | solution.py:289
  115.6 7.9 %collective-permute-start.7 = (bf16[2,2,2,8,512]{4,3,2,1,0:T(8,128)(2,1)S(1)}, bf16[2,2,2,8,512]{4,3,2,1,0:T(8,128)(2,1)S(1)}, u32[]{:S(2)}, u32[]{:S(2)}) collective-permute-start(bf16[2,2,2,8,512]{4,3,2,1,0:T(8,128)(2,1)S(1)} %get-tuple-element.13), channel_id=1, source_target_pairs={{0,14},{1,15},{2,12},{3,13},{4,10},{5,11},{6,8},{7,9},{8,6},{9,7},... | collective-permute-start | bytes 196616 | tf_op jit(solution)/shard_map/ppermute | solution.py:289

commit v7 on v6

--- a/solution.py
+++ b/solution.py
@@ -86,8 +86,11 @@
         for k, here in enumerate(halves)
         for n, (source, held) in enumerate(((maps_ref, maps), (image_ref, image)))
     ]
-    fetch_table = pltpu.make_async_copy(table_ref, table, arrive.at[4])
-    for copy in inputs + [fetch_table]:
+    fetch_table = [
+        pltpu.make_async_copy(table_ref.at[rows], table.at[rows], arrive.at[4 + k])
+        for k, rows in enumerate((pl.ds(0, len_y), pl.ds(len_y, len_y)))
+    ]
+    for copy in inputs + fetch_table:
         copy.start()
     for i in range(steps):
         if i * 2 % steps == 0:
@@ -105,10 +108,12 @@
                     coil_im = map_re * image_im + map_im * image_re
                     lhs[i, row : row + z_lo] = coil_re.astype(jnp.bfloat16)
                     lhs[i, row + half : row + half + z_lo] = coil_im.astype(jnp.bfloat16)
-    fetch_table.wait()
+    fetch_table[0].wait()
     results = []
     for i in range(steps):
         by_cos = jnp.dot(lhs[i], table[:len_y], preferred_element_type=jnp.float32)
+        if i == 0:
+            fetch_table[1].wait()
         by_sin = jnp.dot(lhs[i], table[len_y:], preferred_element_type=jnp.float32)
         middle = by_cos.shape[1]
         other_cos, by_sin = split_ends(by_cos, by_sin, 1)
@@ -310,7 +315,7 @@
             pltpu.VMEM(table.shape, jnp.bfloat16),
             pltpu.VMEM((steps, 2 * half, len_y), jnp.bfloat16),
             pltpu.VMEM((steps, slabs, z_lo, 2 * LANES), jnp.bfloat16),
-            pltpu.SemaphoreType.DMA((5,)),
+            pltpu.SemaphoreType.DMA((6,)),
             pltpu.SemaphoreType.DMA((steps,)),
         ],
         4 * steps * half * len_y * len_y,

time: 166 us -> 166 us (level)
  no operation moved by 1% of the time
where the time goes in v7:
time: 166 us
  waiting for transfers between devices  74.5 us (45%)
  starting transfers between devices  60.6 us (37%)
  blocking collectives  14.2 us (9%)
  Pallas kernels  8.69 us (5%)
  local copies, waits for them, and re-layouts  4.04 us (2%)
  other arithmetic  3.06 us (2%)
    all_to_all x1, waiting for transfers between devices, shards(): lax.all_to_all(outgoing, 'slab', split_axis=0, concat_axis=0, tiled=True)  47.3 us
    all_to_all x1, waiting for transfers between devices, shards(): lax.all_to_all(back_z.reshape(slabs * groups, z_part, LANES), ('slab', 'c...  24.2 us
    ppermute x7, starting transfers between devices, maps_by_readout(): piece = lax.ppermute(piece, 'coil', [(i, i ^ cores * k) for i in devices])  22.7 us
    all_to_all x1, starting transfers between devices, shards(): lax.all_to_all(outgoing, 'slab', split_axis=0, concat_axis=0, tiled=True)  18.6 us
    all_to_all x1, blocking collectives, shards(): lax.all_to_all(total, 'coil', split_axis=0, concat_axis=0, tiled=True)  14.2 us
    all_to_all x1, starting transfers between devices, shards(): lax.all_to_all(back_z.reshape(slabs * groups, z_part, LANES), ('slab', 'c...  13.1 us
    ppermute x1, starting transfers between devices, maps_by_readout(): got = lax.ppermute(other, 'coil', [(i, i ^ 1) for i in devices])  6.21 us
    pallas_call x1, Pallas kernels, send_forward(): call(forward_y, 'forward_y', jax.ShapeDtypeStruct((slabs, z_lo, steps * 2...  3.55 us
  transfers between devices with their start and end apart: 10, of which 4 were waited for; matrix products, arithmetic and copies ran while one was open for 4% of the time, Pallas kernels for 0%

profile of v7, /device:TPU:1, one launch (start us, length us, event | category | flops | bytes accessed | tf_op | source)
XLA Modules:
  0.0 165.6 jit_solution(4931077517874154280)
XLA Ops:
  0.0 3.6 %forward_y.1 = bf16[32,16,1024]{2,1,0:T(8,128)(2,1)} custom-call(bf16[2,2,8,16,512]{4,3,2,1,0:T(8,128)(2,1)} %maps_ref.1, bf16[2,2,8,16,512]{4,3,2,1,0:T(8,128)(2,1)} %image_ref.1, bf16[1024,256]{1,0:T(8,128)(2,1)} %constant.78.clone.table_ref.columns_ref), custom_call_target="tpu_custom_call" | custom-call | flops 536870912 | bytes 2621440 | tf_op jit(solution)/shard_map/forward_y/pallas_call | solution.py:306
  3.6 0.0 copy-start.3
  3.6 18.6 %all-to-all-start = ((bf16[32,16,1024]{2,1,0:T(8,128)(2,1)}), bf16[32,16,1024]{2,1,0:T(8,128)(2,1)S(1)}, u32[]{:S(2)}, u32[]{:S(2)}) async-start(bf16[32,16,1024]{2,1,0:T(8,128)(2,1)} %forward_y.1), calls=%async_computation | async-start | bytes 2097152 | tf_op jit(solution)/shard_map/all_to_all | solution.py:387
  22.2 0.0 copy-done.3
  22.2 0.7 rev.12
  22.9 0.1 broadcast_select_fusion
  23.1 0.2 slice.17
  23.3 0.0 copy-start.5
  23.3 1.0 slice.16
  24.3 0.0 copy-done.5
  24.3 0.1 rev.14
  24.4 0.1 reshape.31
  24.6 0.5 reverse
  25.1 1.1 slice.20
  26.2 0.2 rev.15
  26.3 0.0 copy-start
  26.4 0.0 copy-start.2
  26.4 1.7 %pad_maximum_fusion.measured_ref = bf16[2,2,8,2,16,512]{5,4,3,2,1,0:T(8,128)(2,1)S(1)} fusion(bf16[2,2,8,2,16,255]{5,4,3,2,1,0:T(8,128)(2,1)} %slice.20, bf16[2,2,8,2,16,257]{5,4,3,2,1,0:T(8,128)(2,1)} %slice.16), kind=kLoop, calls=%fused_computation | loop fusion | flops 2097152 | bytes 2097152 | tf_op jit(solution)/shard_map/concatenate | solution.py:41
  28.1 47.3 %all-to-all-done = bf16[32,16,1024]{2,1,0:T(8,128)(2,1)S(1)} async-done(((bf16[32,16,1024]{2,1,0:T(8,128)(2,1)}), bf16[32,16,1024]{2,1,0:T(8,128)(2,1)S(1)}, u32[]{:S(2)}, u32[]{:S(2)}) %all-to-all-start) | async-done | bytes 1048608 | tf_op jit(solution)/shard_map/all_to_all | solution.py:387
  75.3 0.0 copy-done
  75.4 0.0 copy-done.2
  75.4 2.7 %z_work.1 = bf16[32,8,16,128]{3,2,1,0:T(8,128)(2,1)} custom-call(bf16[512,1024]{1,0:T(8,128)(2,1)S(1)} %bitcast.55, bf16[2,2,8,2,16,512]{5,4,3,2,1,0:T(8,128)(2,1)S(1)} %pad_maximum_fusion.measured_ref, f32[512,128]{1,0:T(8,128)S(1)} %pad_maximum_fusion.1.weight_ref, bf16[1024,256]{1,0:T(8,128)(2,1)S(1)} %copy-done, bf16[512,512]{1,0:T(8,128)(2,1)S(1)} %copy-done.2), custom_call_target="tpu_custom_call" | custom-call | flops 1610612736 | bytes 4194304 | tf_op jit(solution)/shard_map/z_work/pallas_call | solution.py:336
  78.1 0.0 copy-start.4
  78.1 13.1 %all-to-all-start.1 = ((bf16[512,8,128]{2,1,0:T(8,128)(2,1)}), bf16[512,8,128]{2,1,0:T(8,128)(2,1)S(1)}, u32[]{:S(2)}, u32[]{:S(2)}) async-start(bf16[512,8,128]{2,1,0:T(8,128)(2,1)} %bitcast.5), calls=%async_computation.1 | async-start | bytes 2097152 | tf_op jit(solution)/shard_map/all_to_all | solution.py:393
  91.2 0.0 copy-done.4
  91.3 6.2 %collective-permute-start = (bf16[2,2,8,8,512]{4,3,1,0,2:T(8,128)(2,1)S(1)}, bf16[2,2,8,8,512]{4,3,1,0,2:T(8,128)(2,1)S(1)}, u32[]{:S(2)}, u32[]{:S(2)}) collective-permute-start(bf16[2,2,8,8,512]{4,3,1,0,2:T(8,128)(2,1)S(1)} %bitcast.67), channel_id=1, source_target_pairs={{0,1},{1,0},{2,3},{3,2},{4,5},{5,4},{6,7},{7,6},{8,9},{9,8},{10,11... | collective-permute-start | bytes 786440 | tf_op jit(solution)/shard_map/ppermute | solution.py:288
  97.6 0.1 pad_add_fusion.place_ref
  97.7 0.9 collective-permute-done
  98.7 1.9 %collective-permute-start.1 = (bf16[2,2,2,8,512]{4,3,2,1,0:T(8,128)(2,1)S(1)}, bf16[2,2,2,8,512]{4,3,2,1,0:T(8,128)(2,1)S(1)}, u32[]{:S(2)}, u32[]{:S(2)}) collective-permute-start(bf16[2,2,2,8,512]{4,3,2,1,0:T(8,128)(2,1)S(1)} %get-tuple-element.14), channel_id=1, source_target_pairs={{0,2},{1,3},{2,0},{3,1},{4,6},{5,7},{6,4},{7,5},{8,10},{9,11},{10,... | collective-permute-start | bytes 196616 | tf_op jit(solution)/shard_map/ppermute | solution.py:294
  100.6 1.9 %collective-permute-start.2 = (bf16[2,2,2,8,512]{4,3,2,1,0:T(8,128)(2,1)S(1)}, bf16[2,2,2,8,512]{4,3,2,1,0:T(8,128)(2,1)S(1)}, u32[]{:S(2)}, u32[]{:S(2)}) collective-permute-start(bf16[2,2,2,8,512]{4,3,2,1,0:T(8,128)(2,1)S(1)} %get-tuple-element.15), channel_id=1, source_target_pairs={{0,4},{1,5},{2,6},{3,7},{4,0},{5,1},{6,2},{7,3},{8,12},{9,13},{10,... | collective-permute-start | bytes 196616 | tf_op jit(solution)/shard_map/ppermute | solution.py:294
  102.5 4.5 %collective-permute-start.3 = (bf16[2,2,2,8,512]{4,3,2,1,0:T(8,128)(2,1)S(1)}, bf16[2,2,2,8,512]{4,3,2,1,0:T(8,128)(2,1)S(1)}, u32[]{:S(2)}, u32[]{:S(2)}) collective-permute-start(bf16[2,2,2,8,512]{4,3,2,1,0:T(8,128)(2,1)S(1)} %get-tuple-element.16), channel_id=1, source_target_pairs={{0,6},{1,7},{2,4},{3,5},{4,2},{5,3},{6,0},{7,1},{8,14},{9,15},{10,... | collective-permute-start | bytes 196616 | tf_op jit(solution)/shard_map/ppermute | solution.py:294
  107.0 1.9 %collective-permute-start.4 = (bf16[2,2,2,8,512]{4,3,2,1,0:T(8,128)(2,1)S(1)}, bf16[2,2,2,8,512]{4,3,2,1,0:T(8,128)(2,1)S(1)}, u32[]{:S(2)}, u32[]{:S(2)}) collective-permute-start(bf16[2,2,2,8,512]{4,3,2,1,0:T(8,128)(2,1)S(1)} %get-tuple-element.17), channel_id=1, source_target_pairs={{0,8},{1,9},{2,10},{3,11},{4,12},{5,13},{6,14},{7,15},{8,0},{9,1},... | collective-permute-start | bytes 196616 | tf_op jit(solution)/shard_map/ppermute | solution.py:294
  109.0 0.0 copy-start.1
  109.0 4.7 %collective-permute-start.5 = (bf16[2,2,2,8,512]{4,3,2,1,0:T(8,128)(2,1)S(1)}, bf16[2,2,2,8,512]{4,3,2,1,0:T(8,128)(2,1)S(1)}, u32[]{:S(2)}, u32[]{:S(2)}) collective-permute-start(bf16[2,2,2,8,512]{4,3,2,1,0:T(8,128)(2,1)S(1)} %get-tuple-element.18), channel_id=1, source_target_pairs={{0,10},{1,11},{2,8},{3,9},{4,14},{5,15},{6,12},{7,13},{8,2},{9,3},... | collective-permute-start | bytes 196616 | tf_op jit(solution)/shard_map/ppermute | solution.py:294
  113.8 0.0 collective-permute-done.1
  113.8 1.9 %collective-permute-start.6 = (bf16[2,2,2,8,512]{4,3,2,1,0:T(8,128)(2,1)S(1)}, bf16[2,2,2,8,512]{4,3,2,1,0:T(8,128)(2,1)S(1)}, u32[]{:S(2)}, u32[]{:S(2)}) collective-permute-start(bf16[2,2,2,8,512]{4,3,2,1,0:T(8,128)(2,1)S(1)} %fusion.8), channel_id=1, source_target_pairs={{0,12},{1,13},{2,14},{3,15},{4,8},{5,9},{6,10},{7,11},{8,4},{9,5},... | collective-permute-start | bytes 196616 | tf_op jit(solution)/shard_map/ppermute | solution.py:294
  115.7 0.0 collective-permute-done.2
  115.7 5.7 %collective-permute-start.7 = (bf16[2,2,2,8,512]{4,3,2,1,0:T(8,128)(2,1)S(1)}, bf16[2,2,2,8,512]{4,3,2,1,0:T(8,128)(2,1)S(1)}, u32[]{:S(2)}, u32[]{:S(2)}) collective-permute-start(bf16[2,2,2,8,512]{4,3,2,1,0:T(8,128)(2,1)S(1)} %get-tuple-element.13), channel_id=1, source_target_pairs={{0,14},{1,15},{2,12},{3,13},{4,10},{5,11},{6,8},{7,9},{8,6},{9,7},... | collective-permute-start | bytes 196616 | tf_op jit(solution)/shard_map/ppermute | solution.py:294
  121.5 0.0 collective-permute-done.3
  121.5 0.0 collective-permute-done.4
  121.5 0.0 collective-permute-done.5
  121.6 0.0 collective-permute-done.6
  121.6 2.0 %collective-permute-done.7 = bf16[2,2,2,8,512]{4,3,2,1,0:T(8,128)(2,1)S(1)} collective-permute-done((bf16[2,2,2,8,512]{4,3,2,1,0:T(8,128)(2,1)S(1)}, bf16[2,2,2,8,512]{4,3,2,1,0:T(8,128)(2,1)S(1)}, u32[]{:S(2)}, u32[]{:S(2)}) %collective-permute-start.7) | collective-permute-done | bytes 65568 | tf_op jit(solution)/shard_map/ppermute | solution.py:294
  123.6 24.2 %all-to-all-done.1 = bf16[512,8,128]{2,1,0:T(8,128)(2,1)S(1)} async-done(((bf16[512,8,128]{2,1,0:T(8,128)(2,1)}), bf16[512,8,128]{2,1,0:T(8,128)(2,1)S(1)}, u32[]{:S(2)}, u32[]{:S(2)}) %all-to-all-start.1) | async-done | bytes 1048608 | tf_op jit(solution)/shard_map/all_to_all | solution.py:393
  147.8 0.0 copy-done.1
  147.8 2.4 %backward_y.1 = bf16[16,32,512]{2,1,0:T(8,128)(2,1)S(1)} custom-call(s32[2]{0:T(128)S(1)} %pad_add_fusion.place_ref, bf16[32,8,16,128]{3,2,1,0:T(8,128)(2,1)S(1)} %bitcast.54, bf16[8,2,2,2,8,512]{5,4,3,2,1,0:T(8,128)(2,1)S(1)} %bitcast_dynamic-update-slice_fusion.maps_ref, bf16[1024,512]{1,0:T(8,128)(2,1)S(1)} %copy-done.1), custom_call_target="tpu_custom_call" | custom-call | flops 1073741824 | bytes 3145728 | tf_op jit(solution)/shard_map/backward_y/pallas_call | solution.py:361
  150.3 14.2 %all_to_all.15 = bf16[16,32,512]{2,1,0:T(8,128)(2,1)S(1)} all-to-all(bf16[16,32,512]{2,1,0:T(8,128)(2,1)S(1)} %backward_y.1), channel_id=1, replica_groups=mesh['slab'=32,'coil'=16] {'coil'}, dimensions={0} | all-to-all | bytes 1048576 | tf_op jit(solution)/shard_map/all_to_all | solution.py:403
  164.5 1.1 copy_bitcast_fusion
  (20 shorter events, 0.3 us)
Async XLA Ops:
  3.6 18.7 %copy-start.3 = (bf16[2,2,8,2,16,512]{5,4,3,2,1,0:T(8,128)(2,1)S(1)}, bf16[2,2,8,2,16,512]{5,4,3,2,1,0:T(8,128)(2,1)}, u32[]{:S(2)}) copy-start(bf16[2,2,8,2,16,512]{5,4,3,2,1,0:T(8,128)(2,1)} %param.9) | copy-start | bytes 3145732
  3.6 71.8 %all-to-all-start = ((bf16[32,16,1024]{2,1,0:T(8,128)(2,1)}), bf16[32,16,1024]{2,1,0:T(8,128)(2,1)S(1)}, u32[]{:S(2)}, u32[]{:S(2)}) async-start(bf16[32,16,1024]{2,1,0:T(8,128)(2,1)} %forward_y.1), calls=%async_computation | async-start | bytes 2097152 | tf_op jit(solution)/shard_map/all_to_all | solution.py:387
  23.3 1.0 copy-start.5
  26.3 49.0 %copy-start = (bf16[1024,256]{1,0:T(8,128)(2,1)S(1)}, bf16[1024,256]{1,0:T(8,128)(2,1)}, u32[]{:S(2)}) copy-start(bf16[1024,256]{1,0:T(8,128)(2,1)} %constant.78.clone.table_ref.columns_ref) | copy-start | bytes 1572868
  26.4 49.0 %copy-start.2 = (bf16[512,512]{1,0:T(8,128)(2,1)S(1)}, bf16[512,512]{1,0:T(8,128)(2,1)}, u32[]{:S(2)}) copy-start(bf16[512,512]{1,0:T(8,128)(2,1)} %constant.79.clone.rows_ref) | copy-start | bytes 1572868
  78.1 13.1 %copy-start.4 = (bf16[2,2,8,16,512]{4,3,2,1,0:T(8,128)(2,1)S(1)}, bf16[2,2,8,16,512]{4,3,2,1,0:T(8,128)(2,1)}, u32[]{:S(2)}) copy-start(bf16[2,2,8,16,512]{4,3,2,1,0:T(8,128)(2,1)} %maps_ref.1) | copy-start | bytes 1572868
  78.1 69.7 %all-to-all-start.1 = ((bf16[512,8,128]{2,1,0:T(8,128)(2,1)}), bf16[512,8,128]{2,1,0:T(8,128)(2,1)S(1)}, u32[]{:S(2)}, u32[]{:S(2)}) async-start(bf16[512,8,128]{2,1,0:T(8,128)(2,1)} %bitcast.5), calls=%async_computation.1 | async-start | bytes 2097152 | tf_op jit(solution)/shard_map/all_to_all | solution.py:393
  91.3 7.4 %collective-permute-start = (bf16[2,2,8,8,512]{4,3,1,0,2:T(8,128)(2,1)S(1)}, bf16[2,2,8,8,512]{4,3,1,0,2:T(8,128)(2,1)S(1)}, u32[]{:S(2)}, u32[]{:S(2)}) collective-permute-start(bf16[2,2,8,8,512]{4,3,1,0,2:T(8,128)(2,1)S(1)} %bitcast.67), channel_id=1, source_target_pairs={{0,1},{1,0},{2,3},{3,2},{4,5},{5,4},{6,7},{7,6},{8,9},{9,8},{10,11... | collective-permute-start | bytes 786440 | tf_op jit(solution)/shard_map/ppermute | solution.py:288
  98.7 15.1 %collective-permute-start.1 = (bf16[2,2,2,8,512]{4,3,2,1,0:T(8,128)(2,1)S(1)}, bf16[2,2,2,8,512]{4,3,2,1,0:T(8,128)(2,1)S(1)}, u32[]{:S(2)}, u32[]{:S(2)}) collective-permute-start(bf16[2,2,2,8,512]{4,3,2,1,0:T(8,128)(2,1)S(1)} %get-tuple-element.14), channel_id=1, source_target_pairs={{0,2},{1,3},{2,0},{3,1},{4,6},{5,7},{6,4},{7,5},{8,10},{9,11},{10,... | collective-permute-start | bytes 196616 | tf_op jit(solution)/shard_map/ppermute | solution.py:294
  100.6 15.1 %collective-permute-start.2 = (bf16[2,2,2,8,512]{4,3,2,1,0:T(8,128)(2,1)S(1)}, bf16[2,2,2,8,512]{4,3,2,1,0:T(8,128)(2,1)S(1)}, u32[]{:S(2)}, u32[]{:S(2)}) collective-permute-start(bf16[2,2,2,8,512]{4,3,2,1,0:T(8,128)(2,1)S(1)} %get-tuple-element.15), channel_id=1, source_target_pairs={{0,4},{1,5},{2,6},{3,7},{4,0},{5,1},{6,2},{7,3},{8,12},{9,13},{10,... | collective-permute-start | bytes 196616 | tf_op jit(solution)/shard_map/ppermute | solution.py:294
  102.5 19.0 %collective-permute-start.3 = (bf16[2,2,2,8,512]{4,3,2,1,0:T(8,128)(2,1)S(1)}, bf16[2,2,2,8,512]{4,3,2,1,0:T(8,128)(2,1)S(1)}, u32[]{:S(2)}, u32[]{:S(2)}) collective-permute-start(bf16[2,2,2,8,512]{4,3,2,1,0:T(8,128)(2,1)S(1)} %get-tuple-element.16), channel_id=1, source_target_pairs={{0,6},{1,7},{2,4},{3,5},{4,2},{5,3},{6,0},{7,1},{8,14},{9,15},{10,... | collective-permute-start | bytes 196616 | tf_op jit(solution)/shard_map/ppermute | solution.py:294
  107.0 14.5 %collective-permute-start.4 = (bf16[2,2,2,8,512]{4,3,2,1,0:T(8,128)(2,1)S(1)}, bf16[2,2,2,8,512]{4,3,2,1,0:T(8,128)(2,1)S(1)}, u32[]{:S(2)}, u32[]{:S(2)}) collective-permute-start(bf16[2,2,2,8,512]{4,3,2,1,0:T(8,128)(2,1)S(1)} %get-tuple-element.17), channel_id=1, source_target_pairs={{0,8},{1,9},{2,10},{3,11},{4,12},{5,13},{6,14},{7,15},{8,0},{9,1},... | collective-permute-start | bytes 196616 | tf_op jit(solution)/shard_map/ppermute | solution.py:294
  109.0 38.8 %copy-start.1 = (bf16[1024,512]{1,0:T(8,128)(2,1)S(1)}, bf16[1024,512]{1,0:T(8,128)(2,1)}, u32[]{:S(2)}) copy-start(bf16[1024,512]{1,0:T(8,128)(2,1)} %constant.80.clone.table_ref) | copy-start | bytes 3145732
  109.0 12.6 %collective-permute-start.5 = (bf16[2,2,2,8,512]{4,3,2,1,0:T(8,128)(2,1)S(1)}, bf16[2,2,2,8,512]{4,3,2,1,0:T(8,128)(2,1)S(1)}, u32[]{:S(2)}, u32[]{:S(2)}) collective-permute-start(bf16[2,2,2,8,512]{4,3,2,1,0:T(8,128)(2,1)S(1)} %get-tuple-element.18), channel_id=1, source_target_pairs={{0,10},{1,11},{2,8},{3,9},{4,14},{5,15},{6,12},{7,13},{8,2},{9,3},... | collective-permute-start | bytes 196616 | tf_op jit(solution)/shard_map/ppermute | solution.py:294
  113.8 7.8 %collective-permute-start.6 = (bf16[2,2,2,8,512]{4,3,2,1,0:T(8,128)(2,1)S(1)}, bf16[2,2,2,8,512]{4,3,2,1,0:T(8,128)(2,1)S(1)}, u32[]{:S(2)}, u32[]{:S(2)}) collective-permute-start(bf16[2,2,2,8,512]{4,3,2,1,0:T(8,128)(2,1)S(1)} %fusion.8), channel_id=1, source_target_pairs={{0,12},{1,13},{2,14},{3,15},{4,8},{5,9},{6,10},{7,11},{8,4},{9,5},... | collective-permute-start | bytes 196616 | tf_op jit(solution)/shard_map/ppermute | solution.py:294
  115.7 7.9 %collective-permute-start.7 = (bf16[2,2,2,8,512]{4,3,2,1,0:T(8,128)(2,1)S(1)}, bf16[2,2,2,8,512]{4,3,2,1,0:T(8,128)(2,1)S(1)}, u32[]{:S(2)}, u32[]{:S(2)}) collective-permute-start(bf16[2,2,2,8,512]{4,3,2,1,0:T(8,128)(2,1)S(1)} %get-tuple-element.13), channel_id=1, source_target_pairs={{0,14},{1,15},{2,12},{3,13},{4,10},{5,11},{6,8},{7,9},{8,6},{9,7},... | collective-permute-start | bytes 196616 | tf_op jit(solution)/shard_map/ppermute | solution.py:294
